TPU v7x, 32 devices: a whole 2x2x4 slice. The times are simulated.
32 devices in a mesh: fsdp: 8 (over z, x), seq: 4 (over y, core).
Axes of the slice: x: 2, y: 2, z: 4, core: 2. Of those that a mesh axis runs over, the one named last changes fastest.
Arguments:
- inputs: bfloat16 [16384, 768], P(('fsdp', 'seq')), may hold values from -6 to 6
- cotangent: bfloat16 [16384, 768], P(('fsdp', 'seq')), may hold values from -6 to 6
- first_gain: bfloat16 [768], P('fsdp'), may hold values from 0.5 to 1.5
- first_bias: bfloat16 [768], P('fsdp'), may hold values from -1.5 to 1.5
- triple_weight: bfloat16 [768, 2304], P(None, 'fsdp'), may hold values from -0.3125 to 0.3125
- query_bias: bfloat16 [768], P('fsdp'), may hold values from -1.5 to 1.5
- value_bias: bfloat16 [768], P('fsdp'), may hold values from -1.5 to 1.5
- out_weight: bfloat16 [768, 768], P(None, 'fsdp'), may hold values from -0.875 to 0.875
- out_bias: bfloat16 [768], P('fsdp'), may hold values from -1.5 to 1.5
- second_gain: bfloat16 [768], P('fsdp'), may hold values from 0.5 to 1.5
- second_bias: bfloat16 [768], P('fsdp'), may hold values from -1.5 to 1.5
- expand_weight: bfloat16 [768, 3072], P(None, 'fsdp'), may hold values from -0.21875 to 0.21875
- expand_bias: bfloat16 [3072], P('fsdp'), may hold values from -1.5 to 1.5
- reduce_weight: bfloat16 [3072, 768], P(None, 'fsdp'), may hold values from -0.109375 to 0.109375
- reduce_bias: bfloat16 [768], P('fsdp'), may hold values from -1.5 to 1.5
Outputs:
- output: bfloat16 [16384, 768], P(('fsdp', 'seq'))
- grad_inputs: bfloat16 [16384, 768], P(('fsdp', 'seq'))
- grad_first_gain: float32 [768], P('fsdp')
- grad_first_bias: float32 [768], P('fsdp')
- grad_triple_weight: float32 [768, 2304], P(None, 'fsdp')
- grad_query_bias: float32 [768], P('fsdp')
- grad_value_bias: float32 [768], P('fsdp')
- grad_out_weight: float32 [768, 768], P(None, 'fsdp')
- grad_out_bias: float32 [768], P('fsdp')
- grad_second_gain: float32 [768], P('fsdp')
- grad_second_bias: float32 [768], P('fsdp')
- grad_expand_weight: float32 [768, 3072], P(None, 'fsdp')
- grad_expand_bias: float32 [3072], P('fsdp')
- grad_reduce_weight: float32 [3072, 768], P(None, 'fsdp')
- grad_reduce_bias: float32 [768], P('fsdp')
All inputs are finite; a program needn't handle non-finite values.
Results may differ from a plain program's by a relative error of at most 0.017.
Values may be sent and summed in bfloat16 or wider, within the bound.
No kernel may reach another device: no remote copies, remote signals or barrier semaphores. Data moves between devices by JAX's collectives and lax.ppermute only.
A program may use at most 192 MiB of HBM per device.

v0:
```python
import jax
import jax.numpy as jnp
from jax import lax
from jax.sharding import PartitionSpec as P

HEADS = 12
HEAD_DIM = 64
GROUP = 8


EPSILON = 1e-05
NEGATIVE = -1e30


def from_behind(array, axis, by):
    devices = lax.axis_size(axis)
    pairs = [(i, i + by) for i in range(devices) if 0 <= i + by < devices]
    return lax.ppermute(array, axis, pairs)


def layer_norm(value, gain, bias):
    centre = value - jnp.mean(value, axis=-1, keepdims=True)
    spread = jnp.mean(centre * centre, axis=-1, keepdims=True)
    return centre * lax.rsqrt(spread + EPSILON) * gain + bias


def smooth_gelu(value):
    return (
        0.5
        * value
        * (1.0 + jnp.tanh(0.7978845608028654 * (value + 0.044715 * value * value * value)))
    )


def matmul_low(left, right):
    return jnp.dot(left, right, preferred_element_type=jnp.float32)


def outer_sum(left, right):
    return lax.dot_general(
        left, right, (((0,), (0,)), ((), ())), preferred_element_type=jnp.float32
    )


def back_mul(grad, weight):
    return lax.dot_general(
        grad, weight, (((1,), (1,)), ((), ())), preferred_element_type=jnp.float32
    )


def column_sums(value):
    return jnp.sum(value.astype(jnp.float32), axis=0)


def block_scores(queries, key_rows, query_first, key_first, remote):
    scale = queries.shape[-1] ** (-0.5)
    scores = (
        jnp.einsum("qhd,khd->hqk", queries, key_rows, preferred_element_type=jnp.float32) * scale
    )
    if remote:
        return scores
    here = query_first + lax.iota(jnp.int32, queries.shape[0])
    there = key_first + lax.iota(jnp.int32, key_rows.shape[0])
    return jnp.where(there[None, None, :] <= here[None, :, None], scores, NEGATIVE)


def visit_piece(queries, query_first, piece, offset, owner, visit, carry):
    block = queries.shape[0]
    keys_all, values_all = piece

    def advance(number, state):
        first = number * block
        key_rows = lax.dynamic_slice_in_dim(keys_all, first, block, 0)
        value_rows = lax.dynamic_slice_in_dim(values_all, first, block, 0)
        scores = block_scores(queries, key_rows, query_first, first, offset > 0)
        return visit(state, scores, offset, first, key_rows, value_rows)

    if offset == 0:
        return lax.fori_loop(0, query_first // block + 1, advance, carry)

    def run_all(state):
        return lax.fori_loop(0, keys_all.shape[0] // block, advance, state)

    def skip_all(state):
        return state

    return lax.cond(owner >= offset, run_all, skip_all, carry)


def sweep(queries, query_first, pieces, owner, visit, carry):
    for offset in range(len(pieces)):
        carry = visit_piece(queries, query_first, pieces[offset], offset, owner, visit, carry)
    return carry


def attend(queries_all, pieces, owner):
    total_rows, heads_here, head_size = queries_all.shape
    block = min(512, total_rows)

    def one_block(number):
        query_first = number * block
        queries = lax.dynamic_slice_in_dim(queries_all, query_first, block, 0)

        def visit_stats(state, scores, offset, first, key_rows, value_rows):
            top, total = state
            fresh = jnp.maximum(top, jnp.max(scores, axis=-1))
            total = total * jnp.exp(top - fresh) + jnp.sum(
                jnp.exp(scores - fresh[:, :, None]), axis=-1
            )
            return (fresh, total)

        start_state = (
            jnp.full((heads_here, block), NEGATIVE, jnp.float32),
            jnp.zeros((heads_here, block), jnp.float32),
        )
        top, total = sweep(queries, query_first, pieces, owner, visit_stats, start_state)
        log_total = top + jnp.log(total)

        def visit_out(state, scores, offset, first, key_rows, value_rows):
            probs = jnp.exp(scores - log_total[:, :, None]).astype(jnp.bfloat16)
            return state + jnp.einsum(
                "hqk,khd->qhd", probs, value_rows, preferred_element_type=jnp.float32
            )

        summed = sweep(
            queries,
            query_first,
            pieces,
            owner,
            visit_out,
            jnp.zeros((block, heads_here, head_size), jnp.float32),
        )
        return (summed, log_total)

    numbers = jnp.arange(total_rows // block, dtype=jnp.int32)
    summed_all, log_totals = lax.map(one_block, numbers)
    return (summed_all.reshape(total_rows, heads_here, head_size), log_totals)


def add_block(whole, part, offset, first):
    current = lax.dynamic_slice(whole, (offset, first, 0, 0), (1,) + part.shape)
    return lax.dynamic_update_slice(whole, current + part[None], (offset, first, 0, 0))


def attend_back(queries_all, pieces, owner, log_totals, outputs_all, grad_heads):
    total_rows, heads_here, head_size = queries_all.shape
    block = min(512, total_rows)
    scale = head_size ** (-0.5)
    count = len(pieces)

    def one_block(number, carry):
        grad_query_all, grad_keys, grad_values = carry
        query_first = number * block
        queries = lax.dynamic_slice_in_dim(queries_all, query_first, block, 0)
        grad_rows = lax.dynamic_slice_in_dim(grad_heads, query_first, block, 0)
        out_rows = lax.dynamic_slice_in_dim(outputs_all, query_first, block, 0)
        log_total = lax.dynamic_index_in_dim(log_totals, number, 0, keepdims=False)
        delta = jnp.einsum("qhd,qhd->hq", grad_rows.astype(jnp.float32), out_rows)

        def visit_back(state, scores, offset, first, key_rows, value_rows):
            grad_query, keys_acc, values_acc = state
            probs = jnp.exp(scores - log_total[:, :, None])
            values_acc = add_block(
                values_acc,
                jnp.einsum(
                    "hqk,qhd->khd",
                    probs.astype(jnp.bfloat16),
                    grad_rows,
                    preferred_element_type=jnp.float32,
                ),
                offset,
                first,
            )
            grad_probs = jnp.einsum(
                "qhd,khd->hqk", grad_rows, value_rows, preferred_element_type=jnp.float32
            )
            grad_scores = (probs * (grad_probs - delta[:, :, None])).astype(jnp.bfloat16)
            grad_query = (
                grad_query
                + jnp.einsum(
                    "hqk,khd->qhd", grad_scores, key_rows, preferred_element_type=jnp.float32
                )
                * scale
            )
            keys_acc = add_block(
                keys_acc,
                jnp.einsum("hqk,qhd->khd", grad_scores, queries, preferred_element_type=jnp.float32)
                * scale,
                offset,
                first,
            )
            return (grad_query, keys_acc, values_acc)

        start_state = (
            jnp.zeros((block, heads_here, head_size), jnp.float32),
            grad_keys,
            grad_values,
        )
        grad_query, grad_keys, grad_values = sweep(
            queries, query_first, pieces, owner, visit_back, start_state
        )
        grad_query_all = lax.dynamic_update_slice_in_dim(grad_query_all, grad_query, query_first, 0)
        return (grad_query_all, grad_keys, grad_values)

    empty = jnp.zeros((count, total_rows, heads_here, head_size), jnp.float32)
    start_carry = (jnp.zeros((total_rows, heads_here, head_size), jnp.float32), empty, empty)
    return lax.fori_loop(0, total_rows // block, one_block, start_carry)


def on_device(
    inputs,
    cotangent,
    first_gain,
    first_bias,
    triple_weight,
    query_bias,
    value_bias,
    out_weight,
    out_bias,
    second_gain,
    second_bias,
    expand_weight,
    expand_bias,
    reduce_weight,
    reduce_bias,
):
    weights = (
        lax.all_gather(first_gain, "fsdp", axis=0, tiled=True),
        lax.all_gather(first_bias, "fsdp", axis=0, tiled=True),
        lax.all_gather(triple_weight, "fsdp", axis=1, tiled=True),
        lax.all_gather(query_bias, "fsdp", axis=0, tiled=True),
        lax.all_gather(value_bias, "fsdp", axis=0, tiled=True),
        lax.all_gather(out_weight, "fsdp", axis=1, tiled=True),
        lax.all_gather(out_bias, "fsdp", axis=0, tiled=True),
        lax.all_gather(second_gain, "fsdp", axis=0, tiled=True),
        lax.all_gather(second_bias, "fsdp", axis=0, tiled=True),
        lax.all_gather(expand_weight, "fsdp", axis=1, tiled=True),
        lax.all_gather(expand_bias, "fsdp", axis=0, tiled=True),
        lax.all_gather(reduce_weight, "fsdp", axis=1, tiled=True),
        lax.all_gather(reduce_bias, "fsdp", axis=0, tiled=True),
    )
    (
        full_gain1,
        full_bias1,
        full_triple,
        full_query_bias,
        full_value_bias,
        full_out,
        full_out_bias,
        full_gain2,
        full_bias2,
        full_expand,
        full_expand_bias,
        full_reduce,
        full_reduce_bias,
    ) = weights
    tokens, model = inputs.shape
    lanes = lax.axis_size("seq")
    heads_here = HEADS // lanes
    lane_width = model // lanes
    gain1 = full_gain1.astype(jnp.float32)
    bias1 = full_bias1.astype(jnp.float32)
    gain2 = full_gain2.astype(jnp.float32)
    bias2 = full_bias2.astype(jnp.float32)
    input_wide = inputs.astype(jnp.float32)
    normed1 = layer_norm(input_wide, gain1, bias1).astype(jnp.bfloat16)
    triple_bias = jnp.concatenate(
        [full_query_bias, jnp.zeros_like(full_query_bias), full_value_bias]
    ).astype(jnp.float32)
    mixed = (matmul_low(normed1, full_triple) + triple_bias).astype(jnp.bfloat16)
    mixed = mixed.reshape(tokens, 3, lanes, lane_width)
    by_heads = lax.all_to_all(mixed, "seq", split_axis=2, concat_axis=0, tiled=True)
    rows_all = by_heads.shape[0]
    queries_all = by_heads[:, 0, 0].reshape(rows_all, heads_here, HEAD_DIM)
    own_pair = by_heads[:, 1:, 0]
    owner = lax.axis_index("fsdp") % GROUP
    received = [own_pair]
    moving = own_pair
    for offset in range(1, GROUP):
        moving = from_behind(moving, "fsdp", 1)
        received.append(moving)
    pieces = [
        (
            pair[:, 0].reshape(rows_all, heads_here, HEAD_DIM),
            pair[:, 1].reshape(rows_all, heads_here, HEAD_DIM),
        )
        for pair in received
    ]
    outputs_all, log_totals = attend(queries_all, pieces, owner)
    attended = outputs_all.astype(jnp.bfloat16).reshape(rows_all, 1, lane_width)
    by_rows = lax.all_to_all(attended, "seq", split_axis=0, concat_axis=1, tiled=True).reshape(
        tokens, model
    )
    middle = input_wide + matmul_low(by_rows, full_out) + full_out_bias.astype(jnp.float32)
    normed2 = layer_norm(middle, gain2, bias2).astype(jnp.bfloat16)
    pre = matmul_low(normed2, full_expand) + full_expand_bias.astype(jnp.float32)
    act = smooth_gelu(pre).astype(jnp.bfloat16)
    result = (middle + matmul_low(act, full_reduce) + full_reduce_bias.astype(jnp.float32)).astype(
        jnp.bfloat16
    )
    again = (
        lax.all_gather(first_gain, "fsdp", axis=0, tiled=True),
        lax.all_gather(first_bias, "fsdp", axis=0, tiled=True),
        lax.all_gather(triple_weight, "fsdp", axis=1, tiled=True),
        lax.all_gather(query_bias, "fsdp", axis=0, tiled=True),
        lax.all_gather(value_bias, "fsdp", axis=0, tiled=True),
        lax.all_gather(out_weight, "fsdp", axis=1, tiled=True),
        lax.all_gather(out_bias, "fsdp", axis=0, tiled=True),
        lax.all_gather(second_gain, "fsdp", axis=0, tiled=True),
        lax.all_gather(second_bias, "fsdp", axis=0, tiled=True),
        lax.all_gather(expand_weight, "fsdp", axis=1, tiled=True),
        lax.all_gather(expand_bias, "fsdp", axis=0, tiled=True),
        lax.all_gather(reduce_weight, "fsdp", axis=1, tiled=True),
        lax.all_gather(reduce_bias, "fsdp", axis=0, tiled=True),
    )
    back_triple, back_out, back_expand, back_reduce = (again[2], again[5], again[9], again[11])
    grad_reduce_w = outer_sum(act, cotangent)
    grad_reduce_b = column_sums(cotangent)
    grad_act = back_mul(cotangent, back_reduce)
    gelu_pullback = jax.vjp(smooth_gelu, pre)[1]
    grad_pre = gelu_pullback(grad_act)[0].astype(jnp.bfloat16)
    grad_expand_w = outer_sum(normed2, grad_pre)
    grad_expand_b = column_sums(grad_pre)
    norm_pullback = jax.vjp(layer_norm, middle, gain2, bias2)[1]
    grad_mid_norm, grad_gain2, grad_bias2 = norm_pullback(back_mul(grad_pre, back_expand))
    grad_middle = cotangent.astype(jnp.float32) + grad_mid_norm
    grad_branch = grad_middle.astype(jnp.bfloat16)
    grad_out_w = outer_sum(by_rows, grad_branch)
    grad_out_b = column_sums(grad_branch)
    grad_attended = (
        back_mul(grad_branch, back_out).astype(jnp.bfloat16).reshape(tokens, lanes, lane_width)
    )
    grad_heads = lax.all_to_all(
        grad_attended, "seq", split_axis=1, concat_axis=0, tiled=True
    ).reshape(rows_all, heads_here, HEAD_DIM)
    grad_query_all, grad_keys, grad_values = attend_back(
        queries_all, pieces, owner, log_totals, outputs_all, grad_heads
    )
    pair_grads = jnp.stack([grad_keys, grad_values], axis=2)
    gathered = pair_grads[GROUP - 1]
    for offset in range(GROUP - 1, 0, -1):
        gathered = (
            from_behind(gathered.astype(jnp.bfloat16), "fsdp", -1).astype(gathered.dtype)
            + pair_grads[offset - 1]
        )
    grad_triple_heads = jnp.concatenate(
        [
            grad_query_all.reshape(rows_all, 1, lane_width),
            gathered.reshape(rows_all, 2, lane_width),
        ],
        axis=1,
    )
    grad_triple_heads = grad_triple_heads.astype(jnp.bfloat16).reshape(rows_all, 3, 1, lane_width)
    grad_mixed = lax.all_to_all(
        grad_triple_heads, "seq", split_axis=0, concat_axis=2, tiled=True
    ).reshape(tokens, 3 * model)
    grad_triple_w = outer_sum(normed1, grad_mixed)
    grad_query_b = column_sums(grad_mixed[:, :model])
    grad_value_b = column_sums(grad_mixed[:, 2 * model :])
    first_pullback = jax.vjp(layer_norm, input_wide, gain1, bias1)[1]
    grad_in_norm, grad_gain1, grad_bias1 = first_pullback(back_mul(grad_mixed, back_triple))
    grad_in = (grad_middle + grad_in_norm).astype(jnp.bfloat16)
    summed = (
        lax.psum_scatter(grad_gain1, "fsdp", scatter_dimension=0, tiled=True),
        lax.psum_scatter(grad_bias1, "fsdp", scatter_dimension=0, tiled=True),
        lax.psum_scatter(grad_triple_w, "fsdp", scatter_dimension=1, tiled=True),
        lax.psum_scatter(grad_query_b, "fsdp", scatter_dimension=0, tiled=True),
        lax.psum_scatter(grad_value_b, "fsdp", scatter_dimension=0, tiled=True),
        lax.psum_scatter(grad_out_w, "fsdp", scatter_dimension=1, tiled=True),
        lax.psum_scatter(grad_out_b, "fsdp", scatter_dimension=0, tiled=True),
        lax.psum_scatter(grad_gain2, "fsdp", scatter_dimension=0, tiled=True),
        lax.psum_scatter(grad_bias2, "fsdp", scatter_dimension=0, tiled=True),
        lax.psum_scatter(grad_expand_w, "fsdp", scatter_dimension=1, tiled=True),
        lax.psum_scatter(grad_expand_b, "fsdp", scatter_dimension=0, tiled=True),
        lax.psum_scatter(grad_reduce_w, "fsdp", scatter_dimension=1, tiled=True),
        lax.psum_scatter(grad_reduce_b, "fsdp", scatter_dimension=0, tiled=True),
    )
    totals = (
        lax.psum(summed[0].astype(jnp.bfloat16), "seq").astype(jnp.float32),
        lax.psum(summed[1].astype(jnp.bfloat16), "seq").astype(jnp.float32),
        lax.psum(summed[2].astype(jnp.bfloat16), "seq").astype(jnp.float32),
        lax.psum(summed[3].astype(jnp.bfloat16), "seq").astype(jnp.float32),
        lax.psum(summed[4].astype(jnp.bfloat16), "seq").astype(jnp.float32),
        lax.psum(summed[5].astype(jnp.bfloat16), "seq").astype(jnp.float32),
        lax.psum(summed[6].astype(jnp.bfloat16), "seq").astype(jnp.float32),
        lax.psum(summed[7].astype(jnp.bfloat16), "seq").astype(jnp.float32),
        lax.psum(summed[8].astype(jnp.bfloat16), "seq").astype(jnp.float32),
        lax.psum(summed[9].astype(jnp.bfloat16), "seq").astype(jnp.float32),
        lax.psum(summed[10].astype(jnp.bfloat16), "seq").astype(jnp.float32),
        lax.psum(summed[11].astype(jnp.bfloat16), "seq").astype(jnp.float32),
        lax.psum(summed[12].astype(jnp.bfloat16), "seq").astype(jnp.float32),
    )
    return (
        result,
        grad_in,
        totals[0],
        totals[1],
        totals[2],
        totals[3],
        totals[4],
        totals[5],
        totals[6],
        totals[7],
        totals[8],
        totals[9],
        totals[10],
        totals[11],
        totals[12],
    )


def solution(mesh):
    placed = (
        P(("fsdp", "seq"), None),
        P(("fsdp", "seq"), None),
        P("fsdp"),
        P("fsdp"),
        P(None, "fsdp"),
        P("fsdp"),
        P("fsdp"),
        P(None, "fsdp"),
        P("fsdp"),
        P("fsdp"),
        P("fsdp"),
        P(None, "fsdp"),
        P("fsdp"),
        P(None, "fsdp"),
        P("fsdp"),
    )
    return jax.shard_map(
        on_device,
        mesh=mesh,
        in_specs=placed,
        out_specs=(
            P(("fsdp", "seq"), None),
            P(("fsdp", "seq"), None),
            P("fsdp"),
            P("fsdp"),
            P(None, "fsdp"),
            P("fsdp"),
            P("fsdp"),
            P(None, "fsdp"),
            P("fsdp"),
            P("fsdp"),
            P("fsdp"),
            P(None, "fsdp"),
            P("fsdp"),
            P(None, "fsdp"),
            P("fsdp"),
        ),
        check_vma=False,
    )
```

profile of v0, /device:TPU:0, one launch (start us, length us, event | category | flops | bytes accessed | tf_op | source)
XLA Modules:
  0.0 2768.7 jit_solution(4016279400807349206)
XLA Ops:
  20.2 40.2 %all-reduce.18 = (bf16[768]{0:T(1024)(128)(2,1)S(1)}, bf16[768]{0:T(1024)(128)(2,1)S(1)}, bf16[768]{0:T(1024)(128)(2,1)S(1)}, bf16[768]{0:T(1024)(128)(2,1)S(1)}...) all-reduce(bf16[768]{0:T(1024)(128)(2,1)S(1)} %dynamic-update-slice, ...), channel_id=1, replica_groups=mesh['fsdp'=8,'seq'=4] {'fsdp'}, use_global_device_ids=true, to_apply=%add.3 | all-reduce | flops 6144 | bytes 24576
  60.5 18.1 all-gather.6.cloned.1.call-done
  78.6 5.8 fusion.340
  84.4 2.9 copy.159
  89.0 3.6 all-to-all-start
  93.4 27.7 %all-to-all-done = bf16[512,3,4,192]{0,3,1,2:T(8,128)(2,1)S(1)} async-done(((bf16[512,3,4,192]{0,3,1,2:T(8,128)(2,1)}), bf16[512,3,4,192]{0,3,1,2:T(8,128)(2,1)S(1)}, u32[]{:S(2)}, u32[]{:S(2)}) %all-to-all-start) | async-done | bytes 2359328 | tf_op jit(solution)/shard_map/all_to_all | solution.py:272
  128.3 39.7 %collective-permute-done = bf16[2048,2,192]{0,2,1:T(8,128)(2,1)S(1)} collective-permute-done((bf16[2048,2,192]{0,2,1:T(8,128)(2,1)S(1)}, bf16[2048,2,192]{0,2,1:T(8,128)(2,1)S(1)}, u32[]{:S(2)}, u32[]{:S(2)}) %collective-permute-start) | collective-permute-done | bytes 1572896 | tf_op jit(solution)/shard_map/ppermute | solution.py:18
  168.0 23.6 collective-permute-start.1
  191.5 43.2 %collective-permute-done.1 = bf16[2048,2,192]{0,2,1:T(8,128)(2,1)S(1)} collective-permute-done((bf16[2048,2,192]{0,2,1:T(8,128)(2,1)S(1)}, bf16[2048,2,192]{0,2,1:T(8,128)(2,1)S(1)}, u32[]{:S(2)}, u32[]{:S(2)}) %collective-permute-start.1) | collective-permute-done | bytes 1572896 | tf_op jit(solution)/shard_map/ppermute | solution.py:18
  234.8 21.7 collective-permute-start.2
  256.5 32.1 %collective-permute-done.2 = bf16[2048,2,192]{0,2,1:T(8,128)(2,1)S(1)} collective-permute-done((bf16[2048,2,192]{0,2,1:T(8,128)(2,1)S(1)}, bf16[2048,2,192]{0,2,1:T(8,128)(2,1)S(1)}, u32[]{:S(2)}, u32[]{:S(2)}) %collective-permute-start.2) | collective-permute-done | bytes 1572896 | tf_op jit(solution)/shard_map/ppermute | solution.py:18
  289.8 5.4 collective-permute-start.3
  295.1 31.2 %collective-permute-done.3 = bf16[2048,2,192]{0,2,1:T(8,128)(2,1)S(1)} collective-permute-done((bf16[2048,2,192]{0,2,1:T(8,128)(2,1)S(1)}, bf16[2048,2,192]{0,2,1:T(8,128)(2,1)S(1)}, u32[]{:S(2)}, u32[]{:S(2)}) %collective-permute-start.3) | collective-permute-done | bytes 1572896 | tf_op jit(solution)/shard_map/ppermute | solution.py:18
  327.5 6.5 collective-permute-start.4
  334.0 29.2 %collective-permute-done.4 = bf16[2048,2,192]{0,2,1:T(8,128)(2,1)} collective-permute-done((bf16[2048,2,192]{0,2,1:T(8,128)(2,1)S(1)}, bf16[2048,2,192]{0,2,1:T(8,128)(2,1)}, u32[]{:S(2)}, u32[]{:S(2)}) %collective-permute-start.4) | collective-permute-done | bytes 1572896 | tf_op jit(solution)/shard_map/ppermute | solution.py:18
  363.2 6.4 collective-permute-start.5
  375.2 29.4 %collective-permute-done.5 = bf16[2048,2,192]{0,2,1:T(8,128)(2,1)} collective-permute-done((bf16[2048,2,192]{0,2,1:T(8,128)(2,1)}, bf16[2048,2,192]{0,2,1:T(8,128)(2,1)}, u32[]{:S(2)}, u32[]{:S(2)}) %collective-permute-start.5) | collective-permute-done | bytes 1572896 | tf_op jit(solution)/shard_map/ppermute | solution.py:18
  404.6 21.5 collective-permute-start.6
  428.9 2.8 fusion.399
  434.4 37.2 %collective-permute-done.6 = bf16[2048,2,192]{0,2,1:T(8,128)(2,1)S(1)} collective-permute-done((bf16[2048,2,192]{0,2,1:T(8,128)(2,1)}, bf16[2048,2,192]{0,2,1:T(8,128)(2,1)S(1)}, u32[]{:S(2)}, u32[]{:S(2)}) %collective-permute-start.6) | collective-permute-done | bytes 1572896 | tf_op jit(solution)/shard_map/ppermute | solution.py:18
  472.9 59.3 %while.445 = (s32[]{:T(128)}, f32[4,512,3,64]{1,3,2,0:T(8,128)}, f32[4,3,512]{2,1,0:T(4,128)}, pred[]{:T(512)}, pred[]{:T(512)}, /*index=5*/pred[]{:T(512)}, pre...) while((s32[]{:T(128)}, f32[4,512,3,64]{1,3,2,0:T(8,128)}, ...), condition=%wide.region_79.80_spmd, body=%wide.region_2.79_spmd.sunk | while | flops 2469948928 | bytes 68133920 | solution.py:136
  483.9 3.6 while.448
  488.3 5.0 while.449
  496.4 5.3 while.448
  502.6 7.5 while.449
  513.2 7.1 while.448
  521.2 10.0 while.449
  540.0 3.9 reshape.401
  544.0 5.0 all-to-all-start.1
  549.1 467.9 %all-gather = bf16[8,1,384]{2,1,0:T(2,128)(2,1)S(1)} all-gather(bf16[1,1,384]{2,1,0:T(2,128)(2,1)S(1)} %reshape.370), channel_id=1, replica_groups=mesh['fsdp'=8,'seq'=4] {'fsdp'}, dimensions={0}, use_global_device_ids=true | all-gather | bytes 6912 | tf_op jit(solution)/shard_map/all_gather | solution.py:238
  1019.7 5.8 copy.164
  1025.5 3.0 all_to_all.51
  1034.7 8.2 fusion.391
  1042.9 11.9 convert_reduce_fusion
  1054.8 3.5 multiply_reduce_fusion.1
  1064.2 9.5 fusion.392
  1073.7 4.8 copy.168
  1078.5 2.9 convolution_convert_fusion
  1083.8 3.5 all-to-all-start.2
  1087.4 8.9 fusion.390
  1100.5 2.8 reshape.343
  1104.3 6.2 broadcast_in_dim.295.clone
  1110.5 6.2 broadcast_in_dim.295
  1116.7 116.5 %while.447 = (s32[]{:T(128)}, bf16[2048,3,64]{0,2,1:T(8,128)(2,1)}, f32[8,2048,3,64]{1,3,2,0:T(8,128)}, f32[8,2048,3,64]{1,3,2,0:T(8,128)}, pred[]{:T(512)}, /*i...) while((s32[]{:T(128)}, bf16[2048,3,64]{0,2,1:T(8,128)(2,1)}, ...), condition=%wide.region_115.116_spmd, body=%wide.region_84.115_spmd.sunk | while | flops 4082925056 | bytes 160622608 | solution.py:207
  1122.4 8.5 while.450
  1138.6 16.9 while.450
  1163.3 25.5 while.450
  1196.6 33.8 %while.450 = (s32[]{:T(128)}, f32[512,3,64]{0,2,1:T(8,128)S(1)}, f32[8,2048,3,64]{1,3,2,0:T(8,128)}, f32[8,2048,3,64]{1,3,2,0:T(8,128)}, s32[]{:T(128)}, /*index...) while((s32[]{:T(128)}, f32[512,3,64]{0,2,1:T(8,128)S(1)}, ...), condition=%wide.region_86.86_spmd, body=%wide.region_85.85_spmd.sunk | while | flops 511935488 | bytes 18704608 | solution.py:79
  1237.3 174.5 %collective-permute-done.7 = bf16[2048,2,3,64]{0,3,2,1:T(8,128)(2,1)S(1)} collective-permute-done((bf16[2048,2,3,64]{0,3,2,1:T(8,128)(2,1)S(1)}, bf16[2048,2,3,64]{0,3,2,1:T(8,128)(2,1)S(1)}, u32[]{:S(2)}, u32[]{:S(2)}) %collective-permute-start.7) | collective-permute-done | bytes 1572896 | tf_op jit(solution)/shard_map/ppermute | solution.py:18
  1413.6 141.3 %collective-permute-done.8 = bf16[2048,2,3,64]{0,3,2,1:T(8,128)(2,1)S(1)} collective-permute-done((bf16[2048,2,3,64]{0,3,2,1:T(8,128)(2,1)S(1)}, bf16[2048,2,3,64]{0,3,2,1:T(8,128)(2,1)S(1)}, u32[]{:S(2)}, u32[]{:S(2)}) %collective-permute-start.8) | collective-permute-done | bytes 1572896 | tf_op jit(solution)/shard_map/ppermute | solution.py:18
  1556.7 189.3 %collective-permute-done.9 = bf16[2048,2,3,64]{0,3,2,1:T(8,128)(2,1)S(1)} collective-permute-done((bf16[2048,2,3,64]{0,3,2,1:T(8,128)(2,1)S(1)}, bf16[2048,2,3,64]{0,3,2,1:T(8,128)(2,1)S(1)}, u32[]{:S(2)}, u32[]{:S(2)}) %collective-permute-start.9) | collective-permute-done | bytes 1572896 | tf_op jit(solution)/shard_map/ppermute | solution.py:18
  1747.9 186.0 %collective-permute-done.10 = bf16[2048,2,3,64]{0,3,2,1:T(8,128)(2,1)S(1)} collective-permute-done((bf16[2048,2,3,64]{0,3,2,1:T(8,128)(2,1)S(1)}, bf16[2048,2,3,64]{0,3,2,1:T(8,128)(2,1)S(1)}, u32[]{:S(2)}, u32[]{:S(2)}) %collective-permute-start.10) | collective-permute-done | bytes 1572896 | tf_op jit(solution)/shard_map/ppermute | solution.py:18
  1935.8 187.2 %collective-permute-done.11 = bf16[2048,2,3,64]{0,3,2,1:T(8,128)(2,1)S(1)} collective-permute-done((bf16[2048,2,3,64]{0,3,2,1:T(8,128)(2,1)S(1)}, bf16[2048,2,3,64]{0,3,2,1:T(8,128)(2,1)S(1)}, u32[]{:S(2)}, u32[]{:S(2)}) %collective-permute-start.11) | collective-permute-done | bytes 1572896 | tf_op jit(solution)/shard_map/ppermute | solution.py:18
  2124.9 184.3 %collective-permute-done.12 = bf16[2048,2,3,64]{0,3,2,1:T(8,128)(2,1)S(1)} collective-permute-done((bf16[2048,2,3,64]{0,3,2,1:T(8,128)(2,1)S(1)}, bf16[2048,2,3,64]{0,3,2,1:T(8,128)(2,1)S(1)}, u32[]{:S(2)}, u32[]{:S(2)}) %collective-permute-start.12) | collective-permute-done | bytes 1572896 | tf_op jit(solution)/shard_map/ppermute | solution.py:18
  2311.2 180.7 %collective-permute-done.13 = bf16[2048,2,3,64]{0,3,2,1:T(8,128)(2,1)S(1)} collective-permute-done((bf16[2048,2,3,64]{0,3,2,1:T(8,128)(2,1)S(1)}, bf16[2048,2,3,64]{0,3,2,1:T(8,128)(2,1)S(1)}, u32[]{:S(2)}, u32[]{:S(2)}) %collective-permute-start.13) | collective-permute-done | bytes 1572896 | tf_op jit(solution)/shard_map/ppermute | solution.py:18
  2492.6 4.8 copy.170
  2497.4 55.1 %all_to_all.63 = bf16[2048,3,1,192]{3,1,2,0:T(4,128)(2,1)} all-to-all(bf16[2048,3,1,192]{3,1,2,0:T(4,128)(2,1)} %copy.170), channel_id=1, replica_groups=mesh['fsdp'=8,'seq'=4] {'seq'}, dimensions={0} | all-to-all | bytes 4718592 | tf_op jit(solution)/shard_map/all_to_all | solution.py:354
  2552.5 7.4 copy.184
  2563.5 5.2 fusion.386
  2570.4 9.0 add_convert_fusion.1
  2581.1 6.0 fusion.393
  2591.5 108.5 %reduce-scatter.5.cloned.1.call-done = f32[768,288]{0,1:T(8,128)} async-done(((f32[768,2304]{0,1:T(8,128)}), f32[768,288]{0,1:T(8,128)}) %reduce-scatter.5.cloned.1.call-update) | async-done | bytes 884752 | tf_op jit(solution)/shard_map/reduce_scatter | solution.py:366
  2707.7 35.7 %all-reduce.17 = (bf16[768]{0:T(1024)(128)(2,1)S(1)}, bf16[768]{0:T(1024)(128)(2,1)S(1)}, bf16[768]{0:T(1024)(128)(2,1)S(1)}, bf16[768]{0:T(1024)(128)(2,1)S(1)}...) all-reduce(f32[768]{0:T(1024)S(1)} %get-tuple-element.4396, ...), channel_id=2, replica_groups=mesh['fsdp'=8,'seq'=4] {'fsdp'}, use_global_device_ids=true, to_apply=%region_119.120.clone | all-reduce | flops 9216 | bytes 55296
  2744.1 6.3 all-reduce.19
  (596 shorter events, 286.3 us)
Async XLA Ops:
  7.2 71.4 %all-gather.6.cloned.1.call-start = ((), (), s32[]{:S(2)}) async-start(), calls=%async_computation.8 | async-start | bytes 3981312 | tf_op jit(solution)/shard_map/all_gather | solution.py:230
  7.9 1022.8 %all-gather.8.cloned.1.call-start = ((), (), s32[]{:S(2)}) async-start(), calls=%async_computation.9 | async-start | bytes 1327104 | tf_op jit(solution)/shard_map/all_gather | solution.py:233
  10.0 68.6 %copy-start.33 = (f32[512]{0:T(512)}, f32[512]{0:T(512)S(1)}, u32[]{:S(2)}) copy-start(f32[512]{0:T(512)S(1)} %broadcast_multiply_fusion.1) | copy-start | bytes 6148
  11.5 49.0 %copy-start.39 = (f32[512]{0:T(512)}, f32[512]{0:T(512)S(1)}, u32[]{:S(2)}) copy-start(f32[512]{0:T(512)S(1)} %fusion.379) | copy-start | bytes 6148
  11.5 67.1 %copy-start.35 = (f32[512]{0:T(512)}, f32[512]{0:T(512)S(1)}, u32[]{:S(2)}) copy-start(f32[512]{0:T(512)S(1)} %fusion.384) | copy-start | bytes 6148
  60.5 18.1 copy-start.31
  60.5 18.1 copy-start.45
  89.0 32.1 %all-to-all-start = ((bf16[512,3,4,192]{0,3,1,2:T(8,128)(2,1)}), bf16[512,3,4,192]{0,3,1,2:T(8,128)(2,1)S(1)}, u32[]{:S(2)}, u32[]{:S(2)}) async-start(bf16[512,3,4,192]{0,3,1,2:T(8,128)(2,1)} %copy.160), calls=%async_computation | async-start | bytes 4718592 | tf_op jit(solution)/shard_map/all_to_all | solution.py:272
  92.6 942.0 %all-gather.10.cloned.1.call-start = ((), (), s32[]{:S(2)}) async-start(), calls=%async_computation.10 | async-start | bytes 5308416 | tf_op jit(solution)/shard_map/all_gather | solution.py:237
  93.4 949.5 %all-gather.12.cloned.1.call-start = ((), (), s32[]{:S(2)}) async-start(), calls=%async_computation.11 | async-start | bytes 5308416 | tf_op jit(solution)/shard_map/all_gather | solution.py:239
  125.8 42.2 %collective-permute-start = (bf16[2048,2,192]{0,2,1:T(8,128)(2,1)S(1)}, bf16[2048,2,192]{0,2,1:T(8,128)(2,1)S(1)}, u32[]{:S(2)}, u32[]{:S(2)}) collective-permute-start(bf16[2048,2,192]{0,2,1:T(8,128)(2,1)S(1)} %slice_bitcast_fusion), channel_id=1, source_target_pairs={{0,4},{4,8},{8,12},{12,16},{16,20},{20,24},{24,28},{1,5},{5,9},{9,... | collective-permute-start | bytes 4718600 | tf_op jit(solution)/shard_map/ppermute | solution.py:18
  168.0 23.6 copy-start.24
  168.0 66.8 %collective-permute-start.1 = (bf16[2048,2,192]{0,2,1:T(8,128)(2,1)S(1)}, bf16[2048,2,192]{0,2,1:T(8,128)(2,1)S(1)}, u32[]{:S(2)}, u32[]{:S(2)}) collective-permute-start(bf16[2048,2,192]{0,2,1:T(8,128)(2,1)S(1)} %collective-permute-done), channel_id=1, source_target_pairs={{0,4},{4,8},{8,12},{12,16},{16,20},{20,24},{24,28},{1,5},{5,9},{9,... | collective-permute-start | bytes 4718600 | tf_op jit(solution)/shard_map/ppermute | solution.py:18
  234.8 21.7 copy-start.28
  234.8 53.9 %collective-permute-start.2 = (bf16[2048,2,192]{0,2,1:T(8,128)(2,1)S(1)}, bf16[2048,2,192]{0,2,1:T(8,128)(2,1)S(1)}, u32[]{:S(2)}, u32[]{:S(2)}) collective-permute-start(bf16[2048,2,192]{0,2,1:T(8,128)(2,1)S(1)} %collective-permute-done.1), channel_id=1, source_target_pairs={{0,4},{4,8},{8,12},{12,16},{16,20},{20,24},{24,28},{1,5},{5,9},{9,... | collective-permute-start | bytes 4718600 | tf_op jit(solution)/shard_map/ppermute | solution.py:18
  289.8 36.6 %collective-permute-start.3 = (bf16[2048,2,192]{0,2,1:T(8,128)(2,1)S(1)}, bf16[2048,2,192]{0,2,1:T(8,128)(2,1)S(1)}, u32[]{:S(2)}, u32[]{:S(2)}) collective-permute-start(bf16[2048,2,192]{0,2,1:T(8,128)(2,1)S(1)} %collective-permute-done.2), channel_id=1, source_target_pairs={{0,4},{4,8},{8,12},{12,16},{16,20},{20,24},{24,28},{1,5},{5,9},{9,... | collective-permute-start | bytes 4718600 | tf_op jit(solution)/shard_map/ppermute | solution.py:18
  327.5 35.7 %collective-permute-start.4 = (bf16[2048,2,192]{0,2,1:T(8,128)(2,1)S(1)}, bf16[2048,2,192]{0,2,1:T(8,128)(2,1)}, u32[]{:S(2)}, u32[]{:S(2)}) collective-permute-start(bf16[2048,2,192]{0,2,1:T(8,128)(2,1)S(1)} %collective-permute-done.3), channel_id=1, source_target_pairs={{0,4},{4,8},{8,12},{12,16},{16,20},{20,24},{24,28},{1,5},{5,9},{9,... | collective-permute-start | bytes 4718600 | tf_op jit(solution)/shard_map/ppermute | solution.py:18
  363.2 41.4 %collective-permute-start.5 = (bf16[2048,2,192]{0,2,1:T(8,128)(2,1)}, bf16[2048,2,192]{0,2,1:T(8,128)(2,1)}, u32[]{:S(2)}, u32[]{:S(2)}) collective-permute-start(bf16[2048,2,192]{0,2,1:T(8,128)(2,1)} %collective-permute-done.4), channel_id=1, source_target_pairs={{0,4},{4,8},{8,12},{12,16},{16,20},{20,24},{24,28},{1,5},{5,9},{9,... | collective-permute-start | bytes 4718600 | tf_op jit(solution)/shard_map/ppermute | solution.py:18
  373.2 53.0 %copy-start.23 = (bf16[2048,2,192]{0,2,1:T(8,128)(2,1)S(1)}, bf16[2048,2,192]{0,2,1:T(8,128)(2,1)}, u32[]{:S(2)}) copy-start(bf16[2048,2,192]{0,2,1:T(8,128)(2,1)} %copy-done.22) | copy-start | bytes 4718596
  374.2 53.3 %copy-start.27 = (bf16[2048,2,192]{0,2,1:T(8,128)(2,1)S(1)}, bf16[2048,2,192]{0,2,1:T(8,128)(2,1)}, u32[]{:S(2)}) copy-start(bf16[2048,2,192]{0,2,1:T(8,128)(2,1)} %copy-done.26) | copy-start | bytes 4718596
  404.6 66.9 %collective-permute-start.6 = (bf16[2048,2,192]{0,2,1:T(8,128)(2,1)}, bf16[2048,2,192]{0,2,1:T(8,128)(2,1)S(1)}, u32[]{:S(2)}, u32[]{:S(2)}) collective-permute-start(bf16[2048,2,192]{0,2,1:T(8,128)(2,1)} %collective-permute-done.5), channel_id=1, source_target_pairs={{0,4},{4,8},{8,12},{12,16},{16,20},{20,24},{24,28},{1,5},{5,9},{9,... | collective-permute-start | bytes 4718600 | tf_op jit(solution)/shard_map/ppermute | solution.py:18
  536.4 12.6 copy-start.53
  536.4 12.7 copy-start.52
  536.4 12.7 copy-start.51
  536.4 12.7 copy-start.50
  544.0 473.1 %all-to-all-start.1 = ((bf16[4,2,49152]{2,1,0:T(2,128)(2,1)}), bf16[4,2,49152]{2,1,0:T(2,128)(2,1)S(1)}, u32[]{:S(2)}, u32[]{:S(2)}) async-start(bf16[4,2,49152]{2,1,0:T(2,128)(2,1)} %reshape.401), calls=%async_computation.1 | async-start | bytes 1572864 | tf_op jit(solution)/shard_map/all_to_all | solution.py:291
  549.0 2030.4 %reduce-scatter.7.cloned.1.call-start = ((), (), s32[]{:S(2)}) async-start(), calls=%async_computation.13 | async-start | bytes 2654208 | tf_op jit(solution)/shard_map/reduce_scatter | solution.py:369
  1017.0 47.2 %copy-start.42 = (f32[8,1,384]{2,1,0:T(1,128)}, f32[8,1,384]{2,1,0:T(1,128)S(1)}, u32[]{:S(2)}) copy-start(f32[8,1,384]{2,1,0:T(1,128)S(1)} %convert_element_type.559) | copy-start | bytes 36868
  1019.7 11.0 copy-start.7
  1034.6 8.3 copy-start.16
  1042.9 11.9 copy-start.13
  1042.9 11.9 copy-start.54
  1059.0 5.2 copy-start.37
  1064.2 1522.9 %reduce-scatter.11.cloned.1.call-start = ((), (), s32[]{:S(2)}) async-start(), calls=%async_computation.15 | async-start | bytes 10616832 | tf_op jit(solution)/shard_map/reduce_scatter | solution.py:375
  1073.7 4.8 copy-start.21
  1083.8 15.2 all-to-all-start.2
  1087.3 1502.0 %reduce-scatter.9.cloned.1.call-start = ((), (), s32[]{:S(2)}) async-start(), calls=%async_computation.14 | async-start | bytes 10616832 | tf_op jit(solution)/shard_map/reduce_scatter | solution.py:373
  1096.3 1603.7 %reduce-scatter.5.cloned.1.call-start = ((), (), s32[]{:S(2)}) async-start(), calls=%async_computation.12 | async-start | bytes 7962624 | tf_op jit(solution)/shard_map/reduce_scatter | solution.py:366
  1116.9 14.0 copy-start.3
  1133.2 22.3 copy-start.3
  1157.8 31.0 %copy-start.3 = (bf16[2048,3,64]{0,2,1:T(8,128)(2,1)}, bf16[2048,3,64]{0,2,1:T(8,128)(2,1)S(1)}, u32[]{:S(2)}) copy-start(bf16[2048,3,64]{0,2,1:T(8,128)(2,1)S(1)} %get-tuple-element.7697) | copy-start | bytes 2359300 | tf_op jit(solution)/shard_map/while
  1191.2 39.3 %copy-start.3 = (bf16[2048,3,64]{0,2,1:T(8,128)(2,1)}, bf16[2048,3,64]{0,2,1:T(8,128)(2,1)S(1)}, u32[]{:S(2)}) copy-start(bf16[2048,3,64]{0,2,1:T(8,128)(2,1)S(1)} %get-tuple-element.7697) | copy-start | bytes 2359300 | tf_op jit(solution)/shard_map/while
  1233.2 178.5 %slice-start = ((s8[12582912]{0:T(1024)(128)(4,1)}), s8[4194304]{0:T(1024)(128)(4,1)S(1)}, s32[]{:S(2)}) async-start(s8[12582912]{0:T(1024)(128)(4,1)} %bitcast.712), calls=%async_computation.17 | async-start | bytes 8388608
  1233.2 178.5 %slice-start.1 = ((s8[12582912]{0:T(1024)(128)(4,1)}), s8[4194304]{0:T(1024)(128)(4,1)S(1)}, s32[]{:S(2)}) async-start(s8[12582912]{0:T(1024)(128)(4,1)} %bitcast.712), calls=%async_computation.18 | async-start | bytes 8388608
  1233.2 178.5 %slice-start.2 = ((s8[12582912]{0:T(1024)(128)(4,1)}), s8[4194304]{0:T(1024)(128)(4,1)S(1)}, s32[]{:S(2)}) async-start(s8[12582912]{0:T(1024)(128)(4,1)} %bitcast.712), calls=%async_computation.19 | async-start | bytes 8388608
  1233.3 178.5 %copy-start = (f32[8,2048,3,64]{1,3,2,0:T(8,128)S(1)}, f32[8,2048,3,64]{1,3,2,0:T(8,128)}, u32[]{:S(2)}) copy-start(f32[8,2048,3,64]{1,3,2,0:T(8,128)} %get-tuple-element.4261) | copy-start | bytes 37748740
  1235.7 176.0 %collective-permute-start.7 = (bf16[2048,2,3,64]{0,3,2,1:T(8,128)(2,1)S(1)}, bf16[2048,2,3,64]{0,3,2,1:T(8,128)(2,1)S(1)}, u32[]{:S(2)}, u32[]{:S(2)}) collective-permute-start(bf16[2048,2,3,64]{0,3,2,1:T(8,128)(2,1)S(1)} %fusion.382), channel_id=1, source_target_pairs={{4,0},{8,4},{12,8},{16,12},{20,16},{24,20},{28,24},{5,1},{9,5},{13... | collective-permute-start | bytes 4718600 | tf_op jit(solution)/shard_map/ppermute | solution.py:18
  1412.3 142.6 %collective-permute-start.8 = (bf16[2048,2,3,64]{0,3,2,1:T(8,128)(2,1)S(1)}, bf16[2048,2,3,64]{0,3,2,1:T(8,128)(2,1)S(1)}, u32[]{:S(2)}, u32[]{:S(2)}) collective-permute-start(bf16[2048,2,3,64]{0,3,2,1:T(8,128)(2,1)S(1)} %fusion.350), channel_id=1, source_target_pairs={{4,0},{8,4},{12,8},{16,12},{20,16},{24,20},{28,24},{5,1},{9,5},{13... | collective-permute-start | bytes 4718600 | tf_op jit(solution)/shard_map/ppermute | solution.py:18
  1555.4 190.6 %collective-permute-start.9 = (bf16[2048,2,3,64]{0,3,2,1:T(8,128)(2,1)S(1)}, bf16[2048,2,3,64]{0,3,2,1:T(8,128)(2,1)S(1)}, u32[]{:S(2)}, u32[]{:S(2)}) collective-permute-start(bf16[2048,2,3,64]{0,3,2,1:T(8,128)(2,1)S(1)} %fusion.354), channel_id=1, source_target_pairs={{4,0},{8,4},{12,8},{16,12},{20,16},{24,20},{28,24},{5,1},{9,5},{13... | collective-permute-start | bytes 4718600 | tf_op jit(solution)/shard_map/ppermute | solution.py:18
  1746.6 187.3 %collective-permute-start.10 = (bf16[2048,2,3,64]{0,3,2,1:T(8,128)(2,1)S(1)}, bf16[2048,2,3,64]{0,3,2,1:T(8,128)(2,1)S(1)}, u32[]{:S(2)}, u32[]{:S(2)}) collective-permute-start(bf16[2048,2,3,64]{0,3,2,1:T(8,128)(2,1)S(1)} %fusion.358), channel_id=1, source_target_pairs={{4,0},{8,4},{12,8},{16,12},{20,16},{24,20},{28,24},{5,1},{9,5},{13... | collective-permute-start | bytes 4718600 | tf_op jit(solution)/shard_map/ppermute | solution.py:18
  1934.5 188.5 %collective-permute-start.11 = (bf16[2048,2,3,64]{0,3,2,1:T(8,128)(2,1)S(1)}, bf16[2048,2,3,64]{0,3,2,1:T(8,128)(2,1)S(1)}, u32[]{:S(2)}, u32[]{:S(2)}) collective-permute-start(bf16[2048,2,3,64]{0,3,2,1:T(8,128)(2,1)S(1)} %fusion.362), channel_id=1, source_target_pairs={{4,0},{8,4},{12,8},{16,12},{20,16},{24,20},{28,24},{5,1},{9,5},{13... | collective-permute-start | bytes 4718600 | tf_op jit(solution)/shard_map/ppermute | solution.py:18
  2123.6 185.6 %collective-permute-start.12 = (bf16[2048,2,3,64]{0,3,2,1:T(8,128)(2,1)S(1)}, bf16[2048,2,3,64]{0,3,2,1:T(8,128)(2,1)S(1)}, u32[]{:S(2)}, u32[]{:S(2)}) collective-permute-start(bf16[2048,2,3,64]{0,3,2,1:T(8,128)(2,1)S(1)} %fusion.366), channel_id=1, source_target_pairs={{4,0},{8,4},{12,8},{16,12},{20,16},{24,20},{28,24},{5,1},{9,5},{13... | collective-permute-start | bytes 4718600 | tf_op jit(solution)/shard_map/ppermute | solution.py:18
  2309.7 182.7 %copy-start.18 = (bf16[2048,3,64]{0,2,1:T(8,128)(2,1)S(1)}, bf16[2048,3,64]{0,2,1:T(8,128)(2,1)}, u32[]{:S(2)}) copy-start(bf16[2048,3,64]{0,2,1:T(8,128)(2,1)} %get-tuple-element.4259) | copy-start | bytes 2359300
  2309.7 182.1 %collective-permute-start.13 = (bf16[2048,2,3,64]{0,3,2,1:T(8,128)(2,1)S(1)}, bf16[2048,2,3,64]{0,3,2,1:T(8,128)(2,1)S(1)}, u32[]{:S(2)}, u32[]{:S(2)}) collective-permute-start(bf16[2048,2,3,64]{0,3,2,1:T(8,128)(2,1)S(1)} %fusion.344), channel_id=1, source_target_pairs={{4,0},{8,4},{12,8},{16,12},{20,16},{24,20},{28,24},{5,1},{9,5},{13... | collective-permute-start | bytes 4718600 | tf_op jit(solution)/shard_map/ppermute | solution.py:18
  2559.9 3.7 copy-start.34
  2559.9 3.7 copy-start.36
  2559.9 3.7 copy-start.46
  2568.7 186.3 %all-reduce.23.cloned.1.call-start = ((), (), s32[]{:S(2)}) async-start(), calls=%async_computation.16 | async-start | bytes 3538944 | tf_op jit(solution)/shard_map/psum | solution.py:381
  2581.1 6.0 copy-start.40
  2702.0 4.1 copy-start.6
  2702.0 4.1 copy-start.17
  2702.0 4.1 copy-start.38
  2702.0 4.1 copy-start.15
  2755.1 5.8 copy-start.30
  (33 other events, 57.1 us)
Sparse Core Ops, SparseCore 0:
  10.2 68.3 all-gather.5
  80.8 39.6 all-gather.7
  122.6 115.1 all-gather.9
  369.8 118.2 all-gather.11
  1064.3 69.7 reduce-scatter.6
  1137.6 162.2 reduce-scatter.10
  1303.5 173.7 reduce-scatter.8
  2568.9 131.0 reduce-scatter.4
  2703.9 45.8 all-reduce.22
where the time goes:
time: 2800 us; the launch traced here: 2770 us
  waiting for transfers between devices  1640 us (59%)
  blocking collectives  605 us (22%)
  matrix products  188 us (7%)
  local copies, waits for them, and re-layouts  128 us (5%)
  starting transfers between devices  110 us (4%)
  other arithmetic  69.6 us (2%)
    ppermute x14, waiting for transfers between devices, from_behind(): return lax.ppermute(array, axis, pairs)  1490 us
    all_gather x1, blocking collectives, on_device(): lax.all_gather(expand_bias, 'fsdp', axis=0, tiled=True)  468 us
    reduce_scatter x1, waiting for transfers between devices, on_device(): lax.psum_scatter(grad_triple_w, 'fsdp', scatter_dimension=1, tiled=True)  109 us
    ppermute x14, starting transfers between devices, from_behind(): return lax.ppermute(array, axis, pairs)  97.1 us
    unnamed x2, blocking collectives  75.9 us
  transfers between devices with their start and end apart: 26, of which 18 were waited for; matrix products, arithmetic and copies ran while one was open for 12% of the time, Pallas kernels for 0%

commit v1 on v0

v1 whole, which is shorter than its diff:
```python
import functools

import jax
import jax.numpy as jnp
from jax import lax
from jax.experimental import pallas as pl
from jax.experimental.pallas import tpu as pltpu
from jax.sharding import Mesh
from jax.sharding import PartitionSpec as P

HEADS = 12
HEAD_DIM = 64
GROUP = 8
EPSILON = 1e-05
NEG = -1e30
LOG2E = 1.4426950408889634
CH = 512
BF = jnp.bfloat16
F32 = jnp.float32
WEIGHT_AXES = ("g", "z", "x")
RING = ("x", "y", "c")
ALL = ("g", "z", "x", "y", "c")
def dotf(a,b): return lax.dot_general(a,b,(((1,),(0,)),((),())),preferred_element_type=jnp.float32)

def fill(kv_ref, kva, vt):
    n=kv_ref.shape[0]
    def body(i,_):
        rows=pl.ds(pl.multiple_of(i*CH,CH),CH)
        blk=kv_ref[rows,:]
        lane=lax.broadcasted_iota(jnp.int32,(CH,128),1)
        one=jnp.where((lane>=64)&(lane<67),1.0,0.0).astype(jnp.bfloat16)
        kva[rows,0:128]=blk
        kva[rows,128:256]=jnp.where(lane<64,blk,one)
        t=blk.T
        cols=pl.ds(pl.multiple_of(i*CH,CH),CH)
        if vt.shape[0]==80:
            vt[0:64,cols]=t[64:128]
            vt[64:80,cols]=jnp.ones((16,CH),jnp.bfloat16)
        else:
            vt[:,cols]=t[0:64]
        return 0
    lax.fori_loop(0,n//CH,body,0)

def pos(j,strips):
    return pl.multiple_of((lax.rem(j,8)*strips+lax.div(j,8))*CH,CH)

def fwd_kernel(strips, unroll, r_ref, qt_ref, kv_ref, ot_ref, lse_ref, kva, vt, m_s, acc):
    r=r_ref[0]; i=pl.program_id(0)
    @pl.when(i==0)
    def _(): fill(kv_ref,kva,vt)
    qt=qt_ref[...]
    m_s[...]=jnp.full(m_s.shape,NEG,jnp.float32)
    acc[...]=jnp.zeros(acc.shape,jnp.float32)
    def step(js,diag):
        ss=[]
        for j in js:
            p0=pos(j,strips)
            s=dotf(kva[pl.ds(p0,CH),:],qt)
            ss.append(s)
        if diag:
            ki=lax.broadcasted_iota(jnp.int32,(CH,CH),0); qi=lax.broadcasted_iota(jnp.int32,(CH,CH),1)
            ss[-1]=jnp.where(ki<=qi,ss[-1],NEG)
        m0=m_s[...]
        m1=m0
        for s in ss: m1=jnp.maximum(m1,jnp.max(s,axis=0,keepdims=True))
        al=jnp.exp2(m0-m1)
        o=acc[...]*al
        for j,s in zip(js,ss):
            p=jnp.exp2(s-m1).astype(jnp.bfloat16)
            o=o+dotf(vt[:,pl.ds(pos(j,strips),CH)],p)
        acc[...]=o
        m_s[...]=m1
    n=i*8+r
    def body(t,_):
        step([t*unroll+u for u in range(unroll)],False); return 0
    nt=lax.div(n,unroll)
    lax.fori_loop(0,nt,body,0)
    def tail(j,_):
        step([j],False); return 0
    lax.fori_loop(nt*unroll,n,tail,0)
    step([n],True)
    o=acc[...]
    l=o[64:65]
    ot_ref[...]=o[0:64]/l
    lse_ref[...]=jnp.broadcast_to(m_s[...]+jnp.log2(l),lse_ref.shape)

def attend(r,qt,kv,unroll=2):
    n=kv.shape[0]; rows=qt.shape[1]; strips=rows//CH
    return pl.pallas_call(functools.partial(fwd_kernel,strips,unroll),
      grid=(strips,),
      in_specs=[pl.BlockSpec(memory_space=pltpu.SMEM),pl.BlockSpec((256,CH),lambda i:(0,i)),pl.BlockSpec((n,128),lambda i:(0,0))],
      out_specs=[pl.BlockSpec((64,CH),lambda i:(0,i)),pl.BlockSpec((8,CH),lambda i:(0,i))],
      out_shape=[jax.ShapeDtypeStruct((64,rows),jnp.float32),jax.ShapeDtypeStruct((8,rows),jnp.float32)],
      scratch_shapes=[pltpu.VMEM((n,256),jnp.bfloat16),pltpu.VMEM((80,n),jnp.bfloat16),pltpu.VMEM((1,CH),jnp.float32),pltpu.VMEM((80,CH),jnp.float32)],
      compiler_params=pltpu.CompilerParams(vmem_limit_bytes=56*2**20),
      cost_estimate=pl.CostEstimate(flops=20_000_000_000,bytes_accessed=8*2**20,transcendentals=n*rows//2),
    )(r,qt,kv)

def bwd_kernel(strips, r_ref, qt_ref, dot_ref, qn_ref, don_ref, kv_ref, dqt_ref, dkv_ref, kva, kt, dkv, dq):
    r=r_ref[0]; i=pl.program_id(0)
    @pl.when(i==0)
    def _():
        fill(kv_ref,kva,kt)
        def z(t,_):
            dkv[pl.ds(pl.multiple_of(t*CH,CH),CH),:]=jnp.zeros((CH,128),jnp.float32); return 0
        lax.fori_loop(0,dkv.shape[0]//CH,z,0)
    dq[...]=jnp.zeros(dq.shape,jnp.float32)
    def step(j,diag):
        p0=pos(j,strips)
        ks=kva[pl.ds(p0,CH),:]
        s=dotf(ks,qt_ref[...])
        if diag:
            ki=lax.broadcasted_iota(jnp.int32,(CH,CH),0); qi=lax.broadcasted_iota(jnp.int32,(CH,CH),1)
            s=jnp.where(ki<=qi,s,NEG)
        p=jnp.exp2(s)
        dp=dotf(ks,dot_ref[...])
        ds=(p*dp).astype(jnp.bfloat16)
        p=p.astype(jnp.bfloat16)
        dkv[pl.ds(p0,CH),:]+=dotf(p,don_ref[...])+dotf(ds,qn_ref[...])
        dq[...]+=dotf(kt[:,pl.ds(p0,CH)],ds)
    n=i*8+r
    def body(j,_):
        step(j,False); return 0
    lax.fori_loop(0,n,body,0)
    step(n,True)
    dqt_ref[...]=(dq[...]*0.125).astype(dqt_ref.dtype)
    @pl.when(i==strips-1)
    def _():
        def w(t,_):
            rows=pl.ds(pl.multiple_of(t*CH,CH),CH)
            dkv_ref[rows,:]=dkv[rows,:].astype(jnp.bfloat16); return 0
        lax.fori_loop(0,dkv.shape[0]//CH,w,0)

def attend_back(r,qt,dot_,qn,don,kv):
    n=kv.shape[0]; rows=qt.shape[1]; strips=rows//CH
    return pl.pallas_call(functools.partial(bwd_kernel,strips),
      grid=(strips,),
      in_specs=[pl.BlockSpec(memory_space=pltpu.SMEM),pl.BlockSpec((256,CH),lambda i:(0,i)),pl.BlockSpec((256,CH),lambda i:(0,i)),
        pl.BlockSpec((CH,128),lambda i:(i,0)),pl.BlockSpec((CH,128),lambda i:(i,0)),pl.BlockSpec((n,128),lambda i:(0,0))],
      out_specs=[pl.BlockSpec((64,CH),lambda i:(0,i)),pl.BlockSpec((n,128),lambda i:(0,0))],
      out_shape=[jax.ShapeDtypeStruct((64,rows),jnp.bfloat16),jax.ShapeDtypeStruct((n,128),jnp.bfloat16)],
      scratch_shapes=[pltpu.VMEM((n,256),jnp.bfloat16),pltpu.VMEM((64,n),jnp.bfloat16),pltpu.VMEM((n,128),jnp.float32),pltpu.VMEM((64,CH),jnp.float32)],
      compiler_params=pltpu.CompilerParams(vmem_limit_bytes=56*2**20),
      cost_estimate=pl.CostEstimate(flops=50_000_000_000,bytes_accessed=12*2**20,transcendentals=n*rows//2),
    )(r,qt,dot_,qn,don,kv)


def layer_norm(value, gain, bias):
    centre = value - jnp.mean(value, axis=-1, keepdims=True)
    spread = jnp.mean(centre * centre, axis=-1, keepdims=True)
    return centre * lax.rsqrt(spread + EPSILON) * gain + bias


def smooth_gelu(value):
    return (
        0.5
        * value
        * (1.0 + jnp.tanh(0.7978845608028654 * (value + 0.044715 * value * value * value)))
    )


def mm(spec, a, b):
    return jnp.einsum(spec, a, b, preferred_element_type=F32)


def low_parts(value, count):
    parts = []
    for _ in range(count):
        part = lax.reduce_precision(value, 8, 7)
        parts.append(part.astype(BF))
        value = value - part
    return parts


def swap(array, axis):
    return lax.ppermute(array, axis, [(0, 1), (1, 0)])


def seq_sum(shard):
    total = shard.astype(F32) + swap(shard, "y").astype(F32)
    total = total.astype(BF)
    return total.astype(F32) + swap(total, "c").astype(F32)


def on_device(
    inputs,
    cotangent,
    first_gain,
    first_bias,
    triple_weight,
    query_bias,
    value_bias,
    out_weight,
    out_bias,
    second_gain,
    second_bias,
    expand_weight,
    expand_bias,
    reduce_weight,
    reduce_bias,
):
    tokens, model = inputs.shape
    hidden_here = expand_weight.shape[1]
    here = out_weight.shape[1]
    three = triple_weight.shape[1]
    shards = lax.axis_size("g") * lax.axis_size("z") * lax.axis_size("x")
    hidden = hidden_here * shards
    zs = lax.axis_size("z")
    z = lax.axis_index("z")
    ring_at = (lax.axis_index("x") * lax.axis_size("y") + lax.axis_index("y")) * lax.axis_size(
        "c"
    ) + lax.axis_index("c")
    ring_at = ring_at.astype(jnp.int32)[None]
    heads = HEADS // zs
    width = heads * HEAD_DIM
    rows = tokens * zs

    small = jnp.concatenate(
        [
            first_gain,
            first_bias,
            query_bias,
            value_bias,
            out_bias,
            second_gain,
            second_bias,
            reduce_bias,
            expand_bias,
        ]
    )
    extra = -(-small.shape[0] // (model * 16)) * 16
    small_rows = jnp.pad(small, (0, extra * model - small.shape[0])).reshape(extra, model)

    x_all = lax.all_gather(inputs, "z", axis=0, tiled=True)
    first_pack = lax.all_gather(
        jnp.concatenate([pad_rows(triple_weight.T), small_rows]), WEIGHT_AXES, axis=0, tiled=False
    )
    padded = first_pack.shape[1] - extra
    triple = first_pack[:, :three].reshape(3 * model, model)
    flat_small = first_pack[:, padded:].reshape(shards, extra * model)
    vectors = [flat_small[:, i * here : (i + 1) * here].reshape(model).astype(F32) for i in range(8)]
    gain1, bias1, q_bias, v_bias, o_bias, gain2, bias2, r_bias = vectors
    e_bias = flat_small[:, 8 * here : 8 * here + hidden_here].reshape(hidden).astype(F32)

    out_t = lax.all_gather(out_weight.T, WEIGHT_AXES, axis=0, tiled=True)
    expand_t = lax.all_gather(expand_weight.T, WEIGHT_AXES, axis=0, tiled=True)
    reduce_t = lax.all_gather(reduce_weight.T, WEIGHT_AXES, axis=0, tiled=True)

    w_q = lax.dynamic_slice_in_dim(triple, z * width, width, 0)
    w_k = lax.dynamic_slice_in_dim(triple, model + z * width, width, 0)
    w_v = lax.dynamic_slice_in_dim(triple, 2 * model + z * width, width, 0)
    w_kv = jnp.stack(
        [w_k.reshape(heads, HEAD_DIM, model), w_v.reshape(heads, HEAD_DIM, model)], axis=1
    )
    w_kv = w_kv.reshape(2 * width, model)
    b_q = lax.dynamic_slice_in_dim(q_bias, z * width, width, 0)
    b_v = lax.dynamic_slice_in_dim(v_bias, z * width, width, 0).reshape(heads, HEAD_DIM)
    b_kv = jnp.stack([jnp.zeros_like(b_v), b_v], axis=1).reshape(2 * width)

    normed1 = layer_norm(x_all.astype(F32), gain1, bias1).astype(BF)
    kv = (mm("tm,fm->tf", normed1, w_kv) + b_kv).astype(BF)
    pairs = [
        lax.all_gather(kv[:, h * 128 : (h + 1) * 128], RING, axis=0, tiled=True)
        for h in range(heads)
    ]
    q_t = (mm("fm,tm->ft", w_q, normed1) + b_q[:, None]).astype(BF)
    blank = jnp.zeros((HEAD_DIM, rows), BF)
    scaled = q_t.astype(F32) * (LOG2E * HEAD_DIM**-0.5)
    q_hi, q_lo = low_parts(scaled, 2)

    outs, lses = [], []
    for h in range(heads):
        part = slice(h * HEAD_DIM, (h + 1) * HEAD_DIM)
        packed = jnp.concatenate([q_hi[part], blank, q_lo[part], blank])
        out_h, lse_h = attend(ring_at, packed, pairs[h], 4)
        outs.append(out_h)
        lses.append(lse_h[0:1])
    out_all = jnp.concatenate(outs)
    att = lax.all_to_all(out_all.astype(BF), "z", split_axis=1, concat_axis=0, tiled=True)

    wide = inputs.astype(F32)
    middle = wide + mm("ft,mf->tm", att, out_t) + o_bias
    normed2 = layer_norm(middle, gain2, bias2).astype(BF)
    pre = mm("tm,hm->th", normed2, expand_t) + e_bias
    act = smooth_gelu(pre).astype(BF)
    result = (middle + mm("th,mh->tm", act, reduce_t) + r_bias).astype(BF)

    grad_reduce_t = mm("tm,th->mh", cotangent, act).astype(BF)
    cot = cotangent.astype(F32)
    grad_reduce_b = jnp.sum(cot, axis=0)
    grad_act = mm("tm,mh->th", cotangent, reduce_t)
    grad_pre_wide = jax.vjp(smooth_gelu, pre)[1](grad_act)[0]
    grad_pre = grad_pre_wide.astype(BF)
    grad_expand_t = mm("th,tm->hm", grad_pre, normed2).astype(BF)
    grad_expand_b = jnp.sum(grad_pre.astype(F32), axis=0)
    grad_mid_norm, grad_gain2, grad_bias2 = jax.vjp(layer_norm, middle, gain2, bias2)[1](
        mm("th,hm->tm", grad_pre, expand_t)
    )
    grad_middle = cot + grad_mid_norm
    grad_branch = grad_middle.astype(BF)
    grad_out_t = mm("tm,ft->mf", grad_branch, att).astype(BF)
    grad_out_b = jnp.sum(grad_branch.astype(F32), axis=0)
    grad_att = mm("mf,tm->ft", out_t, grad_branch).astype(BF)
    grad_heads = lax.all_to_all(grad_att, "z", split_axis=0, concat_axis=1, tiled=True)

    dqs, dkvs = [], []
    for h in range(heads):
        part = slice(h * HEAD_DIM, (h + 1) * HEAD_DIM)
        g_h = grad_heads[part]
        delta = jnp.sum(g_h.astype(F32) * outs[h], axis=0, keepdims=True)
        tail = jnp.zeros((HEAD_DIM - 3, rows), BF)
        q_pack = jnp.concatenate([q_hi[part], blank, q_lo[part], *low_parts(-lses[h], 3), tail])
        g_pack = jnp.concatenate([blank, g_h, blank, *low_parts(-delta, 3), tail])
        q_rows = jnp.concatenate([q_t[part] * BF(0.125), blank]).T
        g_rows = jnp.concatenate([blank, g_h]).T
        dq_h, dkv_h = attend_back(ring_at, q_pack, g_pack, q_rows, g_rows, pairs[h])
        dqs.append(dq_h)
        dkvs.append(lax.psum_scatter(dkv_h, RING, scatter_dimension=0, tiled=True))
    dq = jnp.concatenate(dqs)
    dkv = jnp.concatenate(dkvs, axis=1)

    mlp_pack = jnp.concatenate(
        [
            grad_expand_t.reshape(shards, hidden_here, model),
            grad_out_t.reshape(shards, here, model),
        ],
        axis=1,
    )
    mlp_pack = lax.psum_scatter(mlp_pack, WEIGHT_AXES, scatter_dimension=0, tiled=False)
    grad_reduce_t = lax.psum_scatter(grad_reduce_t, WEIGHT_AXES, scatter_dimension=0, tiled=True)
    mlp_pack = seq_sum(mlp_pack)
    grad_reduce_w = seq_sum(grad_reduce_t).T
    grad_expand_w = mlp_pack[:hidden_here].T
    grad_out_w = mlp_pack[hidden_here:].T

    grad_w_q = mm("ft,tm->fm", dq, normed1)
    grad_w_kv = mm("tf,tm->fm", dkv, normed1).reshape(heads, 2, HEAD_DIM, model)
    grad_q_b = jnp.sum(dq.astype(F32), axis=1)
    grad_v_b = jnp.sum(dkv.astype(F32), axis=0).reshape(heads, 2, HEAD_DIM)[:, 1].reshape(width)
    part_norm = mm("ft,fm->tm", dq, w_q) + mm("tf,fm->tm", dkv, w_kv)
    grad_normed = lax.psum_scatter(part_norm.astype(BF), "z", scatter_dimension=0, tiled=True)
    grad_in_norm, grad_gain1, grad_bias1 = jax.vjp(layer_norm, wide, gain1, bias1)[1](
        grad_normed.astype(F32)
    )
    grad_in = (grad_middle + grad_in_norm).astype(BF)

    triple_grad = jnp.zeros((3 * model, model), BF)
    for at, piece in enumerate(
        (
            grad_w_q,
            grad_w_kv[:, 0].reshape(width, model),
            grad_w_kv[:, 1].reshape(width, model),
        )
    ):
        triple_grad = lax.dynamic_update_slice(
            triple_grad, piece.astype(BF), (at * model + z * width, 0)
        )
    placed_q = lax.dynamic_update_slice(jnp.zeros((model,), F32), grad_q_b, (z * width,))
    placed_v = lax.dynamic_update_slice(jnp.zeros((model,), F32), grad_v_b, (z * width,))
    small_grads = jnp.concatenate(
        [
            v.reshape(shards, -1)
            for v in (
                grad_gain1,
                grad_bias1,
                placed_q,
                placed_v,
                grad_out_b,
                grad_gain2,
                grad_bias2,
                grad_reduce_b,
                grad_expand_b,
            )
        ],
        axis=1,
    )
    small_grads = jnp.pad(small_grads, ((0, 0), (0, extra * model - small_grads.shape[1])))
    last = jnp.concatenate(
        [
            jnp.pad(
                triple_grad.reshape(shards, three, model), ((0, 0), (0, padded - three), (0, 0))
            ),
            small_grads.astype(BF).reshape(shards, extra, model),
        ],
        axis=1,
    )
    last = seq_sum(lax.psum_scatter(last, WEIGHT_AXES, scatter_dimension=0, tiled=False))
    grad_triple_w = last[:three].T
    flat = last[padded:].reshape(-1)
    vecs = [flat[i * here : (i + 1) * here] for i in range(8)]
    grad_e_b = flat[8 * here : 8 * here + hidden_here]
    return (
        result,
        grad_in,
        vecs[0],
        vecs[1],
        grad_triple_w,
        vecs[2],
        vecs[3],
        grad_out_w,
        vecs[4],
        vecs[5],
        vecs[6],
        grad_expand_w,
        grad_e_b,
        grad_reduce_w,
        vecs[7],
    )


def pad_rows(array):
    short = -array.shape[0] % 16
    return jnp.pad(array, ((0, short), (0, 0))) if short else array


def solution(mesh):
    fsdp, seq = mesh.shape["fsdp"], mesh.shape["seq"]
    wide = Mesh(
        mesh.devices.reshape(fsdp // GROUP, GROUP // 2, 2, seq // 2, 2), ("g", "z", "x", "y", "c")
    )
    rows = P(ALL, None)
    vector = P(WEIGHT_AXES)
    matrix = P(None, WEIGHT_AXES)
    return jax.shard_map(
        on_device,
        mesh=wide,
        in_specs=(
            rows,
            rows,
            vector,
            vector,
            matrix,
            vector,
            vector,
            matrix,
            vector,
            vector,
            vector,
            matrix,
            vector,
            matrix,
            vector,
        ),
        out_specs=(
            rows,
            rows,
            vector,
            vector,
            matrix,
            vector,
            vector,
            matrix,
            vector,
            vector,
            vector,
            matrix,
            vector,
            matrix,
            vector,
        ),
        check_vma=False,
    )
```

time: 2800 us -> 1260 us (0.45)
  waiting for transfers between devices: 1640 us -> 741 us
  blocking collectives: 605 us -> 0 us
  Pallas kernels: 0 us -> 237 us
  matrix products: 188 us -> 70.7 us
  starting transfers between devices: 110 us -> 15.7 us
    ppermute x14 -> x6, waiting for transfers between devices: 1490 us -> 21 us  [swap(): return lax.ppermute(array, axis, [(0, 1), (1, 0)])]
    all_gather x1 -> x0, blocking collectives: 468 us -> none  [on_device(): lax.all_gather(expand_bias, 'fsdp', axis=0, tiled=True)]
    all_gather x4 -> x8, waiting for transfers between devices: 18.1 us -> 306 us  [the longest x1 73.2 us: on_device(): reduce_t = lax.all_gather(reduce_weight.T, WEIGHT_AXES, axis=0, tiled=True)]
    reduce_scatter x4 -> x7, waiting for transfers between devices: 109 us -> 385 us  [the longest x1 114 us: on_device(): lax.psum_scatter(mlp_pack, WEIGHT_AXES, scatter_dimension=0, tiled=False)]
    pallas_call x0 -> x6, Pallas kernels: none -> 237 us  [the longest x3 147 us: attend_back(): pl.pallas_call(functools.partial(bwd_kernel, strips), grid=(strips,), in_...]
    dot_general x82 -> x15, matrix products: 188 us -> 70.7 us  [mm(): return jnp.einsum(spec, a, b, preferred_element_type=F32)]
    ppermute x14 -> x6, starting transfers between devices: 97.1 us -> 4.65 us  [swap(): return lax.ppermute(array, axis, [(0, 1), (1, 0)])]
    unnamed x2 -> x0, blocking collectives: 75.9 us -> none
  transfers between devices with their start and end apart: 26 -> 23, of which waited for: 18 -> 19; matrix products, arithmetic and copies ran while one was open for 12% -> 14% of each run, Pallas kernels for 0% -> 15%
where the time goes in v1:
time: 1260 us; the launch traced here: 1250 us
  waiting for transfers between devices  741 us (59%)
  Pallas kernels  237 us (19%)
  local copies, waits for them, and re-layouts  119 us (9%)
  matrix products  70.7 us (6%)
  other arithmetic  53.6 us (4%)
  starting transfers between devices  15.7 us (1%)
  between operations  15.3 us (1%)
    pallas_call x3, Pallas kernels, attend_back(): pl.pallas_call(functools.partial(bwd_kernel, strips), grid=(strips,), in_...  147 us
    reduce_scatter x1, waiting for transfers between devices, on_device(): lax.psum_scatter(mlp_pack, WEIGHT_AXES, scatter_dimension=0, tiled=False)  114 us
    reduce_scatter x3, waiting for transfers between devices, on_device(): dkvs.append(lax.psum_scatter(dkv_h, RING, scatter_dimension=0, tiled=True))  104 us
    reduce_scatter x1, waiting for transfers between devices, on_device(): lax.psum_scatter(grad_reduce_t, WEIGHT_AXES, scatter_dimension=0, tiled=T...  92 us
    pallas_call x3, Pallas kernels, attend(): pl.pallas_call(functools.partial(fwd_kernel, strips, unroll), grid=(strip...  89.1 us
    all_gather x1, waiting for transfers between devices, on_device(): reduce_t = lax.all_gather(reduce_weight.T, WEIGHT_AXES, axis=0, tiled=True)  73.2 us
    all_gather x1, waiting for transfers between devices, on_device(): expand_t = lax.all_gather(expand_weight.T, WEIGHT_AXES, axis=0, tiled=True)  71.3 us
    dot_general x15, matrix products, mm(): return jnp.einsum(spec, a, b, preferred_element_type=F32)  70.7 us
  transfers between devices with their start and end apart: 23, of which 19 were waited for; matrix products, arithmetic and copies ran while one was open for 14% of the time, Pallas kernels for 15%

profile of v1, /device:TPU:0, one launch (start us, length us, event | category | flops | bytes accessed | tf_op | source)
XLA Modules:
  0.0 1251.5 jit_solution(15288478341814397931)
XLA Ops:
  8.0 6.1 concatenate.78
  16.0 59.8 %all-gather.10.cloned.1.call-done = bf16[2048,768]{1,0:T(8,128)(2,1)} async-done(((bf16[512,768]{1,0:T(8,128)(2,1)}), bf16[2048,768]{1,0:T(8,128)(2,1)}) %all-gather.10.cloned.1.call-update) | async-done | bytes 3145744 | tf_op jit(solution)/shard_map/all_gather | solution.py:234
  75.8 2.5 convert_reduce_fusion
  79.7 65.2 %all-gather.24.cloned.1.call-done = bf16[2432,768]{1,0:T(8,128)(2,1)} async-done(((bf16[304,768]{1,0:T(8,128)(2,1)}), bf16[2432,768]{1,0:T(8,128)(2,1)}) %all-gather.24.cloned.1.call-update) | async-done | bytes 3735568 | tf_op jit(solution)/shard_map/all_gather | solution.py:235
  145.9 4.1 slice.200
  154.3 1.8 add_convert_fusion.1
  160.9 3.1 reduce-precision_convert_fusion
  166.1 3.2 pad_maximum_fusion.4
  169.3 2.4 copy.122.qt_ref
  174.6 18.2 %all-gather.16.cloned.1.call-done.kv_ref = bf16[16384,128]{1,0:T(8,128)(2,1)} async-done(((bf16[2048,128]{1,0:T(8,128)(2,1)}), bf16[16384,128]{1,0:T(8,128)(2,1)}) %all-gather.16.cloned.1.call-update) | async-done | bytes 4194320 | tf_op jit(solution)/shard_map/all_gather | solution.py:263
  192.8 29.7 %shard_map.264 = (f32[64,2048]{1,0:T(8,128)}, f32[8,2048]{1,0:T(8,128)}) custom-call(s32[1]{0:T(128)} %bitcast.r_ref, bf16[256,2048]{1,0:T(8,128)(2,1)} %copy.122.qt_ref, bf16[16384,128]{1,0:T(8,128)(2,1)} %all-gather.16.cloned.1.call-done.kv_ref), custom_call_target="tpu_custom_call" | custom-call | flops 20000000000 | bytes 8388608 | tf_op jit(solution)/shard_map/pallas_call | solution.py:89
  223.6 7.7 all-gather.14.cloned.1.call-done.kv_ref
  231.3 29.7 %shard_map.263 = (f32[64,2048]{1,0:T(8,128)}, f32[8,2048]{1,0:T(8,128)}) custom-call(s32[1]{0:T(128)} %bitcast.r_ref, bf16[256,2048]{1,0:T(8,128)(2,1)} %copy.121.qt_ref, bf16[16384,128]{1,0:T(8,128)(2,1)} %all-gather.14.cloned.1.call-done.kv_ref), custom_call_target="tpu_custom_call" | custom-call | flops 20000000000 | bytes 8388608 | tf_op jit(solution)/shard_map/pallas_call | solution.py:89
  262.1 8.4 all-gather.12.cloned.1.call-done.kv_ref
  270.5 29.7 %shard_map.262 = (f32[64,2048]{1,0:T(8,128)}, f32[8,2048]{1,0:T(8,128)}) custom-call(s32[1]{0:T(128)} %bitcast.r_ref, bf16[256,2048]{1,0:T(8,128)(2,1)} %copy.120.qt_ref, bf16[16384,128]{1,0:T(8,128)(2,1)} %all-gather.12.cloned.1.call-done.kv_ref), custom_call_target="tpu_custom_call" | custom-call | flops 20000000000 | bytes 8388608 | tf_op jit(solution)/shard_map/pallas_call | solution.py:89
  302.3 4.9 all-to-all-start
  313.1 2.3 all-gather.18.cloned.1.call-done
  315.4 20.4 %all-to-all-done = bf16[192,4,512]{2,0,1:T(8,128)(2,1)} async-done(((bf16[192,4,512]{2,0,1:T(8,128)(2,1)}), bf16[192,4,512]{2,0,1:T(8,128)(2,1)}, u32[]{:S(2)}, u32[]{:S(2)}) %all-to-all-start) | async-done | bytes 786464 | tf_op jit(solution)/shard_map/all_to_all | solution.py:279
  335.8 2.4 fusion.66
  338.6 71.3 %all-gather.20.cloned.1.call-done = bf16[3072,768]{0,1:T(8,128)(2,1)} async-done(((bf16[384,768]{0,1:T(8,128)(2,1)}), bf16[3072,768]{0,1:T(8,128)(2,1)}) %all-gather.20.cloned.1.call-update) | async-done | bytes 4718608 | tf_op jit(solution)/shard_map/all_gather | solution.py:246
  409.9 7.1 fusion.51
  416.9 73.2 %all-gather.22.cloned.1.call-done = bf16[768,3072]{1,0:T(8,128)(2,1)} async-done(((bf16[96,3072]{1,0:T(8,128)(2,1)}), bf16[768,3072]{1,0:T(8,128)(2,1)}) %all-gather.22.cloned.1.call-update) | async-done | bytes 4718608 | tf_op jit(solution)/shard_map/all_gather | solution.py:247
  490.1 11.6 fusion.52
  501.7 3.5 multiply_reduce_fusion
  510.9 4.3 all-to-all-start.1
  517.6 5.5 concatenate.87
  523.1 2.3 copy.134.qt_ref
  527.5 2.7 fusion.32
  530.3 4.4 all-to-all-done.1
  534.7 1.9 fusion.60
  540.4 2.4 fusion.30
  542.8 5.3 concatenate.88
  549.5 48.9 %shard_map.265 = (bf16[64,2048]{1,0:T(8,128)(2,1)}, bf16[16384,128]{1,0:T(8,128)(2,1)}) custom-call(s32[1]{0:T(128)} %bitcast.r_ref, bf16[256,2048]{1,0:T(8,128)(2,1)} %copy.134.qt_ref, bf16[256,2048]{1,0:T(8,128)(2,1)} %copy.135.dot_ref, bf16[2048,128]{1,0:T(8,128)(2,1)} %pad_bitcast_fusion.5.qn_ref, bf16[2048,128]{1,0:T(8,128)(2,1)} %pad_bitcast_fusion.4.don_ref, ...), custom_call_target="tpu_custom_call" | custom-call | flops 49999998976 | bytes 12582912 | tf_op jit(solution)/shard_map/pallas_call | solution.py:136
  600.8 5.5 concatenate.91
  606.3 2.3 copy.143.qt_ref
  612.7 2.4 fusion.34
  615.0 5.3 concatenate.92
  622.8 49.6 %shard_map.266 = (bf16[64,2048]{1,0:T(8,128)(2,1)}, bf16[16384,128]{1,0:T(8,128)(2,1)}) custom-call(s32[1]{0:T(128)} %bitcast.r_ref, bf16[256,2048]{1,0:T(8,128)(2,1)} %copy.143.qt_ref, bf16[256,2048]{1,0:T(8,128)(2,1)} %copy.144.dot_ref, bf16[2048,128]{1,0:T(8,128)(2,1)} %pad_bitcast_fusion.3.qn_ref, bf16[2048,128]{1,0:T(8,128)(2,1)} %pad_bitcast_fusion.2.don_ref, ...), custom_call_target="tpu_custom_call" | custom-call | flops 49999998976 | bytes 12582912 | tf_op jit(solution)/shard_map/pallas_call | solution.py:136
  676.4 5.5 concatenate.95
  681.9 2.3 copy.152.qt_ref
  686.9 2.4 fusion.38
  689.3 5.3 concatenate.96
  697.0 49.0 %shard_map.267 = (bf16[64,2048]{1,0:T(8,128)(2,1)}, bf16[16384,128]{1,0:T(8,128)(2,1)}) custom-call(s32[1]{0:T(128)} %bitcast.r_ref, bf16[256,2048]{1,0:T(8,128)(2,1)} %copy.152.qt_ref, bf16[256,2048]{1,0:T(8,128)(2,1)} %copy.153.dot_ref, bf16[2048,128]{1,0:T(8,128)(2,1)} %pad_bitcast_fusion.1.qn_ref, bf16[2048,128]{1,0:T(8,128)(2,1)} %pad_bitcast_fusion.don_ref, ...), custom_call_target="tpu_custom_call" | custom-call | flops 49999998976 | bytes 12582912 | tf_op jit(solution)/shard_map/pallas_call | solution.py:136
  747.1 4.7 fusion.44
  753.0 9.5 reduce-scatter.12.cloned.1.call-done
  763.7 94.1 %reduce-scatter.14.cloned.1.call-done = bf16[2048,128]{1,0:T(8,128)(2,1)} async-done(((bf16[16384,128]{1,0:T(8,128)(2,1)}), bf16[2048,128]{1,0:T(8,128)(2,1)}) %reduce-scatter.14.cloned.1.call-update) | async-done | bytes 524304 | tf_op jit(solution)/shard_map/reduce_scatter | solution.py:318
  859.0 6.3 add_convert_fusion
  866.4 8.7 fusion.12
  875.1 6.7 copy.158
  882.9 2.1 convolution_convert_fusion.2
  885.0 4.7 convolution_convert_fusion.1
  889.8 2.9 pad_maximum_fusion
  894.9 2.1 broadcast_in_dim.20
  900.4 3.3 convolution_convert_fusion.4
  905.3 20.5 %reduce-scatter.16.cloned.1.call-done = bf16[512,768]{1,0:T(8,128)(2,1)} async-done(((bf16[2048,768]{1,0:T(8,128)(2,1)}), bf16[512,768]{1,0:T(8,128)(2,1)}) %reduce-scatter.16.cloned.1.call-update) | async-done | bytes 786448 | tf_op jit(solution)/shard_map/reduce_scatter | solution.py:341
  925.7 1.8 fusion.22
  929.0 4.1 pad_maximum_fusion.1
  933.2 92.0 %reduce-scatter.22.cloned.1.call-done = bf16[96,3072]{1,0:T(8,128)(2,1)} async-done(((bf16[768,3072]{1,0:T(8,128)(2,1)}), bf16[96,3072]{1,0:T(8,128)(2,1)}) %reduce-scatter.22.cloned.1.call-update) | async-done | bytes 589840 | tf_op jit(solution)/shard_map/reduce_scatter | solution.py:330
  1026.7 114.1 %reduce-scatter.20.cloned.1.call-done = bf16[1,480,768]{2,1,0:T(8,128)(2,1)} async-done(((bf16[8,480,768]{2,1,0:T(8,128)(2,1)}), bf16[1,480,768]{2,1,0:T(8,128)(2,1)}) %reduce-scatter.20.cloned.1.call-update) | async-done | bytes 737296 | tf_op jit(solution)/shard_map/reduce_scatter | solution.py:329
  1143.8 15.4 %collective-permute-done.2 = bf16[480,768]{1,0:T(8,128)(2,1)} collective-permute-done((bf16[480,768]{1,0:T(8,128)(2,1)}, bf16[480,768]{1,0:T(8,128)(2,1)}, u32[]{:S(2)}, u32[]{:S(2)}) %collective-permute-start.2) | collective-permute-done | bytes 737312 | tf_op jit(solution)/shard_map/ppermute | solution.py:176
  1160.9 9.2 add_convert_fusion.3
  1171.4 55.3 %reduce-scatter.18.cloned.1.call-done = bf16[1,304,768]{2,1,0:T(8,128)(2,1)} async-done(((bf16[8,304,768]{2,1,0:T(8,128)(2,1)}), bf16[1,304,768]{2,1,0:T(8,128)(2,1)}) %reduce-scatter.18.cloned.1.call-update) | async-done | bytes 466960 | tf_op jit(solution)/shard_map/reduce_scatter | solution.py:387
  1229.2 2.8 copy.156
  1233.8 5.5 collective-permute-done
  (313 shorter events, 95.1 us)
Async XLA Ops:
  7.2 68.6 %all-gather.10.cloned.1.call-start = ((), (), s32[]{:S(2)}) async-start(), calls=%async_computation.9 | async-start | bytes 3932160 | tf_op jit(solution)/shard_map/all_gather | solution.py:234
  7.9 137.0 %all-gather.24.cloned.1.call-start = ((), (), s32[]{:S(2)}) async-start(), calls=%async_computation.22 | async-start | bytes 4202496 | tf_op jit(solution)/shard_map/all_gather | solution.py:235
  16.0 176.8 %all-gather.16.cloned.1.call-start = ((), (), s32[]{:S(2)}) async-start(), calls=%async_computation.12 | async-start | bytes 4718592 | tf_op jit(solution)/shard_map/all_gather | solution.py:263
  75.8 2.8 copy-start
  151.5 2.8 copy-start.42
  157.5 73.8 %all-gather.14.cloned.1.call-start = ((), (), s32[]{:S(2)}) async-start(), calls=%async_computation.11 | async-start | bytes 4718592 | tf_op jit(solution)/shard_map/all_gather | solution.py:263
  158.1 112.5 %all-gather.12.cloned.1.call-start = ((), (), s32[]{:S(2)}) async-start(), calls=%async_computation.10 | async-start | bytes 4718592 | tf_op jit(solution)/shard_map/all_gather | solution.py:263
  158.7 156.7 %all-gather.18.cloned.1.call-start = ((), (), s32[]{:S(2)}) async-start(), calls=%async_computation.13 | async-start | bytes 1327104 | tf_op jit(solution)/shard_map/all_gather | solution.py:245
  159.2 250.6 %all-gather.20.cloned.1.call-start = ((), (), s32[]{:S(2)}) async-start(), calls=%async_computation.14 | async-start | bytes 5308416 | tf_op jit(solution)/shard_map/all_gather | solution.py:246
  160.0 330.2 %all-gather.22.cloned.1.call-start = ((), (), s32[]{:S(2)}) async-start(), calls=%async_computation.15 | async-start | bytes 5308416 | tf_op jit(solution)/shard_map/all_gather | solution.py:247
  166.0 3.3 copy-start.10
  166.0 3.3 copy-start.12
  169.3 2.4 copy-start.23
  169.3 3.9 copy-start.22
  300.2 8.0 copy-start.34
  301.4 7.7 copy-start.33
  302.3 7.7 copy-start.32
  302.3 33.5 %all-to-all-start = ((bf16[192,4,512]{2,0,1:T(8,128)(2,1)}), bf16[192,4,512]{2,0,1:T(8,128)(2,1)}, u32[]{:S(2)}, u32[]{:S(2)}) async-start(bf16[192,4,512]{2,0,1:T(8,128)(2,1)} %pad_maximum_fusion.8), calls=%async_computation | async-start | bytes 1572864 | tf_op jit(solution)/shard_map/all_to_all | solution.py:279
  308.1 101.8 %copy-start.58 = (f32[768]{0:T(1024)}, f32[768]{0:T(1024)S(1)}, u32[]{:S(2)}) copy-start(f32[768]{0:T(1024)S(1)} %reshape.429) | copy-start | bytes 9220
  308.2 197.0 %copy-start.49 = (f32[768]{0:T(1024)}, f32[768]{0:T(1024)S(1)}, u32[]{:S(2)}) copy-start(f32[768]{0:T(1024)S(1)} %reshape.428) | copy-start | bytes 9220
  308.2 182.0 %copy-start.51 = (f32[3072]{0:T(1024)}, f32[3072]{0:T(1024)S(1)}, u32[]{:S(2)}) copy-start(f32[3072]{0:T(1024)S(1)} %reshape.430) | copy-start | bytes 36868
  308.2 27.6 %copy-start.1 = (bf16[512,768]{1,0:T(8,128)(2,1)S(1)}, bf16[512,768]{1,0:T(8,128)(2,1)}, u32[]{:S(2)}) copy-start(bf16[512,768]{1,0:T(8,128)(2,1)} %param.15) | copy-start | bytes 2359300
  338.2 167.0 %copy-start.6 = (f32[512,768]{1,0:T(8,128)}, f32[512,768]{1,0:T(8,128)S(1)}, u32[]{:S(2)}) copy-start(f32[512,768]{1,0:T(8,128)S(1)} %get-tuple-element.178) | copy-start | bytes 4718596
  338.2 167.0 %copy-start.46 = (f32[512]{0:T(512)}, f32[512]{0:T(512)S(1)}, u32[]{:S(2)}) copy-start(f32[512]{0:T(512)S(1)} %broadcast_multiply_fusion.2) | copy-start | bytes 6148
  338.6 166.7 %copy-start.53 = (f32[512]{0:T(512)}, f32[512]{0:T(512)S(1)}, u32[]{:S(2)}) copy-start(f32[512]{0:T(512)S(1)} %fusion.47) | copy-start | bytes 6148
  338.6 151.6 %copy-start.26 = (bf16[512,768]{1,0:T(8,128)(2,1)S(1)}, bf16[512,768]{1,0:T(8,128)(2,1)}, u32[]{:S(2)}) copy-start(bf16[512,768]{1,0:T(8,128)(2,1)} %param.16) | copy-start | bytes 2359300
  490.1 11.6 copy-start.62
  501.7 3.5 copy-start.64
  505.9 3.1 copy-start.63
  509.8 6.0 copy-start.20
  510.9 6.2 copy-start.31
  510.9 23.8 %all-to-all-start.1 = ((bf16[4,192,512]{2,1,0:T(8,128)(2,1)}), bf16[4,192,512]{2,1,0:T(8,128)(2,1)}, u32[]{:S(2)}, u32[]{:S(2)}) async-start(bf16[4,192,512]{2,1,0:T(8,128)(2,1)} %bitcast.13), calls=%async_computation.1 | async-start | bytes 1572864 | tf_op jit(solution)/shard_map/all_to_all | solution.py:304
  515.3 2.3 copy-start.19
  515.3 236.5 %reduce-scatter.10.cloned.1.call-start = ((), (), s32[]{:S(2)}) async-start(), calls=%async_computation.16 | async-start | bytes 4718592 | tf_op jit(solution)/shard_map/reduce_scatter | solution.py:318
  598.4 2.4 copy-start.13
  598.4 2.4 copy-start.17
  598.5 164.1 %reduce-scatter.12.cloned.1.call-start = ((), (), s32[]{:S(2)}) async-start(), calls=%async_computation.17 | async-start | bytes 4718592 | tf_op jit(solution)/shard_map/reduce_scatter | solution.py:318
  606.3 3.7 copy-start.35
  672.4 4.0 copy-start.11
  672.4 4.0 copy-start.15
  672.5 185.4 %reduce-scatter.14.cloned.1.call-start = ((), (), s32[]{:S(2)}) async-start(), calls=%async_computation.18 | async-start | bytes 4718592 | tf_op jit(solution)/shard_map/reduce_scatter | solution.py:318
  746.0 179.7 %reduce-scatter.16.cloned.1.call-start = ((), (), s32[]{:S(2)}) async-start(), calls=%async_computation.19 | async-start | bytes 3932160 | tf_op jit(solution)/shard_map/reduce_scatter | solution.py:341
  751.8 107.2 %copy-start.30 = (bf16[3,2,64,768]{3,2,1,0:T(8,128)(2,1)S(1)}, bf16[3,2,64,768]{3,2,1,0:T(8,128)(2,1)}, u32[]{:S(2)}) copy-start(bf16[3,2,64,768]{3,2,1,0:T(8,128)(2,1)} %copy-done.29) | copy-start | bytes 1769476
  865.3 160.0 %reduce-scatter.22.cloned.1.call-start = ((), (), s32[]{:S(2)}) async-start(), calls=%async_computation.23 | async-start | bytes 5308416 | tf_op jit(solution)/shard_map/reduce_scatter | solution.py:330
  881.8 3.2 copy-start.47
  881.8 3.2 copy-start.50
  881.8 3.2 copy-start.54
  881.8 3.2 copy-start.59
  881.8 259.0 %reduce-scatter.20.cloned.1.call-start = ((), (), s32[]{:S(2)}) async-start(), calls=%async_computation.21 | async-start | bytes 6635520 | tf_op jit(solution)/shard_map/reduce_scatter | solution.py:329
  892.7 333.9 %reduce-scatter.18.cloned.1.call-start = ((), (), s32[]{:S(2)}) async-start(), calls=%async_computation.20 | async-start | bytes 4202496 | tf_op jit(solution)/shard_map/reduce_scatter | solution.py:387
  894.9 3.2 copy-start.25
  903.7 22.0 %copy-start.43 = (f32[768]{0:T(1024)S(1)}, f32[768]{0:T(1024)}, u32[]{:S(2)}) copy-start(f32[768]{0:T(1024)} %copy-done.42) | copy-start | bytes 9220
  933.2 209.1 %copy-start.48 = (f32[8,96]{1,0:T(8,128)S(1)}, f32[8,96]{1,0:T(8,128)}, u32[]{:S(2)}) copy-start(f32[8,96]{1,0:T(8,128)} %get-tuple-element.153) | copy-start | bytes 9220
  933.2 227.7 %copy-start.8 = (f32[512,768]{1,0:T(8,128)S(1)}, f32[512,768]{1,0:T(8,128)}, u32[]{:S(2)}) copy-start(f32[512,768]{1,0:T(8,128)} %copy-done.6) | copy-start | bytes 4718596
  1025.3 117.1 %collective-permute-start.4 = (bf16[96,3072]{1,0:T(8,128)(2,1)}, bf16[96,3072]{1,0:T(8,128)(2,1)}, u32[]{:S(2)}, u32[]{:S(2)}) collective-permute-start(bf16[96,3072]{1,0:T(8,128)(2,1)} %reduce-scatter.22.cloned.1.call-done), channel_id=1, source_target_pairs={{0,2},{2,0},{1,3},{3,1},{4,6},{6,4},{5,7},{7,5},{8,10},{10,8},{9,1... | collective-permute-start | bytes 1769480 | tf_op jit(solution)/shard_map/ppermute | solution.py:176
  1140.8 18.4 %collective-permute-start.2 = (bf16[480,768]{1,0:T(8,128)(2,1)}, bf16[480,768]{1,0:T(8,128)(2,1)}, u32[]{:S(2)}, u32[]{:S(2)}) collective-permute-start(bf16[480,768]{1,0:T(8,128)(2,1)} %bitcast.129), channel_id=1, source_target_pairs={{0,2},{2,0},{1,3},{3,1},{4,6},{6,4},{5,7},{7,5},{8,10},{10,8},{9,1... | collective-permute-start | bytes 2211848 | tf_op jit(solution)/shard_map/ppermute | solution.py:176
  1143.8 26.3 %collective-permute-start.5 = (bf16[96,3072]{1,0:T(8,128)(2,1)S(1)}, bf16[96,3072]{1,0:T(8,128)(2,1)S(1)}, u32[]{:S(2)}, u32[]{:S(2)}) collective-permute-start(bf16[96,3072]{1,0:T(8,128)(2,1)S(1)} %add_convert_fusion.6), channel_id=1, source_target_pairs={{0,1},{1,0},{2,3},{3,2},{4,5},{5,4},{6,7},{7,6},{8,9},{9,8},{10,11... | collective-permute-start | bytes 1769480 | tf_op jit(solution)/shard_map/ppermute | solution.py:176
  1160.8 10.4 collective-permute-start.3
  1171.4 56.8 %copy-start.9 = (f32[480,768]{1,0:T(8,128)}, f32[480,768]{1,0:T(8,128)S(1)}, u32[]{:S(2)}) copy-start(f32[480,768]{1,0:T(8,128)S(1)} %convert_add_fusion.1) | copy-start | bytes 4423684
  1226.6 12.6 %collective-permute-start = (bf16[304,768]{1,0:T(8,128)(2,1)}, bf16[304,768]{1,0:T(8,128)(2,1)}, u32[]{:S(2)}, u32[]{:S(2)}) collective-permute-start(bf16[304,768]{1,0:T(8,128)(2,1)} %bitcast.133), channel_id=1, source_target_pairs={{0,2},{2,0},{1,3},{3,1},{4,6},{6,4},{5,7},{7,5},{8,10},{10,8},{9,1... | collective-permute-start | bytes 1400840 | tf_op jit(solution)/shard_map/ppermute | solution.py:176
  1229.2 11.4 copy-start.4
  1229.2 11.4 copy-start.45
  1232.0 8.6 copy-start.28
  1240.5 1.9 collective-permute-start.1
  (24 other events, 33.8 us)
Sparse Core Ops, SparseCore 0:
  9.6 66.1 all-gather.9
  78.6 66.2 all-gather.23
  157.6 35.1 all-gather.15
  194.5 36.7 all-gather.13
  233.6 36.8 all-gather.11
  272.6 42.7 all-gather.17
  317.4 92.3 all-gather.19
  412.0 78.0 all-gather.21
  598.6 68.6 reduce-scatter.9
  672.6 89.9 reduce-scatter.11
  765.9 91.8 reduce-scatter.13
  865.4 60.2 reduce-scatter.15
  929.8 95.3 reduce-scatter.21
  1029.2 111.5 reduce-scatter.19
  1144.8 81.8 reduce-scatter.17

commit v2 on v1

v2 whole, which is shorter than its diff:
```python
import functools

import jax
import jax.numpy as jnp
from jax import lax
from jax.experimental import pallas as pl
from jax.experimental.pallas import tpu as pltpu
from jax.sharding import Mesh
from jax.sharding import PartitionSpec as P

HEADS = 12
HEAD_DIM = 64
GROUP = 8
EPSILON = 1e-05
NEG = -1e30
LOG2E = 1.4426950408889634
CH = 512
BF = jnp.bfloat16
F32 = jnp.float32
WEIGHT_AXES = ("g", "z", "x")
RING = ("x", "y", "c")
ALL = ("g", "z", "x", "y", "c")


def dotf(a, b):
    return lax.dot_general(a, b, (((1,), (0,)), ((), ())), preferred_element_type=F32)


def block_at(index):
    return pl.ds(pl.multiple_of(index * CH, CH), CH)


def fill_keys(kv_ref, wide, turned, first, ones):
    lane = lax.broadcasted_iota(jnp.int32, (CH, 128), 1)
    unit = jnp.where((lane >= 64) & (lane < 67), 1.0, 0.0).astype(BF)

    def body(i, _):
        at = block_at(i)
        block = kv_ref[at, :]
        wide[at, 0:128] = block
        wide[at, 128:256] = jnp.where(lane < 64, block, unit)
        turned[0:64, at] = block.T[first : first + 64]
        if ones:
            turned[64:80, at] = jnp.ones((16, CH), BF)
        return 0

    lax.fori_loop(0, kv_ref.shape[0] // CH, body, 0)


def split_low(value, count):
    parts = []
    for _ in range(count):
        part = value.astype(BF)
        parts.append(part)
        value = value - part.astype(F32)
    return parts


def pack_query(pack, query):
    hi, lo = split_low(query.astype(F32) * (LOG2E * 0.125), 2)
    pack[0:64, :] = hi
    pack[64:128, :] = jnp.zeros((64, CH), BF)
    pack[128:192, :] = lo
    pack[192:256, :] = jnp.zeros((64, CH), BF)


def pack_shift(pack, shift):
    parts = [jnp.broadcast_to(p.astype(F32), (16, CH)) for p in split_low(shift, 3)]
    at = lax.broadcasted_iota(jnp.int32, (16, CH), 0)
    rows = jnp.where(at == 0, parts[0], jnp.where(at == 1, parts[1], parts[2]))
    pack[192:208, :] = jnp.where(at < 3, rows, 0.0).astype(BF)


def flip_of(info, strip):
    return 7 * lax.rem(strip + info[1], 2)


def key_place(info, chunk, strips):
    strip = lax.div(chunk, 8)
    holder = lax.rem(chunk, 8) ^ flip_of(info, strip) ^ info[2]
    return holder * strips + strip


def causal(scores):
    key = lax.broadcasted_iota(jnp.int32, scores.shape, 0)
    query = lax.broadcasted_iota(jnp.int32, scores.shape, 1)
    return jnp.where(key <= query, scores, NEG)


def forward_kernel(
    strips, unroll, r_ref, q_ref, kv_ref, out_ref, lse_ref, wide, turned, pack, top_s, acc
):
    i = pl.program_id(0)
    count = i * 8 + (r_ref[0] ^ flip_of(r_ref, i))

    @pl.when(i == 0)
    def _():
        fill_keys(kv_ref, wide, turned, 64, True)

    pack_query(pack, q_ref[...])
    top_s[...] = jnp.full(top_s.shape, NEG, F32)
    acc[...] = jnp.zeros(acc.shape, F32)

    def step(chunks, last):
        places = [block_at(key_place(r_ref, c, strips)) for c in chunks]
        scores = [dotf(wide[at, :], pack[...]) for at in places]
        if last:
            scores[-1] = causal(scores[-1])
        before = top_s[...]
        top = before
        for s in scores:
            top = jnp.maximum(top, jnp.max(s, axis=0, keepdims=True))
        total = acc[...] * jnp.exp2(before - top)
        for at, s in zip(places, scores):
            total = total + dotf(turned[:, at], jnp.exp2(s - top).astype(BF))
        acc[...] = total
        top_s[...] = top

    def many(t, _):
        step([t * unroll + u for u in range(unroll)], False)
        return 0

    def single(c, _):
        step([c], False)
        return 0

    rounds = lax.div(count, unroll)
    lax.fori_loop(0, rounds, many, 0)
    lax.fori_loop(rounds * unroll, count, single, 0)
    step([count], True)
    mass = acc[64:65, :]
    out_ref[...] = acc[0:64, :] / mass
    lse_ref[...] = jnp.broadcast_to(top_s[...] + jnp.log2(mass), lse_ref.shape)


def attend(r, query, kv, unroll=4):
    keys, rows = kv.shape[0], query.shape[1]
    strips = rows // CH
    return pl.pallas_call(
        functools.partial(forward_kernel, strips, unroll),
        grid=(strips,),
        in_specs=[
            pl.BlockSpec(memory_space=pltpu.SMEM),
            pl.BlockSpec((64, CH), lambda i: (0, i)),
            pl.BlockSpec((keys, 128), lambda i: (0, 0)),
        ],
        out_specs=[
            pl.BlockSpec((64, CH), lambda i: (0, i)),
            pl.BlockSpec((8, CH), lambda i: (0, i)),
        ],
        out_shape=[
            jax.ShapeDtypeStruct((64, rows), F32),
            jax.ShapeDtypeStruct((8, rows), F32),
        ],
        scratch_shapes=[
            pltpu.VMEM((keys, 256), BF),
            pltpu.VMEM((80, keys), BF),
            pltpu.VMEM((256, CH), BF),
            pltpu.VMEM((1, CH), F32),
            pltpu.VMEM((80, CH), F32),
        ],
        compiler_params=pltpu.CompilerParams(vmem_limit_bytes=56 * 2**20),
        cost_estimate=pl.CostEstimate(
            flops=40 * 10**9, bytes_accessed=8 * 2**20, transcendentals=keys * rows // 2
        ),
    )(r, query, kv)


def backward_kernel(
    strips,
    unroll,
    r_ref,
    q_ref,
    g_ref,
    out_ref,
    lse_ref,
    kv_ref,
    dq_ref,
    dkv_ref,
    wide,
    turned,
    dkv,
    dq,
    q_pack,
    g_pack,
    q_rows,
    g_rows,
):
    i = pl.program_id(0)
    count = i * 8 + (r_ref[0] ^ flip_of(r_ref, i))

    @pl.when(i == 0)
    def _():
        fill_keys(kv_ref, wide, turned, 0, False)

        def clear(t, _):
            dkv[block_at(t), :] = jnp.zeros((CH, 128), F32)
            return 0

        lax.fori_loop(0, dkv.shape[0] // CH, clear, 0)

    query, grad = q_ref[...], g_ref[...]
    blank = jnp.zeros((64, CH), BF)
    pack_query(q_pack, query)
    pack_shift(q_pack, -lse_ref[0:1, :])
    g_pack[0:64, :] = blank
    g_pack[64:128, :] = grad
    g_pack[128:256, :] = jnp.zeros((128, CH), BF)
    pack_shift(g_pack, -jnp.sum(grad.astype(F32) * out_ref[...], axis=0, keepdims=True))
    q_rows[...] = jnp.concatenate([query * BF(0.125), blank]).T
    g_rows[...] = jnp.concatenate([blank, grad]).T
    dq[...] = jnp.zeros(dq.shape, F32)

    def step(chunks, last):
        places = [block_at(key_place(r_ref, c, strips)) for c in chunks]
        scores = [dotf(wide[at, :], q_pack[...]) for at in places]
        grads = [dotf(wide[at, :], g_pack[...]) for at in places]
        if last:
            scores[-1] = causal(scores[-1])
        total = dq[...]
        for at, s, g in zip(places, scores, grads):
            p = jnp.exp2(s)
            ds = (p * g).astype(BF)
            dkv[at, :] += dotf(p.astype(BF), g_rows[...]) + dotf(ds, q_rows[...])
            total = total + dotf(turned[:, at], ds)
        dq[...] = total

    def many(t, _):
        step([t * unroll + u for u in range(unroll)], False)
        return 0

    def single(c, _):
        step([c], False)
        return 0

    rounds = lax.div(count, unroll)
    lax.fori_loop(0, rounds, many, 0)
    if unroll > 1:
        lax.fori_loop(rounds * unroll, count, single, 0)
    step([count], True)
    dq_ref[...] = (dq[...] * 0.125).astype(dq_ref.dtype)

    @pl.when(i == strips - 1)
    def _():
        def write(t, _):
            dkv_ref[block_at(t), :] = dkv[block_at(t), :].astype(BF)
            return 0

        lax.fori_loop(0, dkv.shape[0] // CH, write, 0)


def attend_back(r, query, grad, out, lse, kv, unroll=2):
    keys, rows = kv.shape[0], query.shape[1]
    strips = rows // CH
    strip = pl.BlockSpec((64, CH), lambda i: (0, i))
    whole = pl.BlockSpec((keys, 128), lambda i: (0, 0))
    return pl.pallas_call(
        functools.partial(backward_kernel, strips, unroll),
        grid=(strips,),
        in_specs=[
            pl.BlockSpec(memory_space=pltpu.SMEM),
            strip,
            strip,
            strip,
            pl.BlockSpec((8, CH), lambda i: (0, i)),
            whole,
        ],
        out_specs=[strip, whole],
        out_shape=[
            jax.ShapeDtypeStruct((64, rows), BF),
            jax.ShapeDtypeStruct((keys, 128), BF),
        ],
        scratch_shapes=[
            pltpu.VMEM((keys, 256), BF),
            pltpu.VMEM((64, keys), BF),
            pltpu.VMEM((keys, 128), F32),
            pltpu.VMEM((64, CH), F32),
            pltpu.VMEM((256, CH), BF),
            pltpu.VMEM((256, CH), BF),
            pltpu.VMEM((CH, 128), BF),
            pltpu.VMEM((CH, 128), BF),
        ],
        compiler_params=pltpu.CompilerParams(vmem_limit_bytes=56 * 2**20),
        cost_estimate=pl.CostEstimate(
            flops=100 * 10**9, bytes_accessed=12 * 2**20, transcendentals=keys * rows // 2
        ),
    )(r, query, grad, out, lse, kv)


def normalise(value):
    centre = value - jnp.mean(value, axis=-1, keepdims=True)
    spread = jnp.mean(centre * centre, axis=-1, keepdims=True)
    root = lax.rsqrt(spread + EPSILON)
    return centre * root, root


def normalise_back(grad, unit, root, gain):
    f = grad * gain
    first = jnp.mean(f, axis=-1, keepdims=True)
    second = jnp.mean(f * unit, axis=-1, keepdims=True)
    return root * (f - first - unit * second)


def smooth_gelu(value):
    return (
        0.5
        * value
        * (1.0 + jnp.tanh(0.7978845608028654 * (value + 0.044715 * value * value * value)))
    )


def mm(spec, a, b):
    return jnp.einsum(spec, a, b, preferred_element_type=F32)


def swap(array, axis):
    return lax.ppermute(array, axis, [(0, 1), (1, 0)])


def swap_sum(array, axis):
    return array.astype(F32) + swap(array, axis).astype(F32)


def in_order(at, own, other, axis):
    return jnp.where(
        at == 0, jnp.concatenate([own, other], axis), jnp.concatenate([other, own], axis)
    )


def part(array, index, size, axis):
    return lax.dynamic_slice_in_dim(array, index * size, size, axis)


def pad_rows(array, rows):
    return jnp.pad(array, ((0, rows - array.shape[0]), (0, 0)))


def spread_groups(blocks, depth, ring):
    return [
        [b * depth * ring + z * ring + (r if z % 2 == 0 else ring - 1 - r) for z in range(depth)]
        for b in range(blocks)
        for r in range(ring)
    ]


def by_ring(array, ring, distance):
    size = lax.axis_size("g") * lax.axis_size("z")
    pairs = [
        (b * ring + r, b * ring + (r ^ distance)) for b in range(size) for r in range(ring)
    ]
    return lax.ppermute(array, ALL, pairs)


def fetch_triple(triple_weight, small, at):
    z, x, c = at
    turned = triple_weight.T
    three, model = turned.shape
    half = model // 2
    width = model // 4
    extra = small.shape[0] // half
    mine = jnp.concatenate([part(turned, c, half, 1), pad_rows(small.reshape(extra, half), 16)])
    both = in_order(x, mine[None], swap(mine, "x")[None], 0)
    pairs = both[:, :three].reshape(3, width, half)
    pairs = jnp.concatenate([pairs, jnp.zeros((1, width, half), BF)])
    slots = lax.dynamic_slice_in_dim(jnp.concatenate([pairs, pairs]), z, 4, 0)
    vectors = pad_rows(both[:, three : three + extra].reshape(2 * extra, half), 16)
    slots = jnp.concatenate([slots, jnp.broadcast_to(vectors, (4, 16, half))], axis=1)
    got = lax.all_to_all(slots, "z", split_axis=0, concat_axis=0, tiled=True)
    own = jnp.concatenate(
        [
            lax.dynamic_index_in_dim(got, (z + 4 * kind) // 3, 0, keepdims=False)[:width]
            for kind in range(3)
        ]
    )
    weights = in_order(c, own, swap(own, "c"), 1)
    return weights, got[:, width : width + 2 * extra].reshape(8, extra * half)


def fetch_triple_whole(triple_weight, small, at):
    z, x, c = at
    model = triple_weight.shape[0]
    width = model // 4
    whole = lax.all_gather(triple_weight.T, WEIGHT_AXES, axis=0, tiled=True)
    vectors = lax.all_gather(small, WEIGHT_AXES, axis=0, tiled=False)
    rows = [lax.dynamic_slice_in_dim(whole, k * model + z * width, width, 0) for k in range(3)]
    return jnp.concatenate(rows), vectors


def send_triple(grads, small, at):
    z, x, c = at
    model = grads.shape[1]
    half = model // 2
    width = model // 4
    three = 3 * width // 2
    extra = small.shape[1] // half
    low = grads.astype(BF)
    vectors = small.astype(BF).reshape(8 * extra, half)
    vectors = pad_rows(vectors, 32)
    mine = jnp.concatenate([part(low, c, half, 1), vectors])
    other = jnp.concatenate([part(low, 1 - c, half, 1), vectors])
    total = (mine.astype(F32) + swap(other, "c").astype(F32)).astype(BF)
    total = swap_sum(total, "y").astype(BF)
    by_depth = total[3 * width : 3 * width + 8 * extra].reshape(4, 2 * extra, half)
    by_depth = jnp.pad(by_depth, ((0, 0), (0, 16 - 2 * extra), (0, 0)))
    slots = jnp.zeros((4, width, half), BF)
    for kind in range(3):
        piece = total[kind * width : (kind + 1) * width][None]
        slots = lax.dynamic_update_slice(slots, piece, ((z + 4 * kind) // 3, 0, 0))
    got = lax.all_to_all(
        jnp.concatenate([slots, by_depth], axis=1), "z", split_axis=0, concat_axis=0, tiled=True
    )
    pairs = jnp.concatenate(
        [
            lax.dynamic_index_in_dim(got, (i - z) % 4, 0, keepdims=False)[:width]
            for i in range(3)
        ]
    )
    sums = jnp.sum(got[:, width : width + 2 * extra].astype(F32), axis=0).astype(BF)

    def portion(index):
        rows = part(pairs, index, three, 0)
        return jnp.concatenate([rows, pad_rows(part(sums, index, extra, 0), 16)])

    total = portion(x).astype(F32) + swap(portion(1 - x), "x").astype(F32)
    own = total[:three].astype(BF)
    shard = in_order(c, own, swap(own, "c"), 1).astype(F32)
    return shard.T, total[three : three + extra].reshape(-1)


def send_triple_whole(grads, small, at):
    z, x, c = at
    model = grads.shape[1]
    width = model // 4
    whole = jnp.zeros((3 * model, model), BF)
    for kind in range(3):
        piece = grads[kind * width : (kind + 1) * width].astype(BF)
        whole = lax.dynamic_update_slice(whole, piece, (kind * model + z * width, 0))
    shard = lax.psum_scatter(whole, WEIGHT_AXES, scatter_dimension=0, tiled=True)
    vectors = lax.psum_scatter(small, WEIGHT_AXES, scatter_dimension=0, tiled=False)
    shard = swap_sum(swap_sum(shard, "y").astype(BF), "c")
    return shard.T, swap_sum(swap_sum(vectors, "y"), "c")


def on_device(
    inputs,
    cotangent,
    first_gain,
    first_bias,
    triple_weight,
    query_bias,
    value_bias,
    out_weight,
    out_bias,
    second_gain,
    second_bias,
    expand_weight,
    expand_bias,
    reduce_weight,
    reduce_bias,
):
    tokens, model = inputs.shape
    hidden_here = expand_weight.shape[1]
    here = out_weight.shape[1]
    blocks, depth = lax.axis_size("g"), lax.axis_size("z")
    shards = blocks * depth * lax.axis_size("x")
    ring = lax.axis_size("x") * lax.axis_size("y") * lax.axis_size("c")
    z, x, y, c = [lax.axis_index(name).astype(jnp.int32) for name in ("z", "x", "y", "c")]
    at = (z, x, c)
    r = (x * lax.axis_size("y") + y) * lax.axis_size("c") + c
    heads = HEADS // depth
    width = heads * HEAD_DIM
    half_hidden = hidden_here // 2
    half_model = model // 2
    groups = spread_groups(blocks, depth, ring)
    info_far = jnp.stack([r, z % 2, r])
    info_abs = jnp.stack([r, z % 2, jnp.zeros_like(r)])
    special = shards == 8 and blocks == 1

    small = jnp.concatenate(
        [
            first_gain,
            first_bias,
            query_bias,
            value_bias,
            out_bias,
            second_gain,
            second_bias,
            reduce_bias,
            expand_bias,
        ]
    )
    x_all = lax.all_gather(inputs, ALL, axis_index_groups=groups, axis=0, tiled=True)
    weights, flat_small = (fetch_triple if special else fetch_triple_whole)(
        triple_weight, small, at
    )
    vectors = [flat_small[:, i * here : (i + 1) * here].reshape(model).astype(F32) for i in range(8)]
    gain1, bias1, q_bias, v_bias, o_bias, gain2, bias2, r_bias = vectors
    e_bias = flat_small[:, 8 * here : 8 * here + hidden_here].astype(F32)

    w_q = weights[:width]
    w_kv = weights[width:].reshape(2, heads, HEAD_DIM, model).transpose(1, 0, 2, 3)
    w_kv = w_kv.reshape(2 * width, model)
    b_q = part(q_bias, z, width, 0)
    b_v = part(v_bias, z, width, 0).reshape(heads, HEAD_DIM)
    b_kv = jnp.stack([jnp.zeros_like(b_v), b_v], axis=1).reshape(2 * width)

    unit1, _ = normalise(x_all.astype(F32))
    normed1 = (unit1 * gain1 + bias1).astype(BF)
    kv = (mm("tm,fm->tf", normed1, w_kv) + b_kv).astype(BF)
    q_t = (mm("fm,tm->ft", w_q, normed1) + b_q[:, None]).astype(BF)

    def head(array, h):
        return array[h * HEAD_DIM : (h + 1) * HEAD_DIM]

    def pair(h):
        return kv[:, h * 128 : (h + 1) * 128]

    keys = [lax.all_gather(pair(0), RING, axis=0, tiled=True)]
    for h in range(1, heads):
        pieces = [pair(h)] + [by_ring(pair(h), ring, d) for d in range(1, ring)]
        keys.append(jnp.concatenate(pieces))
    infos = [info_abs] + [info_far] * (heads - 1)

    own_b = jnp.concatenate(
        [
            part(out_weight.T, c, half_model, 1),
            reduce_half(reduce_weight, c, half_hidden),
        ],
        axis=1,
    )
    own_a = part(expand_weight.T, c, half_hidden, 0)
    own_a, own_b, keys[0] = lax.optimization_barrier((own_a, own_b, keys[0]))
    mine_b = lax.all_gather(own_b, WEIGHT_AXES, axis=0, tiled=True)
    mine_a = lax.all_gather(own_a, WEIGHT_AXES, axis=0, tiled=True)
    both_b = (mine_b, swap(mine_b, "c"))
    expand_t = (mine_a, swap(mine_a, "c"))
    out_t = [b[:, :half_model] for b in both_b]
    reduce_t = [b[:, half_model:] for b in both_b]

    outs, lses = [], []
    for h in range(heads):
        out_h, lse_h = attend(infos[h], head(q_t, h), keys[h])
        outs.append(out_h)
        lses.append(lse_h)
    out_all = jnp.concatenate([o.astype(BF) for o in outs])
    att = lax.all_to_all(
        out_all, ALL, split_axis=1, concat_axis=0, axis_index_groups=groups, tiled=True
    )

    sides = (c, 1 - c)
    atts = [part(att, side, half_model, 0) for side in sides]
    wide = inputs.astype(F32)
    middle = wide + o_bias
    for a, w in zip(atts, out_t):
        middle = middle + mm("ft,mf->tm", a, w)
    unit2, root2 = normalise(middle)
    normed2 = (unit2 * gain2 + bias2).astype(BF)
    total = middle + r_bias
    grad_normed = 0.0
    acts, grads_a, grads_r, grads_e = [], [], [], []
    for side, w_e, w_r in zip(sides, expand_t, reduce_t):
        bias = part(e_bias, side, half_hidden, 1).reshape(-1)
        pre = mm("tm,hm->th", normed2, w_e) + bias
        act, pullback = jax.vjp(smooth_gelu, pre)
        act = act.astype(BF)
        total = total + mm("th,mh->tm", act, w_r)
        grads_r.append(mm("tm,th->mh", cotangent, act).astype(BF))
        grad_pre = pullback(mm("tm,mh->th", cotangent, w_r))[0].astype(BF)
        grads_a.append(mm("th,tm->hm", grad_pre, normed2).astype(BF))
        grads_e.append(jnp.sum(grad_pre.astype(F32), axis=0).reshape(shards, half_hidden))
        grad_normed = grad_normed + mm("th,hm->tm", grad_pre, w_e)
    result = total.astype(BF)
    cot = cotangent.astype(F32)
    grad_reduce_b = jnp.sum(cot, axis=0)
    grad_gain2 = jnp.sum(grad_normed * unit2, axis=0)
    grad_bias2 = jnp.sum(grad_normed, axis=0)
    grad_expand_b = in_order(c, grads_e[0], grads_e[1], 1)
    grad_middle = cot + normalise_back(grad_normed, unit2, root2, gain2)
    grad_branch = grad_middle.astype(BF)
    grad_out_b = jnp.sum(grad_branch.astype(F32), axis=0)
    grad_atts = [mm("mf,tm->ft", w, grad_branch).astype(BF) for w in out_t]
    grad_att = in_order(c, grad_atts[0], grad_atts[1], 0)
    grad_heads = lax.all_to_all(
        grad_att, ALL, split_axis=0, concat_axis=1, axis_index_groups=groups, tiled=True
    )
    grads_o = [mm("tm,ft->mf", grad_branch, a).astype(BF) for a in atts]

    sum_a = (grads_a[0].astype(F32) + swap(grads_a[1], "c").astype(F32)).astype(BF)
    sum_r = (grads_r[0].astype(F32) + swap(grads_r[1], "c").astype(F32)).astype(BF)
    sum_o = (grads_o[0].astype(F32) + swap(grads_o[1], "c").astype(F32)).astype(BF)
    sum_b = jnp.concatenate([sum_o, sum_r], axis=1)
    sum_a = lax.psum_scatter(sum_a, WEIGHT_AXES, scatter_dimension=0, tiled=True)
    sum_b = lax.psum_scatter(sum_b, WEIGHT_AXES, scatter_dimension=0, tiled=True)

    dqs, dkvs = [None] * heads, [None] * heads
    for h in list(range(1, heads)) + [0]:
        dq_h, dkv_h = attend_back(
            infos[h], head(q_t, h), head(grad_heads, h), outs[h], lses[h], keys[h]
        )
        dqs[h] = dq_h
        if h == 0:
            dkv_h, sum_a, sum_b = lax.optimization_barrier((dkv_h, sum_a, sum_b))
            dkvs[h] = lax.psum_scatter(dkv_h, RING, scatter_dimension=0, tiled=True)
        else:
            pieces = dkv_h.reshape(ring, depth * tokens, 128)
            added = pieces[0].astype(F32)
            for d in range(1, ring):
                added = added + by_ring(pieces[d], ring, d).astype(F32)
            dkvs[h] = added.astype(BF)

    sum_a = swap_sum(sum_a, "y").astype(BF)
    sum_b = swap_sum(sum_b, "y").astype(BF)
    full_a = in_order(c, sum_a, swap(sum_a, "c"), 0)
    other_b = swap(sum_b, "c")
    full_o = in_order(c, sum_b[:, :half_model], other_b[:, :half_model], 1)
    full_r = in_order(
        c,
        sum_b[:, half_model:].reshape(here, shards, 1, half_hidden),
        other_b[:, half_model:].reshape(here, shards, 1, half_hidden),
        2,
    ).reshape(here, shards * hidden_here)
    grad_expand_w = full_a.T.astype(F32)
    grad_out_w = full_o.T.astype(F32)
    grad_reduce_w = full_r.T.astype(F32)

    dq = jnp.concatenate(dqs)
    dkv = jnp.concatenate(dkvs, axis=1)
    grad_w_q = mm("ft,tm->fm", dq, normed1)
    grad_w_kv = mm("tf,tm->fm", dkv, normed1).reshape(heads, 2, HEAD_DIM, model)
    grad_w = jnp.concatenate([grad_w_q, grad_w_kv.transpose(1, 0, 2, 3).reshape(2 * width, model)])
    grad_q_b = jnp.sum(dq.astype(F32), axis=1)
    grad_v_b = jnp.sum(dkv.astype(F32), axis=0).reshape(heads, 2, HEAD_DIM)[:, 1].reshape(width)
    part_norm = mm("ft,fm->tm", dq, w_q) + mm("tf,fm->tm", dkv, w_kv)
    grad_gain1 = jnp.sum(part_norm * unit1, axis=0)
    grad_bias1 = jnp.sum(part_norm, axis=0)
    grad_normed1 = lax.psum_scatter(
        part_norm.astype(BF), ALL, scatter_dimension=0, axis_index_groups=groups, tiled=True
    ).astype(F32)
    unit_in, root_in = normalise(wide)
    grad_in = (grad_middle + normalise_back(grad_normed1, unit_in, root_in, gain1)).astype(BF)

    placed_q = lax.dynamic_update_slice(jnp.zeros((model,), F32), grad_q_b, (z * width,))
    placed_v = lax.dynamic_update_slice(jnp.zeros((model,), F32), grad_v_b, (z * width,))
    small_grads = jnp.concatenate(
        [
            v.reshape(shards, -1)
            for v in (
                grad_gain1,
                grad_bias1,
                placed_q,
                placed_v,
                grad_out_b,
                grad_gain2,
                grad_bias2,
                grad_reduce_b,
                grad_expand_b,
            )
        ],
        axis=1,
    )
    grad_triple_w, flat = (send_triple if special else send_triple_whole)(grad_w, small_grads, at)
    vecs = [flat[i * here : (i + 1) * here] for i in range(8)]
    grad_e_b = flat[8 * here : 8 * here + hidden_here]
    return (
        result,
        grad_in,
        vecs[0],
        vecs[1],
        grad_triple_w,
        vecs[2],
        vecs[3],
        grad_out_w,
        vecs[4],
        vecs[5],
        vecs[6],
        grad_expand_w,
        grad_e_b,
        grad_reduce_w,
        vecs[7],
    )


def reduce_half(weight, c, half):
    pieces = weight.reshape(-1, 2, half, weight.shape[1])
    return part(pieces, c, 1, 1).reshape(-1, weight.shape[1]).T


def solution(mesh):
    fsdp, seq = mesh.shape["fsdp"], mesh.shape["seq"]
    wide = Mesh(
        mesh.devices.reshape(fsdp // GROUP, GROUP // 2, 2, seq // 2, 2), ("g", "z", "x", "y", "c")
    )
    rows = P(ALL, None)
    vector = P(WEIGHT_AXES)
    matrix = P(None, WEIGHT_AXES)
    return jax.shard_map(
        on_device,
        mesh=wide,
        in_specs=(
            rows,
            rows,
            vector,
            vector,
            matrix,
            vector,
            vector,
            matrix,
            vector,
            vector,
            vector,
            matrix,
            vector,
            matrix,
            vector,
        ),
        out_specs=(
            rows,
            rows,
            vector,
            vector,
            matrix,
            vector,
            vector,
            matrix,
            vector,
            vector,
            vector,
            matrix,
            vector,
            matrix,
            vector,
        ),
        check_vma=False,
    )
```

time: 1260 us -> 839 us (0.67)
  waiting for transfers between devices: 741 us -> 308 us
  local copies, waits for them, and re-layouts: 119 us -> 67.9 us
  Pallas kernels: 237 us -> 280 us
  starting transfers between devices: 15.7 us -> 52.6 us
  other arithmetic: 53.6 us -> 35.3 us
    reduce_scatter x7 -> x3, waiting for transfers between devices: 385 us -> 20.4 us  [the longest x1 20.3 us: on_device(): lax.psum_scatter(sum_a, WEIGHT_AXES, scatter_dimension=0, tiled=True)]
    all_gather x8 -> x4, waiting for transfers between devices: 306 us -> 13.9 us  [the longest x1 13.9 us: on_device(): mine_a = lax.all_gather(own_a, WEIGHT_AXES, axis=0, tiled=True)]
    ppermute x0 -> x28, waiting for transfers between devices: none -> 121 us  [by_ring(): return lax.ppermute(array, ALL, pairs)]
    ppermute x6 -> x15, waiting for transfers between devices: 21 us -> 111 us  [swap(): return lax.ppermute(array, axis, [(0, 1), (1, 0)])]
    concatenate x19 -> x2, local copies, waits for them, and re-layouts: 49.9 us -> 0.9 us  [on_device(): keys.append(jnp.concatenate(pieces))]
    pallas_call x6, Pallas kernels: 237 us -> 280 us  [the longest x3 170 us: attend_back(): pl.pallas_call(functools.partial(backward_kernel, strips, unroll), grid=(...]
    ppermute x0 -> x28, starting transfers between devices: none -> 24.6 us  [by_ring(): return lax.ppermute(array, ALL, pairs)]
    all_to_all x2 -> x4, waiting for transfers between devices: 24.9 us -> 40.7 us  [the longest x1 18.1 us: fetch_triple(): got = lax.all_to_all(slots, 'z', split_axis=0, concat_axis=0, tiled=True)]
  transfers between devices with their start and end apart: 23 -> 55, of which waited for: 19 -> 23; matrix products, arithmetic and copies ran while one was open for 14% -> 17% of each run, Pallas kernels for 15% -> 34%
where the time goes in v2:
time: 839 us; the launch traced here: 833 us
  waiting for transfers between devices  308 us (37%)
  Pallas kernels  280 us (33%)
  matrix products  73.6 us (9%)
  local copies, waits for them, and re-layouts  67.9 us (8%)
  starting transfers between devices  52.6 us (6%)
  other arithmetic  35.3 us (4%)
  between operations  15.7 us (2%)
    pallas_call x3, Pallas kernels, attend_back(): pl.pallas_call(functools.partial(backward_kernel, strips, unroll), grid=(...  170 us
    ppermute x28, waiting for transfers between devices, by_ring(): return lax.ppermute(array, ALL, pairs)  121 us
    ppermute x15, waiting for transfers between devices, swap(): return lax.ppermute(array, axis, [(0, 1), (1, 0)])  111 us
    pallas_call x3, Pallas kernels, attend(): pl.pallas_call(functools.partial(forward_kernel, strips, unroll), grid=(s...  110 us
    dot_general x24, matrix products, mm(): return jnp.einsum(spec, a, b, preferred_element_type=F32)  73.6 us
    ppermute x28, starting transfers between devices, by_ring(): return lax.ppermute(array, ALL, pairs)  24.6 us
    unnamed x123, local copies, waits for them, and re-layouts  20.5 us
    reduce_scatter x1, waiting for transfers between devices, on_device(): lax.psum_scatter(sum_a, WEIGHT_AXES, scatter_dimension=0, tiled=True)  20.3 us
  transfers between devices with their start and end apart: 55, of which 23 were waited for; matrix products, arithmetic and copies ran while one was open for 17% of the time, Pallas kernels for 34%

profile of v2, /device:TPU:0, one launch (start us, length us, event | category | flops | bytes accessed | tf_op | source)
XLA Modules:
  0.0 832.5 jit_solution(8743821610361069109)
XLA Ops:
  7.9 6.1 concatenate.112
  15.1 3.0 collective-permute-start
  18.1 49.2 %collective-permute-done = bf16[304,384]{1,0:T(8,128)(2,1)S(1)} collective-permute-done((bf16[304,384]{1,0:T(8,128)(2,1)S(1)}, bf16[304,384]{1,0:T(8,128)(2,1)S(1)}, u32[]{:S(2)}, u32[]{:S(2)}) %collective-permute-start) | collective-permute-done | bytes 233504 | tf_op jit(solution)/shard_map/ppermute | solution.py:317
  68.9 5.8 all-to-all-start
  74.7 18.1 %all-to-all-done = bf16[4,208,384]{2,1,0:T(8,128)(2,1)S(1)} async-done(((bf16[4,208,384]{2,1,0:T(8,128)(2,1)}), bf16[4,208,384]{2,1,0:T(8,128)(2,1)S(1)}, u32[]{:S(2)}, u32[]{:S(2)}) %all-to-all-start) | async-done | bytes 639008 | tf_op jit(solution)/shard_map/all_to_all | solution.py:368
  95.2 2.8 convert_reduce_fusion
  100.9 1.8 add_convert_fusion.1
  106.5 2.5 dynamic-slice_reduce_fusion
  115.8 3.1 fusion.22
  121.5 9.7 %collective-permute-done.10 = bf16[2048,128]{1,0:T(8,128)(2,1)S(1)} collective-permute-done((bf16[2048,128]{1,0:T(8,128)(2,1)S(1)}, bf16[2048,128]{1,0:T(8,128)(2,1)S(1)}, u32[]{:S(2)}, u32[]{:S(2)}) %collective-permute-start.10) | collective-permute-done | bytes 524320 | tf_op jit(solution)/shard_map/ppermute | solution.py:351
  132.0 18.9 %collective-permute-done.11 = bf16[2048,128]{1,0:T(8,128)(2,1)S(1)} collective-permute-done((bf16[2048,128]{1,0:T(8,128)(2,1)S(1)}, bf16[2048,128]{1,0:T(8,128)(2,1)S(1)}, u32[]{:S(2)}, u32[]{:S(2)}) %collective-permute-start.11) | collective-permute-done | bytes 524320 | tf_op jit(solution)/shard_map/ppermute | solution.py:351
  153.7 11.9 %collective-permute-done.14 = bf16[2048,128]{1,0:T(8,128)(2,1)S(1)} collective-permute-done((bf16[2048,128]{1,0:T(8,128)(2,1)S(1)}, bf16[2048,128]{1,0:T(8,128)(2,1)S(1)}, u32[]{:S(2)}, u32[]{:S(2)}) %collective-permute-start.14) | collective-permute-done | bytes 524320 | tf_op jit(solution)/shard_map/ppermute | solution.py:351
  166.3 10.2 %collective-permute-done.15 = bf16[2048,128]{1,0:T(8,128)(2,1)S(1)} collective-permute-done((bf16[2048,128]{1,0:T(8,128)(2,1)S(1)}, bf16[2048,128]{1,0:T(8,128)(2,1)S(1)}, u32[]{:S(2)}, u32[]{:S(2)}) %collective-permute-start.15) | collective-permute-done | bytes 524320 | tf_op jit(solution)/shard_map/ppermute | solution.py:351
  176.9 2.0 copy-done.35
  178.9 36.7 %shard_map.264 = (f32[64,2048]{1,0:T(8,128)}, f32[8,2048]{1,0:T(8,128)}) custom-call(s32[3]{0:T(128)} %pad_add_fusion.2.r_ref, bf16[64,2048]{1,0:T(8,128)(2,1)} %get-tuple-element.149.q_ref, bf16[16384,128]{1,0:T(8,128)(2,1)} %copy-done.35), custom_call_target="tpu_custom_call" | custom-call | flops 40000000000 | bytes 8388608 | tf_op jit(solution)/shard_map/pallas_call | solution.py:139
  222.9 10.3 %collective-permute-done.7 = bf16[2048,128]{1,0:T(8,128)(2,1)S(1)} collective-permute-done((bf16[2048,128]{1,0:T(8,128)(2,1)}, bf16[2048,128]{1,0:T(8,128)(2,1)S(1)}, u32[]{:S(2)}, u32[]{:S(2)}) %collective-permute-start.7) | collective-permute-done | bytes 524320 | tf_op jit(solution)/shard_map/ppermute | solution.py:351
  234.1 11.4 %collective-permute-done.8 = bf16[2048,128]{1,0:T(8,128)(2,1)S(1)} collective-permute-done((bf16[2048,128]{1,0:T(8,128)(2,1)}, bf16[2048,128]{1,0:T(8,128)(2,1)S(1)}, u32[]{:S(2)}, u32[]{:S(2)}) %collective-permute-start.8) | collective-permute-done | bytes 524320 | tf_op jit(solution)/shard_map/ppermute | solution.py:351
  246.3 36.7 %shard_map.263 = (f32[64,2048]{1,0:T(8,128)}, f32[8,2048]{1,0:T(8,128)}) custom-call(s32[3]{0:T(128)} %pad_add_fusion.2.r_ref, bf16[64,2048]{1,0:T(8,128)(2,1)} %get-tuple-element.150.q_ref, bf16[16384,128]{1,0:T(8,128)(2,1)} %constant_dynamic-update-slice_fusion.kv_ref), custom_call_target="tpu_custom_call" | custom-call | flops 40000000000 | bytes 8388608 | tf_op jit(solution)/shard_map/pallas_call | solution.py:139
  284.8 36.7 %shard_map.262 = (f32[64,2048]{1,0:T(8,128)}, f32[8,2048]{1,0:T(8,128)}) custom-call(s32[3]{0:T(128)} %pad_add_fusion.r_ref, bf16[64,2048]{1,0:T(8,128)(2,1)} %get-tuple-element.148.q_ref, bf16[16384,128]{1,0:T(8,128)(2,1)} %all-gather.7.cloned.1.call-done.kv_ref), custom_call_target="tpu_custom_call" | custom-call | flops 40000000000 | bytes 8388608 | tf_op jit(solution)/shard_map/pallas_call | solution.py:139
  323.6 5.5 all-to-all-start.1
  329.1 13.9 %all-gather.11.cloned.1.call-done = bf16[1536,768]{1,0:T(8,128)(2,1)} async-done(((bf16[192,768]{1,0:T(8,128)(2,1)}), bf16[1536,768]{1,0:T(8,128)(2,1)}) %all-gather.11.cloned.1.call-update) | async-done | bytes 2359312 | tf_op jit(solution)/shard_map/all_gather | solution.py:534
  343.4 9.8 %all-to-all-done.1 = bf16[192,4,512]{2,0,1:T(8,128)(2,1)S(1)} async-done(((bf16[192,4,512]{2,0,1:T(8,128)(2,1)}), bf16[192,4,512]{2,0,1:T(8,128)(2,1)S(1)}, u32[]{:S(2)}, u32[]{:S(2)}) %all-to-all-start.1) | async-done | bytes 786464 | tf_op jit(solution)/shard_map/all_to_all | solution.py:546
  353.2 1.7 fusion.55
  354.9 1.8 fusion.92
  357.4 3.4 convolution_add_fusion.1
  360.8 3.2 fusion.21
  364.0 5.4 convert_reduce_fusion.1
  371.8 4.1 convert_reduce_fusion.2
  377.3 4.1 multiply_reduce_fusion
  381.5 1.8 fusion.86
  386.5 4.2 all-to-all-start.2
  392.6 4.4 convolution_convert_fusion.2
  402.4 9.8 %all-to-all-done.2 = bf16[4,192,512]{2,1,0:T(8,128)(2,1)} async-done(((bf16[4,192,512]{2,1,0:T(8,128)(2,1)}), bf16[4,192,512]{2,1,0:T(8,128)(2,1)}, u32[]{:S(2)}, u32[]{:S(2)}) %all-to-all-start.2) | async-done | bytes 786464 | tf_op jit(solution)/shard_map/all_to_all | solution.py:583
  412.2 1.9 slice_bitcast_fusion.2
  414.9 4.5 fusion.8
  419.6 3.9 copy.66
  423.5 56.7 %shard_map.267 = (bf16[64,2048]{1,0:T(8,128)(2,1)}, bf16[16384,128]{1,0:T(8,128)(2,1)}) custom-call(s32[3]{0:T(128)} %pad_add_fusion.2.r_ref, bf16[64,2048]{1,0:T(8,128)(2,1)} %get-tuple-element.149.q_ref, bf16[64,2048]{1,0:T(8,128)(2,1)} %bitcast.137, f32[64,2048]{1,0:T(8,128)} %get-tuple-element.36.out_ref, f32[8,2048]{1,0:T(8,128)} %get-tuple-element.43.lse_ref, ...), custom_call_target="tpu_custom_call" | custom-call | flops 99999997952 | bytes 12582912 | tf_op jit(solution)/shard_map/pallas_call | solution.py:257
  480.2 4.0 fusion.88
  490.7 4.5 add_convert_fusion
  495.3 56.5 %shard_map.265 = (bf16[64,2048]{1,0:T(8,128)(2,1)}, bf16[16384,128]{1,0:T(8,128)(2,1)}) custom-call(s32[3]{0:T(128)} %pad_add_fusion.r_ref, bf16[64,2048]{1,0:T(8,128)(2,1)} %get-tuple-element.148.q_ref, bf16[64,2048]{1,0:T(8,128)(2,1)} %bitcast.136, f32[64,2048]{1,0:T(8,128)} %get-tuple-element.34.out_ref, f32[8,2048]{1,0:T(8,128)} %get-tuple-element.39.lse_ref, ...), custom_call_target="tpu_custom_call" | custom-call | flops 99999997952 | bytes 12582912 | tf_op jit(solution)/shard_map/pallas_call | solution.py:257
  553.1 20.3 %reduce-scatter.7.cloned.1.call-done = bf16[192,768]{1,0:T(8,128)(2,1)} async-done(((bf16[1536,768]{1,0:T(8,128)(2,1)}), bf16[192,768]{1,0:T(8,128)(2,1)}) %reduce-scatter.7.cloned.1.call-update) | async-done | bytes 294928 | tf_op jit(solution)/shard_map/reduce_scatter | solution.py:592
  573.5 56.7 %shard_map.266 = (bf16[64,2048]{1,0:T(8,128)(2,1)}, bf16[16384,128]{1,0:T(8,128)(2,1)}) custom-call(s32[3]{0:T(128)} %pad_add_fusion.2.r_ref, bf16[64,2048]{1,0:T(8,128)(2,1)} %get-tuple-element.150.q_ref, bf16[64,2048]{1,0:T(8,128)(2,1)} %bitcast.135, f32[64,2048]{1,0:T(8,128)} %get-tuple-element.35.out_ref, f32[8,2048]{1,0:T(8,128)} %get-tuple-element.41.lse_ref, ...), custom_call_target="tpu_custom_call" | custom-call | flops 99999997952 | bytes 12582912 | tf_op jit(solution)/shard_map/pallas_call | solution.py:257
  631.2 3.8 fusion.87
  637.4 2.2 collective-permute-start.26
  640.1 2.7 convolution_convert_fusion.9
  642.9 27.4 %collective-permute-done.29 = bf16[2048,128]{1,0:T(8,128)(2,1)} collective-permute-done((bf16[2048,128]{1,0:T(8,128)(2,1)S(1)}, bf16[2048,128]{1,0:T(8,128)(2,1)}, u32[]{:S(2)}, u32[]{:S(2)}) %collective-permute-start.29) | collective-permute-done | bytes 524320 | tf_op jit(solution)/shard_map/ppermute | solution.py:351
  673.1 2.7 add_convert_fusion.5
  675.9 9.0 %collective-permute-done.24 = bf16[2048,128]{1,0:T(8,128)(2,1)S(1)} collective-permute-done((bf16[2048,128]{1,0:T(8,128)(2,1)}, bf16[2048,128]{1,0:T(8,128)(2,1)S(1)}, u32[]{:S(2)}, u32[]{:S(2)}) %collective-permute-start.24) | collective-permute-done | bytes 524320 | tf_op jit(solution)/shard_map/ppermute | solution.py:351
  685.7 11.3 %collective-permute-done.22 = bf16[2048,128]{1,0:T(8,128)(2,1)S(1)} collective-permute-done((bf16[2048,128]{1,0:T(8,128)(2,1)}, bf16[2048,128]{1,0:T(8,128)(2,1)S(1)}, u32[]{:S(2)}, u32[]{:S(2)}) %collective-permute-start.22) | collective-permute-done | bytes 524320 | tf_op jit(solution)/shard_map/ppermute | solution.py:351
  697.0 1.9 add_convert_fusion.6
  698.9 3.0 fusion.84
  701.9 4.4 fusion.85
  707.4 4.1 convolution_convert_fusion.4
  717.0 5.8 fusion.27
  724.0 46.8 %collective-permute-done.41 = bf16[192,768]{1,0:T(8,128)(2,1)S(1)} collective-permute-done((bf16[192,768]{1,0:T(8,128)(2,1)}, bf16[192,768]{1,0:T(8,128)(2,1)S(1)}, u32[]{:S(2)}, u32[]{:S(2)}) %collective-permute-start.41) | collective-permute-done | bytes 294944 | tf_op jit(solution)/shard_map/ppermute | solution.py:317
  771.7 9.2 %collective-permute-done.36 = bf16[608,384]{1,0:T(8,128)(2,1)S(1)} collective-permute-done((bf16[608,384]{1,0:T(8,128)(2,1)S(1)}, bf16[608,384]{1,0:T(8,128)(2,1)S(1)}, u32[]{:S(2)}, u32[]{:S(2)}) %collective-permute-start.36) | collective-permute-done | bytes 466976 | tf_op jit(solution)/shard_map/ppermute | solution.py:317
  783.6 4.2 all-to-all-start.3
  787.8 3.7 collective-permute-done.39
  792.8 5.9 add_convert_fusion.2
  802.4 2.9 all-to-all-done.3
  811.5 2.4 copy.62
  813.9 3.6 reshape.322
  821.1 1.7 fusion.41
  822.8 2.6 fusion.37
  (350 shorter events, 96.5 us)
Async XLA Ops:
  7.2 97.3 %copy-start = (bf16[768,384]{1,0:T(8,128)(2,1)S(1)}, bf16[768,384]{1,0:T(8,128)(2,1)}, u32[]{:S(2)}) copy-start(bf16[768,384]{1,0:T(8,128)(2,1)} %param.26) | copy-start | bytes 1769476
  7.2 88.0 %all-gather.5.cloned.1.call-start = ((), (), s32[]{:S(2)}) async-start(), calls=%async_computation.8 | async-start | bytes 3932160 | tf_op jit(solution)/shard_map/all_gather | solution.py:492
  15.1 52.2 %collective-permute-start = (bf16[304,384]{1,0:T(8,128)(2,1)S(1)}, bf16[304,384]{1,0:T(8,128)(2,1)S(1)}, u32[]{:S(2)}, u32[]{:S(2)}) collective-permute-start(bf16[304,384]{1,0:T(8,128)(2,1)S(1)} %get-tuple-element.160), channel_id=1, source_target_pairs={{0,4},{4,0},{1,5},{5,1},{2,6},{6,2},{3,7},{7,3},{8,12},{12,8},{9,1... | collective-permute-start | bytes 700424 | tf_op jit(solution)/shard_map/ppermute | solution.py:317
  68.9 24.0 %all-to-all-start = ((bf16[4,208,384]{2,1,0:T(8,128)(2,1)}), bf16[4,208,384]{2,1,0:T(8,128)(2,1)S(1)}, u32[]{:S(2)}, u32[]{:S(2)}) async-start(bf16[4,208,384]{2,1,0:T(8,128)(2,1)} %pad_maximum_fusion.3), calls=%async_computation | async-start | bytes 1277952 | tf_op jit(solution)/shard_map/all_to_all | solution.py:368
  74.7 143.1 %all-gather.7.cloned.1.call-start = ((), (), s32[]{:S(2)}) async-start(), calls=%async_computation.9 | async-start | bytes 4718592 | tf_op jit(solution)/shard_map/all_gather | solution.py:518
  93.0 1.9 collective-permute-start.1
  95.0 20.8 %copy-start.10 = (bf16[576,768]{1,0:T(8,128)(2,1)}, bf16[576,768]{1,0:T(8,128)(2,1)S(1)}, u32[]{:S(2)}) copy-start(bf16[576,768]{1,0:T(8,128)(2,1)S(1)} %maximum_select_fusion) | copy-start | bytes 2654212
  104.3 179.9 %all-gather.9.cloned.1.call-start = ((), (), s32[]{:S(2)}) async-start(), calls=%async_computation.10 | async-start | bytes 3317760 | tf_op jit(solution)/shard_map/all_gather | solution.py:533
  112.2 7.7 collective-permute-start.9
  112.3 18.9 %collective-permute-start.10 = (bf16[2048,128]{1,0:T(8,128)(2,1)S(1)}, bf16[2048,128]{1,0:T(8,128)(2,1)S(1)}, u32[]{:S(2)}, u32[]{:S(2)}) collective-permute-start(bf16[2048,128]{1,0:T(8,128)(2,1)S(1)} %get-tuple-element.140), channel_id=1, source_target_pairs={{0,2},{1,3},{2,0},{3,1},{4,6},{5,7},{6,4},{7,5},{8,10},{9,11},{10,... | collective-permute-start | bytes 1572872 | tf_op jit(solution)/shard_map/ppermute | solution.py:351
  113.2 37.7 %collective-permute-start.11 = (bf16[2048,128]{1,0:T(8,128)(2,1)S(1)}, bf16[2048,128]{1,0:T(8,128)(2,1)S(1)}, u32[]{:S(2)}, u32[]{:S(2)}) collective-permute-start(bf16[2048,128]{1,0:T(8,128)(2,1)S(1)} %get-tuple-element.140), channel_id=1, source_target_pairs={{0,3},{1,2},{2,1},{3,0},{4,7},{5,6},{6,5},{7,4},{8,11},{9,10},{10,... | collective-permute-start | bytes 1572872 | tf_op jit(solution)/shard_map/ppermute | solution.py:351
  114.1 38.0 %collective-permute-start.12 = (bf16[2048,128]{1,0:T(8,128)(2,1)S(1)}, bf16[2048,128]{1,0:T(8,128)(2,1)S(1)}, u32[]{:S(2)}, u32[]{:S(2)}) collective-permute-start(bf16[2048,128]{1,0:T(8,128)(2,1)S(1)} %get-tuple-element.140), channel_id=1, source_target_pairs={{0,4},{1,5},{2,6},{3,7},{4,0},{5,1},{6,2},{7,3},{8,12},{9,13},{10,... | collective-permute-start | bytes 1572872 | tf_op jit(solution)/shard_map/ppermute | solution.py:351
  114.7 37.8 %collective-permute-start.13 = (bf16[2048,128]{1,0:T(8,128)(2,1)S(1)}, bf16[2048,128]{1,0:T(8,128)(2,1)S(1)}, u32[]{:S(2)}, u32[]{:S(2)}) collective-permute-start(bf16[2048,128]{1,0:T(8,128)(2,1)S(1)} %get-tuple-element.140), channel_id=1, source_target_pairs={{0,5},{1,4},{2,7},{3,6},{4,1},{5,0},{6,3},{7,2},{8,13},{9,12},{10,... | collective-permute-start | bytes 1572872 | tf_op jit(solution)/shard_map/ppermute | solution.py:351
  119.9 45.7 %collective-permute-start.14 = (bf16[2048,128]{1,0:T(8,128)(2,1)S(1)}, bf16[2048,128]{1,0:T(8,128)(2,1)S(1)}, u32[]{:S(2)}, u32[]{:S(2)}) collective-permute-start(bf16[2048,128]{1,0:T(8,128)(2,1)S(1)} %get-tuple-element.140), channel_id=1, source_target_pairs={{0,6},{1,7},{2,4},{3,5},{4,2},{5,3},{6,0},{7,1},{8,14},{9,15},{10,... | collective-permute-start | bytes 1572872 | tf_op jit(solution)/shard_map/ppermute | solution.py:351
  131.3 45.2 %collective-permute-start.15 = (bf16[2048,128]{1,0:T(8,128)(2,1)S(1)}, bf16[2048,128]{1,0:T(8,128)(2,1)S(1)}, u32[]{:S(2)}, u32[]{:S(2)}) collective-permute-start(bf16[2048,128]{1,0:T(8,128)(2,1)S(1)} %get-tuple-element.140), channel_id=1, source_target_pairs={{0,7},{1,6},{2,5},{3,4},{4,3},{5,2},{6,1},{7,0},{8,15},{9,14},{10,... | collective-permute-start | bytes 1572872 | tf_op jit(solution)/shard_map/ppermute | solution.py:351
  151.0 64.7 %collective-permute-start.2 = (bf16[2048,128]{1,0:T(8,128)(2,1)}, bf16[2048,128]{1,0:T(8,128)(2,1)S(1)}, u32[]{:S(2)}, u32[]{:S(2)}) collective-permute-start(bf16[2048,128]{1,0:T(8,128)(2,1)} %get-tuple-element.137), channel_id=1, source_target_pairs={{0,1},{1,0},{2,3},{3,2},{4,5},{5,4},{6,7},{7,6},{8,9},{9,8},{10,11... | collective-permute-start | bytes 1572872 | tf_op jit(solution)/shard_map/ppermute | solution.py:351
  152.0 66.1 %collective-permute-start.3 = (bf16[2048,128]{1,0:T(8,128)(2,1)}, bf16[2048,128]{1,0:T(8,128)(2,1)S(1)}, u32[]{:S(2)}, u32[]{:S(2)}) collective-permute-start(bf16[2048,128]{1,0:T(8,128)(2,1)} %get-tuple-element.137), channel_id=1, source_target_pairs={{0,2},{1,3},{2,0},{3,1},{4,6},{5,7},{6,4},{7,5},{8,10},{9,11},{10,... | collective-permute-start | bytes 1572872 | tf_op jit(solution)/shard_map/ppermute | solution.py:351
  152.4 67.9 %collective-permute-start.4 = (bf16[2048,128]{1,0:T(8,128)(2,1)}, bf16[2048,128]{1,0:T(8,128)(2,1)S(1)}, u32[]{:S(2)}, u32[]{:S(2)}) collective-permute-start(bf16[2048,128]{1,0:T(8,128)(2,1)} %get-tuple-element.137), channel_id=1, source_target_pairs={{0,3},{1,2},{2,1},{3,0},{4,7},{5,6},{6,5},{7,4},{8,11},{9,10},{10,... | collective-permute-start | bytes 1572872 | tf_op jit(solution)/shard_map/ppermute | solution.py:351
  165.6 55.5 %collective-permute-start.5 = (bf16[2048,128]{1,0:T(8,128)(2,1)}, bf16[2048,128]{1,0:T(8,128)(2,1)S(1)}, u32[]{:S(2)}, u32[]{:S(2)}) collective-permute-start(bf16[2048,128]{1,0:T(8,128)(2,1)} %get-tuple-element.137), channel_id=1, source_target_pairs={{0,4},{1,5},{2,6},{3,7},{4,0},{5,1},{6,2},{7,3},{8,12},{9,13},{10,... | collective-permute-start | bytes 1572872 | tf_op jit(solution)/shard_map/ppermute | solution.py:351
  176.5 45.6 %collective-permute-start.6 = (bf16[2048,128]{1,0:T(8,128)(2,1)}, bf16[2048,128]{1,0:T(8,128)(2,1)S(1)}, u32[]{:S(2)}, u32[]{:S(2)}) collective-permute-start(bf16[2048,128]{1,0:T(8,128)(2,1)} %get-tuple-element.137), channel_id=1, source_target_pairs={{0,5},{1,4},{2,7},{3,6},{4,1},{5,0},{6,3},{7,2},{8,13},{9,12},{10,... | collective-permute-start | bytes 1572872 | tf_op jit(solution)/shard_map/ppermute | solution.py:351
  215.6 17.7 %collective-permute-start.7 = (bf16[2048,128]{1,0:T(8,128)(2,1)}, bf16[2048,128]{1,0:T(8,128)(2,1)S(1)}, u32[]{:S(2)}, u32[]{:S(2)}) collective-permute-start(bf16[2048,128]{1,0:T(8,128)(2,1)} %get-tuple-element.137), channel_id=1, source_target_pairs={{0,6},{1,7},{2,4},{3,5},{4,2},{5,3},{6,0},{7,1},{8,14},{9,15},{10,... | collective-permute-start | bytes 1572872 | tf_op jit(solution)/shard_map/ppermute | solution.py:351
  217.8 125.1 %all-gather.11.cloned.1.call-start = ((), (), s32[]{:S(2)}) async-start(), calls=%async_computation.11 | async-start | bytes 2654208 | tf_op jit(solution)/shard_map/all_gather | solution.py:534
  218.1 27.4 %collective-permute-start.8 = (bf16[2048,128]{1,0:T(8,128)(2,1)}, bf16[2048,128]{1,0:T(8,128)(2,1)S(1)}, u32[]{:S(2)}, u32[]{:S(2)}) collective-permute-start(bf16[2048,128]{1,0:T(8,128)(2,1)} %get-tuple-element.137), channel_id=1, source_target_pairs={{0,7},{1,6},{2,5},{3,4},{4,3},{5,2},{6,1},{7,0},{8,15},{9,14},{10,... | collective-permute-start | bytes 1572872 | tf_op jit(solution)/shard_map/ppermute | solution.py:351
  284.2 70.7 %collective-permute-start.16 = (bf16[768,1920]{1,0:T(8,128)(2,1)}, bf16[768,1920]{1,0:T(8,128)(2,1)}, u32[]{:S(2)}, u32[]{:S(2)}) collective-permute-start(bf16[768,1920]{1,0:T(8,128)(2,1)} %all-gather.9.cloned.1.call-done), channel_id=1, source_target_pairs={{0,1},{1,0},{2,3},{3,2},{4,5},{5,4},{6,7},{7,6},{8,9},{9,8},{10,11... | collective-permute-start | bytes 8847368 | tf_op jit(solution)/shard_map/ppermute | solution.py:317
  322.6 32.3 %copy-start.4 = (bf16[512,768]{1,0:T(8,128)(2,1)S(1)}, bf16[512,768]{1,0:T(8,128)(2,1)}, u32[]{:S(2)}) copy-start(bf16[512,768]{1,0:T(8,128)(2,1)} %param.15) | copy-start | bytes 2359300
  323.6 29.7 %all-to-all-start.1 = ((bf16[192,4,512]{2,0,1:T(8,128)(2,1)}), bf16[192,4,512]{2,0,1:T(8,128)(2,1)S(1)}, u32[]{:S(2)}, u32[]{:S(2)}) async-start(bf16[192,4,512]{2,0,1:T(8,128)(2,1)} %bitcast.117), calls=%async_computation.1 | async-start | bytes 1572864 | tf_op jit(solution)/shard_map/all_to_all | solution.py:546
  342.9 14.5 %collective-permute-start.17 = (bf16[1536,768]{1,0:T(8,128)(2,1)}, bf16[1536,768]{1,0:T(8,128)(2,1)}, u32[]{:S(2)}, u32[]{:S(2)}) collective-permute-start(bf16[1536,768]{1,0:T(8,128)(2,1)} %all-gather.11.cloned.1.call-done), channel_id=1, source_target_pairs={{0,1},{1,0},{2,3},{3,2},{4,5},{5,4},{6,7},{7,6},{8,9},{9,8},{10,11... | collective-permute-start | bytes 7077896 | tf_op jit(solution)/shard_map/ppermute | solution.py:317
  356.7 24.7 %copy-start.6 = (f32[512,768]{1,0:T(8,128)}, f32[512,768]{1,0:T(8,128)S(1)}, u32[]{:S(2)}) copy-start(f32[512,768]{1,0:T(8,128)S(1)} %get-tuple-element.182) | copy-start | bytes 4718596
  364.0 50.9 %collective-permute-start.20 = (bf16[768,1536]{0,1:T(8,128)(2,1)}, bf16[768,1536]{0,1:T(8,128)(2,1)}, u32[]{:S(2)}, u32[]{:S(2)}) collective-permute-start(bf16[768,1536]{0,1:T(8,128)(2,1)} %fusion.21), channel_id=1, source_target_pairs={{0,1},{1,0},{2,3},{3,2},{4,5},{5,4},{6,7},{7,6},{8,9},{9,8},{10,11... | collective-permute-start | bytes 7077896 | tf_op jit(solution)/shard_map/ppermute | solution.py:317
  386.5 25.7 %all-to-all-start.2 = ((bf16[4,192,512]{2,1,0:T(8,128)(2,1)}), bf16[4,192,512]{2,1,0:T(8,128)(2,1)}, u32[]{:S(2)}, u32[]{:S(2)}) async-start(bf16[4,192,512]{2,1,0:T(8,128)(2,1)} %bitcast.122), calls=%async_computation.2 | async-start | bytes 1572864 | tf_op jit(solution)/shard_map/all_to_all | solution.py:583
  390.7 161.1 %reduce-scatter.13.cloned.1.call-start = ((), (), s32[]{:S(2)}) async-start(), calls=%async_computation.15 | async-start | bytes 3317760
  391.3 10.6 %collective-permute-start.19 = (bf16[768,384]{0,1:T(8,128)(2,1)S(1)}, bf16[768,384]{0,1:T(8,128)(2,1)S(1)}, u32[]{:S(2)}, u32[]{:S(2)}) collective-permute-start(bf16[768,384]{0,1:T(8,128)(2,1)S(1)} %convolution_convert_fusion.5), channel_id=1, source_target_pairs={{0,1},{1,0},{2,3},{3,2},{4,5},{5,4},{6,7},{7,6},{8,9},{9,8},{10,11... | collective-permute-start | bytes 1769480 | tf_op jit(solution)/shard_map/ppermute | solution.py:317
  397.1 17.8 %copy-start.19 = (bf16[512,768]{1,0:T(8,128)(2,1)S(1)}, bf16[512,768]{1,0:T(8,128)(2,1)}, u32[]{:S(2)}) copy-start(bf16[512,768]{1,0:T(8,128)(2,1)} %param.16) | copy-start | bytes 2359300
  397.1 93.0 %collective-permute-start.18 = (bf16[1536,768]{1,0:T(8,128)(2,1)}, bf16[1536,768]{1,0:T(8,128)(2,1)}, u32[]{:S(2)}, u32[]{:S(2)}) collective-permute-start(bf16[1536,768]{1,0:T(8,128)(2,1)} %convolution_convert_fusion.2), channel_id=1, source_target_pairs={{0,1},{1,0},{2,3},{3,2},{4,5},{5,4},{6,7},{7,6},{8,9},{9,8},{10,11... | collective-permute-start | bytes 7077896 | tf_op jit(solution)/shard_map/ppermute | solution.py:317
  423.4 150.0 %reduce-scatter.7.cloned.1.call-start = ((), (), s32[]{:S(2)}) async-start(), calls=%async_computation.12 | async-start | bytes 2654208 | tf_op jit(solution)/shard_map/reduce_scatter | solution.py:592
  484.2 150.8 %collective-permute-start.34 = (bf16[2048,128]{1,0:T(8,128)(2,1)}, bf16[2048,128]{1,0:T(8,128)(2,1)}, u32[]{:S(2)}, u32[]{:S(2)}) collective-permute-start(bf16[2048,128]{1,0:T(8,128)(2,1)} %get-tuple-element.131), channel_id=1, source_target_pairs={{0,7},{1,6},{2,5},{3,4},{4,3},{5,2},{6,1},{7,0},{8,15},{9,14},{10,... | collective-permute-start | bytes 1572872 | tf_op jit(solution)/shard_map/ppermute | solution.py:351
  485.0 151.6 %collective-permute-start.33 = (bf16[2048,128]{1,0:T(8,128)(2,1)}, bf16[2048,128]{1,0:T(8,128)(2,1)}, u32[]{:S(2)}, u32[]{:S(2)}) collective-permute-start(bf16[2048,128]{1,0:T(8,128)(2,1)} %get-tuple-element.132), channel_id=1, source_target_pairs={{0,6},{1,7},{2,4},{3,5},{4,2},{5,3},{6,0},{7,1},{8,14},{9,15},{10,... | collective-permute-start | bytes 1572872 | tf_op jit(solution)/shard_map/ppermute | solution.py:351
  486.5 150.0 %collective-permute-start.32 = (bf16[2048,128]{1,0:T(8,128)(2,1)}, bf16[2048,128]{1,0:T(8,128)(2,1)}, u32[]{:S(2)}, u32[]{:S(2)}) collective-permute-start(bf16[2048,128]{1,0:T(8,128)(2,1)} %get-tuple-element.133), channel_id=1, source_target_pairs={{0,5},{1,4},{2,7},{3,6},{4,1},{5,0},{6,3},{7,2},{8,13},{9,12},{10,... | collective-permute-start | bytes 1572872 | tf_op jit(solution)/shard_map/ppermute | solution.py:351
  487.6 149.8 %collective-permute-start.31 = (bf16[2048,128]{1,0:T(8,128)(2,1)}, bf16[2048,128]{1,0:T(8,128)(2,1)}, u32[]{:S(2)}, u32[]{:S(2)}) collective-permute-start(bf16[2048,128]{1,0:T(8,128)(2,1)} %get-tuple-element.134), channel_id=1, source_target_pairs={{0,4},{1,5},{2,6},{3,7},{4,0},{5,1},{6,2},{7,3},{8,12},{9,13},{10,... | collective-permute-start | bytes 1572872 | tf_op jit(solution)/shard_map/ppermute | solution.py:351
  490.1 152.7 %collective-permute-start.30 = (bf16[2048,128]{1,0:T(8,128)(2,1)}, bf16[2048,128]{1,0:T(8,128)(2,1)}, u32[]{:S(2)}, u32[]{:S(2)}) collective-permute-start(bf16[2048,128]{1,0:T(8,128)(2,1)} %get-tuple-element.135), channel_id=1, source_target_pairs={{0,3},{1,2},{2,1},{3,0},{4,7},{5,6},{6,5},{7,4},{8,11},{9,10},{10,... | collective-permute-start | bytes 1572872 | tf_op jit(solution)/shard_map/ppermute | solution.py:351
  495.3 203.6 %reduce-scatter.9.cloned.1.call-start = ((), (), s32[]{:S(2)}) async-start(), calls=%async_computation.13 | async-start | bytes 4718592 | tf_op jit(solution)/shard_map/reduce_scatter | solution.py:603
  573.4 247.6 %reduce-scatter.11.cloned.1.call-start = ((), (), s32[]{:S(2)}) async-start(), calls=%async_computation.14 | async-start | bytes 3932160 | tf_op jit(solution)/shard_map/reduce_scatter | solution.py:636
  573.5 56.7 %copy-start.28 = (bf16[64,2048]{1,0:T(8,128)(2,1)S(1)}, bf16[64,2048]{1,0:T(8,128)(2,1)}, u32[]{:S(2)}) copy-start(bf16[64,2048]{1,0:T(8,128)(2,1)} %get-tuple-element.40) | copy-start | bytes 786436
  635.0 35.3 %collective-permute-start.29 = (bf16[2048,128]{1,0:T(8,128)(2,1)S(1)}, bf16[2048,128]{1,0:T(8,128)(2,1)}, u32[]{:S(2)}, u32[]{:S(2)}) collective-permute-start(bf16[2048,128]{1,0:T(8,128)(2,1)S(1)} %copy-done.24), channel_id=1, source_target_pairs={{0,2},{1,3},{2,0},{3,1},{4,6},{5,7},{6,4},{7,5},{8,10},{9,11},{10,... | collective-permute-start | bytes 1572872 | tf_op jit(solution)/shard_map/ppermute | solution.py:351
  636.5 34.7 %collective-permute-start.28 = (bf16[2048,128]{1,0:T(8,128)(2,1)S(1)}, bf16[2048,128]{1,0:T(8,128)(2,1)}, u32[]{:S(2)}, u32[]{:S(2)}) collective-permute-start(bf16[2048,128]{1,0:T(8,128)(2,1)S(1)} %copy-done.23), channel_id=1, source_target_pairs={{0,1},{1,0},{2,3},{3,2},{4,5},{5,4},{6,7},{7,6},{8,9},{9,8},{10,11... | collective-permute-start | bytes 1572872 | tf_op jit(solution)/shard_map/ppermute | solution.py:351
  636.6 34.7 %collective-permute-start.27 = (bf16[2048,128]{1,0:T(8,128)(2,1)}, bf16[2048,128]{1,0:T(8,128)(2,1)}, u32[]{:S(2)}, u32[]{:S(2)}) collective-permute-start(bf16[2048,128]{1,0:T(8,128)(2,1)} %get-tuple-element.124), channel_id=1, source_target_pairs={{0,7},{1,6},{2,5},{3,4},{4,3},{5,2},{6,1},{7,0},{8,15},{9,14},{10,... | collective-permute-start | bytes 1572872 | tf_op jit(solution)/shard_map/ppermute | solution.py:351
  637.4 35.4 %collective-permute-start.26 = (bf16[2048,128]{1,0:T(8,128)(2,1)S(1)}, bf16[2048,128]{1,0:T(8,128)(2,1)}, u32[]{:S(2)}, u32[]{:S(2)}) collective-permute-start(bf16[2048,128]{1,0:T(8,128)(2,1)S(1)} %get-tuple-element.125), channel_id=1, source_target_pairs={{0,6},{1,7},{2,4},{3,5},{4,2},{5,3},{6,0},{7,1},{8,14},{9,15},{10,... | collective-permute-start | bytes 1572872 | tf_op jit(solution)/shard_map/ppermute | solution.py:351
  642.8 33.0 %collective-permute-start.25 = (bf16[2048,128]{1,0:T(8,128)(2,1)}, bf16[2048,128]{1,0:T(8,128)(2,1)S(1)}, u32[]{:S(2)}, u32[]{:S(2)}) collective-permute-start(bf16[2048,128]{1,0:T(8,128)(2,1)} %get-tuple-element.126), channel_id=1, source_target_pairs={{0,5},{1,4},{2,7},{3,6},{4,1},{5,0},{6,3},{7,2},{8,13},{9,12},{10,... | collective-permute-start | bytes 1572872 | tf_op jit(solution)/shard_map/ppermute | solution.py:351
  670.3 14.5 %collective-permute-start.24 = (bf16[2048,128]{1,0:T(8,128)(2,1)}, bf16[2048,128]{1,0:T(8,128)(2,1)S(1)}, u32[]{:S(2)}, u32[]{:S(2)}) collective-permute-start(bf16[2048,128]{1,0:T(8,128)(2,1)} %get-tuple-element.127), channel_id=1, source_target_pairs={{0,4},{1,5},{2,6},{3,7},{4,0},{5,1},{6,2},{7,3},{8,12},{9,13},{10,... | collective-permute-start | bytes 1572872 | tf_op jit(solution)/shard_map/ppermute | solution.py:351
  671.3 14.4 %collective-permute-start.23 = (bf16[2048,128]{1,0:T(8,128)(2,1)}, bf16[2048,128]{1,0:T(8,128)(2,1)S(1)}, u32[]{:S(2)}, u32[]{:S(2)}) collective-permute-start(bf16[2048,128]{1,0:T(8,128)(2,1)} %get-tuple-element.128), channel_id=1, source_target_pairs={{0,3},{1,2},{2,1},{3,0},{4,7},{5,6},{6,5},{7,4},{8,11},{9,10},{10,... | collective-permute-start | bytes 1572872 | tf_op jit(solution)/shard_map/ppermute | solution.py:351
  671.3 25.7 %collective-permute-start.22 = (bf16[2048,128]{1,0:T(8,128)(2,1)}, bf16[2048,128]{1,0:T(8,128)(2,1)S(1)}, u32[]{:S(2)}, u32[]{:S(2)}) collective-permute-start(bf16[2048,128]{1,0:T(8,128)(2,1)} %get-tuple-element.129), channel_id=1, source_target_pairs={{0,2},{1,3},{2,0},{3,1},{4,6},{5,7},{6,4},{7,5},{8,10},{9,11},{10,... | collective-permute-start | bytes 1572872 | tf_op jit(solution)/shard_map/ppermute | solution.py:351
  672.8 24.1 %collective-permute-start.21 = (bf16[2048,128]{1,0:T(8,128)(2,1)}, bf16[2048,128]{1,0:T(8,128)(2,1)S(1)}, u32[]{:S(2)}, u32[]{:S(2)}) collective-permute-start(bf16[2048,128]{1,0:T(8,128)(2,1)} %get-tuple-element.123), channel_id=1, source_target_pairs={{0,1},{1,0},{2,3},{3,2},{4,5},{5,4},{6,7},{7,6},{8,9},{9,8},{10,11... | collective-permute-start | bytes 1572872 | tf_op jit(solution)/shard_map/ppermute | solution.py:351
  675.8 23.1 %copy-start.12 = (bf16[3,2,64,768]{3,2,1,0:T(8,128)(2,1)S(1)}, bf16[3,2,64,768]{3,2,1,0:T(8,128)(2,1)}, u32[]{:S(2)}) copy-start(bf16[3,2,64,768]{3,2,1,0:T(8,128)(2,1)} %copy-done.11) | copy-start | bytes 1769476
  714.1 1.9 collective-permute-start.35
  714.7 56.1 %collective-permute-start.41 = (bf16[192,768]{1,0:T(8,128)(2,1)}, bf16[192,768]{1,0:T(8,128)(2,1)S(1)}, u32[]{:S(2)}, u32[]{:S(2)}) collective-permute-start(bf16[192,768]{1,0:T(8,128)(2,1)} %reduce-scatter.7.cloned.1.call-done), channel_id=1, source_target_pairs={{0,2},{2,0},{1,3},{3,1},{4,6},{6,4},{5,7},{7,5},{8,10},{10,8},{9,1... | collective-permute-start | bytes 884744 | tf_op jit(solution)/shard_map/ppermute | solution.py:317
  716.1 54.8 %copy-start.26 = (bf16[192,768]{1,0:T(8,128)(2,1)S(1)}, bf16[192,768]{1,0:T(8,128)(2,1)}, u32[]{:S(2)}) copy-start(bf16[192,768]{1,0:T(8,128)(2,1)} %reduce-scatter.7.cloned.1.call-done) | copy-start | bytes 884740
  716.1 64.7 %collective-permute-start.36 = (bf16[608,384]{1,0:T(8,128)(2,1)S(1)}, bf16[608,384]{1,0:T(8,128)(2,1)S(1)}, u32[]{:S(2)}, u32[]{:S(2)}) collective-permute-start(bf16[608,384]{1,0:T(8,128)(2,1)S(1)} %add_convert_fusion.9), channel_id=1, source_target_pairs={{0,2},{2,0},{1,3},{3,1},{4,6},{6,4},{5,7},{7,5},{8,10},{10,8},{9,1... | collective-permute-start | bytes 1400840 | tf_op jit(solution)/shard_map/ppermute | solution.py:317
  722.7 68.7 %collective-permute-start.39 = (bf16[96,1920]{0,1:T(8,128)(2,1)S(1)}, bf16[96,1920]{0,1:T(8,128)(2,1)}, u32[]{:S(2)}, u32[]{:S(2)}) collective-permute-start(bf16[96,1920]{0,1:T(8,128)(2,1)S(1)} %copy.67), channel_id=1, source_target_pairs={{0,2},{2,0},{1,3},{3,1},{4,6},{6,4},{5,7},{7,5},{8,10},{10,8},{9,1... | collective-permute-start | bytes 1105928 | tf_op jit(solution)/shard_map/ppermute | solution.py:317
  771.7 21.1 %copy-start.7 = (f32[512,768]{1,0:T(8,128)S(1)}, f32[512,768]{1,0:T(8,128)}, u32[]{:S(2)}) copy-start(f32[512,768]{1,0:T(8,128)} %copy-done.6) | copy-start | bytes 4718596
  771.7 27.1 %collective-permute-start.42 = (bf16[192,768]{1,0:T(8,128)(2,1)}, bf16[192,768]{1,0:T(8,128)(2,1)}, u32[]{:S(2)}, u32[]{:S(2)}) collective-permute-start(bf16[192,768]{1,0:T(8,128)(2,1)} %add_convert_fusion.10), channel_id=1, source_target_pairs={{0,1},{1,0},{2,3},{3,2},{4,5},{5,4},{6,7},{7,6},{8,9},{9,8},{10,11... | collective-permute-start | bytes 884744 | tf_op jit(solution)/shard_map/ppermute | solution.py:317
  783.6 21.7 %all-to-all-start.3 = ((bf16[4,208,384]{2,1,0:T(8,128)(2,1)}), bf16[4,208,384]{2,1,0:T(8,128)(2,1)}, u32[]{:S(2)}, u32[]{:S(2)}) async-start(bf16[4,208,384]{2,1,0:T(8,128)(2,1)} %fusion.48), calls=%async_computation.6 | async-start | bytes 1277952 | tf_op jit(solution)/shard_map/all_to_all | solution.py:409
  792.6 8.8 %collective-permute-start.40 = (bf16[96,1920]{0,1:T(8,128)(2,1)S(1)}, bf16[96,1920]{0,1:T(8,128)(2,1)}, u32[]{:S(2)}, u32[]{:S(2)}) collective-permute-start(bf16[96,1920]{0,1:T(8,128)(2,1)S(1)} %add_convert_fusion.7), channel_id=1, source_target_pairs={{0,1},{1,0},{2,3},{3,2},{4,5},{5,4},{6,7},{7,6},{8,9},{9,8},{10,11... | collective-permute-start | bytes 1105928 | tf_op jit(solution)/shard_map/ppermute | solution.py:317
  808.7 8.8 %collective-permute-start.37 = (bf16[304,384]{1,0:T(8,128)(2,1)}, bf16[304,384]{1,0:T(8,128)(2,1)}, u32[]{:S(2)}, u32[]{:S(2)}) collective-permute-start(bf16[304,384]{1,0:T(8,128)(2,1)} %fusion.74), channel_id=1, source_target_pairs={{0,4},{4,0},{1,5},{5,1},{2,6},{6,2},{3,7},{7,3},{8,12},{12,8},{9,1... | collective-permute-start | bytes 700424 | tf_op jit(solution)/shard_map/ppermute | solution.py:317
  818.5 1.5 collective-permute-start.38
  (43 other events, 217.5 us)
Sparse Core Ops, SparseCore 0:
  9.6 74.7 all-gather.4
  104.4 52.7 all-gather.6
  218.0 61.1 all-gather.8
  284.3 58.5 all-gather.10
  423.6 70.7 reduce-scatter.12
  498.2 75.2 reduce-scatter.6
  577.1 50.3 reduce-scatter.8
  706.5 64.1 reduce-scatter.10

commit v3 on v2

--- a/solution.py
+++ b/solution.py
@@ -77,7 +77,7 @@
 
 def key_place(info, chunk, strips):
     strip = lax.div(chunk, 8)
-    holder = lax.rem(chunk, 8) ^ flip_of(info, strip) ^ info[2]
+    holder = lax.rem(chunk, 8) ^ flip_of(info, strip)
     return holder * strips + strip
 
 
@@ -161,7 +161,7 @@
         ],
         compiler_params=pltpu.CompilerParams(vmem_limit_bytes=56 * 2**20),
         cost_estimate=pl.CostEstimate(
-            flops=40 * 10**9, bytes_accessed=8 * 2**20, transcendentals=keys * rows // 2
+            flops=15 * 10**9, bytes_accessed=8 * 2**20, transcendentals=0
         ),
     )(r, query, kv)
 
@@ -282,7 +282,7 @@
         ],
         compiler_params=pltpu.CompilerParams(vmem_limit_bytes=56 * 2**20),
         cost_estimate=pl.CostEstimate(
-            flops=100 * 10**9, bytes_accessed=12 * 2**20, transcendentals=keys * rows // 2
+            flops=25 * 10**9, bytes_accessed=12 * 2**20, transcendentals=0
         ),
     )(r, query, grad, out, lse, kv)
 
@@ -343,12 +343,68 @@
     ]
 
 
-def by_ring(array, ring, distance):
-    size = lax.axis_size("g") * lax.axis_size("z")
-    pairs = [
-        (b * ring + r, b * ring + (r ^ distance)) for b in range(size) for r in range(ring)
-    ]
-    return lax.ppermute(array, ALL, pairs)
+def pack_weights(expand, reduce, out, c):
+    half_hidden = expand.shape[1] // 2
+    model, here = out.shape
+    e = part(expand.T, c, half_hidden, 0)
+    w = reduce_half(reduce, c, half_hidden)
+    o = part(out.T, c, model // 2, 1)
+    return jnp.concatenate(
+        [
+            e,
+            w[:, :model],
+            w[:, model:],
+            jnp.concatenate([o[: here // 2], o[here // 2 :]], axis=1),
+        ]
+    )
+
+
+def unpack_weights(packed, half_hidden, here):
+    shards, _, model = packed.shape
+    first, second = half_hidden, half_hidden + here
+    e = packed[:, :first].reshape(-1, model)
+    w = jnp.concatenate(
+        [
+            packed[:, first:second].reshape(-1, model),
+            packed[:, second : second + here].reshape(-1, model),
+        ],
+        axis=1,
+    )
+    o = packed[:, second + here :].reshape(shards, here // 2, 2, model // 2)
+    return e, w, o.transpose(0, 2, 1, 3).reshape(-1, model // 2)
+
+
+def pack_grads(e, w, o, shards):
+    model = e.shape[1]
+    here = model // shards
+    o = o.reshape(shards, 2, here // 2, model // 2).transpose(0, 2, 1, 3)
+    return jnp.concatenate(
+        [
+            e.reshape(shards, -1, model),
+            w[:, :model].reshape(shards, here, model),
+            w[:, model:].reshape(shards, here, model),
+            o.reshape(shards, here // 2, model),
+        ],
+        axis=1,
+    )
+
+
+def unpack_grads(own, other, c, half_hidden, here):
+    model = own.shape[1]
+    first, second = half_hidden, half_hidden + here
+
+    def reduce_of(rows):
+        w = jnp.concatenate([rows[first:second], rows[second : second + here]], axis=1)
+        return w.reshape(here, -1, 1, half_hidden)
+
+    def out_of(rows):
+        o = rows[second + here :]
+        return jnp.concatenate([o[:, : model // 2], o[:, model // 2 :]])
+
+    e = in_order(c, own[:first], other[:first], 0)
+    w = in_order(c, reduce_of(own), reduce_of(other), 2).reshape(here, -1)
+    o = in_order(c, out_of(own), out_of(other), 1)
+    return e.T.astype(F32), w.T.astype(F32), o.T.astype(F32)
 
 
 def fetch_triple(triple_weight, small, at):
@@ -472,8 +528,7 @@
     half_hidden = hidden_here // 2
     half_model = model // 2
     groups = spread_groups(blocks, depth, ring)
-    info_far = jnp.stack([r, z % 2, r])
-    info_abs = jnp.stack([r, z % 2, jnp.zeros_like(r)])
+    info = jnp.stack([r, z % 2])
     special = shards == 8 and blocks == 1
 
     small = jnp.concatenate(
@@ -516,33 +571,29 @@
         return kv[:, h * 128 : (h + 1) * 128]
 
     keys = [lax.all_gather(pair(0), RING, axis=0, tiled=True)]
-    for h in range(1, heads):
-        pieces = [pair(h)] + [by_ring(pair(h), ring, d) for d in range(1, ring)]
-        keys.append(jnp.concatenate(pieces))
-    infos = [info_abs] + [info_far] * (heads - 1)
-
-    own_b = jnp.concatenate(
-        [
-            part(out_weight.T, c, half_model, 1),
-            reduce_half(reduce_weight, c, half_hidden),
-        ],
-        axis=1,
-    )
-    own_a = part(expand_weight.T, c, half_hidden, 0)
-    own_a, own_b, keys[0] = lax.optimization_barrier((own_a, own_b, keys[0]))
-    mine_b = lax.all_gather(own_b, WEIGHT_AXES, axis=0, tiled=True)
-    mine_a = lax.all_gather(own_a, WEIGHT_AXES, axis=0, tiled=True)
-    both_b = (mine_b, swap(mine_b, "c"))
-    expand_t = (mine_a, swap(mine_a, "c"))
-    out_t = [b[:, :half_model] for b in both_b]
-    reduce_t = [b[:, half_model:] for b in both_b]
-
+    for h in range(1, heads - 1):
+        own_pair, keys[-1] = lax.optimization_barrier((pair(h), keys[-1]))
+        keys.append(lax.all_gather(own_pair, RING, axis=0, tiled=True))
+    copies = jnp.broadcast_to(pair(heads - 1), (ring,) + pair(0).shape)
+    keys.append(
+        lax.all_to_all(copies, RING, split_axis=0, concat_axis=0, tiled=True).reshape(-1, 128)
+    )
+
+    own_w = pack_weights(expand_weight, reduce_weight, out_weight, c)
+    own_w, keys[1] = lax.optimization_barrier((own_w, keys[1]))
+    mine_w = lax.all_gather(own_w, WEIGHT_AXES, axis=0, tiled=False)
     outs, lses = [], []
     for h in range(heads):
-        out_h, lse_h = attend(infos[h], head(q_t, h), keys[h])
+        q_h = head(q_t, h)
+        if h:
+            q_h, outs[-1] = lax.optimization_barrier((q_h, outs[-1]))
+        out_h, lse_h = attend(info, q_h, keys[h])
         outs.append(out_h)
         lses.append(lse_h)
     out_all = jnp.concatenate([o.astype(BF) for o in outs])
+    mine_w, out_all = lax.optimization_barrier((mine_w, out_all))
+    halves = [unpack_weights(w, half_hidden, here) for w in (mine_w, swap(mine_w, "c"))]
+    expand_t, reduce_t, out_t = zip(*halves)
     att = lax.all_to_all(
         out_all, ALL, split_axis=1, concat_axis=0, axis_index_groups=groups, tiled=True
     )
@@ -585,43 +636,36 @@
     )
     grads_o = [mm("tm,ft->mf", grad_branch, a).astype(BF) for a in atts]
 
-    sum_a = (grads_a[0].astype(F32) + swap(grads_a[1], "c").astype(F32)).astype(BF)
-    sum_r = (grads_r[0].astype(F32) + swap(grads_r[1], "c").astype(F32)).astype(BF)
-    sum_o = (grads_o[0].astype(F32) + swap(grads_o[1], "c").astype(F32)).astype(BF)
-    sum_b = jnp.concatenate([sum_o, sum_r], axis=1)
-    sum_a = lax.psum_scatter(sum_a, WEIGHT_AXES, scatter_dimension=0, tiled=True)
-    sum_b = lax.psum_scatter(sum_b, WEIGHT_AXES, scatter_dimension=0, tiled=True)
-
-    dqs, dkvs = [None] * heads, [None] * heads
-    for h in list(range(1, heads)) + [0]:
-        dq_h, dkv_h = attend_back(
-            infos[h], head(q_t, h), head(grad_heads, h), outs[h], lses[h], keys[h]
-        )
-        dqs[h] = dq_h
-        if h == 0:
-            dkv_h, sum_a, sum_b = lax.optimization_barrier((dkv_h, sum_a, sum_b))
-            dkvs[h] = lax.psum_scatter(dkv_h, RING, scatter_dimension=0, tiled=True)
+    packs = [
+        pack_grads(e, w, o, shards) for e, w, o in zip(grads_a, grads_r, grads_o)
+    ]
+    sum_w = (packs[0].astype(F32) + swap(packs[1], "c").astype(F32)).astype(BF)
+    sum_w = lax.psum_scatter(sum_w, WEIGHT_AXES, scatter_dimension=0, tiled=False)
+
+    dqs, dkvs = [], []
+    for h in range(heads):
+        g_h = head(grad_heads, h)
+        if h:
+            g_h, dqs[-1] = lax.optimization_barrier((g_h, dqs[-1]))
+        if h > 1:
+            g_h, dkvs[h - 2] = lax.optimization_barrier((g_h, dkvs[h - 2]))
+        dq_h, dkv_h = attend_back(info, head(q_t, h), g_h, outs[h], lses[h], keys[h])
+        dqs.append(dq_h)
+        if h == heads - 1:
+            dkv_h, sum_w, dkvs[-1] = lax.optimization_barrier((dkv_h, sum_w, dkvs[-1]))
+            dkvs.append(lax.psum_scatter(dkv_h, RING, scatter_dimension=0, tiled=True))
         else:
-            pieces = dkv_h.reshape(ring, depth * tokens, 128)
-            added = pieces[0].astype(F32)
-            for d in range(1, ring):
-                added = added + by_ring(pieces[d], ring, d).astype(F32)
-            dkvs[h] = added.astype(BF)
-
-    sum_a = swap_sum(sum_a, "y").astype(BF)
-    sum_b = swap_sum(sum_b, "y").astype(BF)
-    full_a = in_order(c, sum_a, swap(sum_a, "c"), 0)
-    other_b = swap(sum_b, "c")
-    full_o = in_order(c, sum_b[:, :half_model], other_b[:, :half_model], 1)
-    full_r = in_order(
-        c,
-        sum_b[:, half_model:].reshape(here, shards, 1, half_hidden),
-        other_b[:, half_model:].reshape(here, shards, 1, half_hidden),
-        2,
-    ).reshape(here, shards * hidden_here)
-    grad_expand_w = full_a.T.astype(F32)
-    grad_out_w = full_o.T.astype(F32)
-    grad_reduce_w = full_r.T.astype(F32)
+            pieces = lax.all_to_all(
+                dkv_h.reshape(ring, depth * tokens, 128), RING, split_axis=0, concat_axis=0, tiled=True
+            )
+            dkvs.append(pieces)
+
+    for h in range(heads - 1):
+        dkvs[h] = jnp.sum(dkvs[h].astype(F32), axis=0).astype(BF)
+    sum_w = swap_sum(sum_w, "y").astype(BF)
+    grad_expand_w, grad_reduce_w, grad_out_w = unpack_grads(
+        sum_w, swap(sum_w, "c"), c, half_hidden, here
+    )
 
     dq = jnp.concatenate(dqs)
     dkv = jnp.concatenate(dkvs, axis=1)

time: 839 us -> 777 us (0.926)
  waiting for transfers between devices: 308 us -> 265 us
  matrix products: 73.6 us -> 59.6 us
  local copies, waits for them, and re-layouts: 67.9 us -> 56.2 us
  other arithmetic: 35.3 us -> 45.7 us
    ppermute x28 -> x0, waiting for transfers between devices: 121 us -> none  [by_ring(): return lax.ppermute(array, ALL, pairs)]
    all_gather x1, waiting for transfers between devices: 0.01 us -> 36.1 us  [on_device(): keys = [lax.all_gather(pair(0), RING, axis=0, tiled=True)]]
    ppermute x28 -> x0, starting transfers between devices: 24.6 us -> none  [by_ring(): return lax.ppermute(array, ALL, pairs)]
    all_gather x2, waiting for transfers between devices: 13.9 us -> 34 us  [the longest x1 34 us: on_device(): keys.append(lax.all_gather(own_pair, RING, axis=0, tiled=True))]
    reduce_scatter x2, waiting for transfers between devices: 20.4 us -> 38.2 us  [the longest x1 38.2 us: on_device(): dkvs.append(lax.psum_scatter(dkv_h, RING, scatter_dimension=0, tiled=True))]
    all_to_all x0 -> x3, starting transfers between devices: none -> 14.1 us  [the longest x2 9.1 us: on_device(): lax.all_to_all(dkv_h.reshape(ring, depth * tokens, 128), RING, split_axis...]
    dot_general x24, matrix products: 73.6 us -> 59.6 us  [mm(): return jnp.einsum(spec, a, b, preferred_element_type=F32)]
    unnamed x123 -> x101, local copies, waits for them, and re-layouts: 20.5 us -> 9.2 us
  transfers between devices with their start and end apart: 55 -> 24, of which waited for: 23 -> 12; matrix products, arithmetic and copies ran while one was open for 17% -> 15% of each run, Pallas kernels for 34% -> 37%
where the time goes in v3:
time: 777 us; the launch traced here: 767 us
  Pallas kernels  280 us (36%)
  waiting for transfers between devices  265 us (34%)
  matrix products  59.6 us (8%)
  local copies, waits for them, and re-layouts  56.2 us (7%)
  other arithmetic  45.7 us (6%)
  starting transfers between devices  44.6 us (6%)
  between operations  15.7 us (2%)
    pallas_call x3, Pallas kernels, attend_back(): pl.pallas_call(functools.partial(backward_kernel, strips, unroll), grid=(...  170 us
    ppermute x10, waiting for transfers between devices, swap(): return lax.ppermute(array, axis, [(0, 1), (1, 0)])  111 us
    pallas_call x3, Pallas kernels, attend(): pl.pallas_call(functools.partial(forward_kernel, strips, unroll), grid=(s...  110 us
    dot_general x24, matrix products, mm(): return jnp.einsum(spec, a, b, preferred_element_type=F32)  59.6 us
    reduce_scatter x1, waiting for transfers between devices, on_device(): dkvs.append(lax.psum_scatter(dkv_h, RING, scatter_dimension=0, tiled=True))  38.2 us
    all_gather x1, waiting for transfers between devices, on_device(): keys = [lax.all_gather(pair(0), RING, axis=0, tiled=True)]  36.1 us
    all_gather x1, waiting for transfers between devices, on_device(): keys.append(lax.all_gather(own_pair, RING, axis=0, tiled=True))  34 us
    all_to_all x1, waiting for transfers between devices, fetch_triple(): got = lax.all_to_all(slots, 'z', split_axis=0, concat_axis=0, tiled=True)  18.1 us
  transfers between devices with their start and end apart: 24, of which 12 were waited for; matrix products, arithmetic and copies ran while one was open for 15% of the time, Pallas kernels for 37%

profile of v3, /device:TPU:0, one launch (start us, length us, event | category | flops | bytes accessed | tf_op | source)
XLA Modules:
  0.0 766.9 jit_solution(6697981709396002229)
XLA Ops:
  7.9 6.1 concatenate.130
  15.1 3.0 collective-permute-start
  18.1 49.2 %collective-permute-done = bf16[304,384]{1,0:T(8,128)(2,1)S(1)} collective-permute-done((bf16[304,384]{1,0:T(8,128)(2,1)S(1)}, bf16[304,384]{1,0:T(8,128)(2,1)S(1)}, u32[]{:S(2)}, u32[]{:S(2)}) %collective-permute-start) | collective-permute-done | bytes 233504 | tf_op jit(solution)/shard_map/ppermute | solution.py:317
  68.9 5.8 all-to-all-start
  74.7 18.1 %all-to-all-done = bf16[4,208,384]{2,1,0:T(8,128)(2,1)S(1)} async-done(((bf16[4,208,384]{2,1,0:T(8,128)(2,1)}), bf16[4,208,384]{2,1,0:T(8,128)(2,1)S(1)}, u32[]{:S(2)}, u32[]{:S(2)}) %all-to-all-start) | async-done | bytes 639008 | tf_op jit(solution)/shard_map/all_to_all | solution.py:424
  95.2 2.8 convert_reduce_fusion
  100.9 1.8 add_convert_fusion.1
  104.1 36.1 %all-gather.8.cloned.1.call-done.kv_ref = bf16[16384,128]{1,0:T(8,128)(2,1)} async-done(((bf16[2048,128]{1,0:T(8,128)(2,1)}), bf16[16384,128]{1,0:T(8,128)(2,1)}) %all-gather.8.cloned.1.call-update) | async-done | bytes 4194320 | tf_op jit(solution)/shard_map/all_gather | solution.py:573
  141.2 2.5 dynamic-slice_reduce_fusion
  145.4 34.0 %all-gather.10.cloned.1.call-done.kv_ref = bf16[16384,128]{1,0:T(8,128)(2,1)} async-done(((bf16[2048,128]{1,0:T(8,128)(2,1)}), bf16[16384,128]{1,0:T(8,128)(2,1)}) %all-gather.10.cloned.1.call-update) | async-done | bytes 4194320 | tf_op jit(solution)/shard_map/all_gather | solution.py:576
  179.4 2.6 broadcast_in_dim.22
  182.0 5.0 all-to-all-start.1
  187.8 3.2 fusion.22
  191.9 36.7 %shard_map.262 = (f32[64,2048]{1,0:T(8,128)}, f32[8,2048]{1,0:T(8,128)}) custom-call(s32[2]{0:T(128)} %pad_add_fusion.r_ref, bf16[64,2048]{1,0:T(8,128)(2,1)} %get-tuple-element.166.q_ref, bf16[16384,128]{1,0:T(8,128)(2,1)} %all-gather.8.cloned.1.call-done.kv_ref), custom_call_target="tpu_custom_call" | custom-call | flops 15000000512 | bytes 8388608 | tf_op jit(solution)/shard_map/pallas_call | solution.py:139
  229.7 36.7 %shard_map.263 = (f32[64,2048]{1,0:T(8,128)}, f32[8,2048]{1,0:T(8,128)}) custom-call(s32[2]{0:T(128)} %pad_add_fusion.r_ref, bf16[64,2048]{1,0:T(8,128)(2,1)} %get-tuple-element.51.q_ref, bf16[16384,128]{1,0:T(8,128)(2,1)} %all-gather.10.cloned.1.call-done.kv_ref), custom_call_target="tpu_custom_call" | custom-call | flops 15000000512 | bytes 8388608 | tf_op jit(solution)/shard_map/pallas_call | solution.py:139
  266.4 36.8 %shard_map.264 = (f32[64,2048]{1,0:T(8,128)}, f32[8,2048]{1,0:T(8,128)}) custom-call(s32[2]{0:T(128)} %pad_add_fusion.r_ref, bf16[64,2048]{1,0:T(8,128)(2,1)} %get-tuple-element.55.q_ref, bf16[16384,128]{1,0:T(8,128)(2,1)} %bitcast.16.kv_ref), custom_call_target="tpu_custom_call" | custom-call | flops 15000000512 | bytes 8388608 | tf_op jit(solution)/shard_map/pallas_call | solution.py:139
  305.9 7.1 all-to-all-start.2
  315.7 3.3 slice.288
  319.1 3.2 fusion.79
  322.3 11.4 %all-to-all-done.2 = bf16[192,4,512]{2,0,1:T(8,128)(2,1)S(1)} async-done(((bf16[192,4,512]{2,0,1:T(8,128)(2,1)}), bf16[192,4,512]{2,0,1:T(8,128)(2,1)S(1)}, u32[]{:S(2)}, u32[]{:S(2)}) %all-to-all-start.2) | async-done | bytes 786464 | tf_op jit(solution)/shard_map/all_to_all | solution.py:597
  335.5 1.8 fusion.91
  339.0 1.4 convolution_add_fusion.2
  340.9 4.7 convert_reduce_fusion.2
  345.6 1.4 fusion.92
  347.0 1.8 slice.364
  348.8 1.4 convolution_add_fusion.1
  350.3 1.6 fusion.21
  351.9 1.8 fusion.78
  353.7 4.4 convert_reduce_fusion.1
  358.1 1.4 convolution_convert_fusion.1
  359.5 2.3 multiply_reduce_fusion
  361.8 1.9 fusion.77
  364.6 2.9 pad_maximum_fusion
  369.7 4.9 all-to-all-start.3
  374.6 1.8 convolution_convert_fusion.6
  376.5 3.6 fusion.20
  381.8 1.4 convolution_convert_fusion.3
  383.3 6.7 add_convert_fusion
  390.0 5.4 all-to-all-done.3
  397.3 57.0 %shard_map.265 = (bf16[64,2048]{1,0:T(8,128)(2,1)}, bf16[16384,128]{1,0:T(8,128)(2,1)}) custom-call(s32[2]{0:T(128)} %pad_add_fusion.r_ref, bf16[64,2048]{1,0:T(8,128)(2,1)} %get-tuple-element.166.q_ref, bf16[64,2048]{1,0:T(8,128)(2,1)} %bitcast.211, f32[64,2048]{1,0:T(8,128)} %get-tuple-element.50.out_ref, f32[8,2048]{1,0:T(8,128)} %get-tuple-element.59.lse_ref, ...), custom_call_target="tpu_custom_call" | custom-call | flops 24999999488 | bytes 12582912 | tf_op jit(solution)/shard_map/pallas_call | solution.py:257
  454.3 4.6 all-to-all-start.4
  459.6 56.6 %shard_map.266 = (bf16[64,2048]{1,0:T(8,128)(2,1)}, bf16[16384,128]{1,0:T(8,128)(2,1)}) custom-call(s32[2]{0:T(128)} %pad_add_fusion.r_ref, bf16[64,2048]{1,0:T(8,128)(2,1)} %get-tuple-element.51.q_ref, bf16[64,2048]{1,0:T(8,128)(2,1)} %bitcast.210, f32[64,2048]{1,0:T(8,128)} %get-tuple-element.54.out_ref, f32[8,2048]{1,0:T(8,128)} %get-tuple-element.63.lse_ref, ...), custom_call_target="tpu_custom_call" | custom-call | flops 24999999488 | bytes 12582912 | tf_op jit(solution)/shard_map/pallas_call | solution.py:257
  516.2 4.5 all-to-all-start.5
  521.5 56.6 %shard_map.267 = (bf16[64,2048]{1,0:T(8,128)(2,1)}, bf16[16384,128]{1,0:T(8,128)(2,1)}) custom-call(s32[2]{0:T(128)} %pad_add_fusion.r_ref, bf16[64,2048]{1,0:T(8,128)(2,1)} %get-tuple-element.55.q_ref, bf16[64,2048]{1,0:T(8,128)(2,1)} %bitcast.209, f32[64,2048]{1,0:T(8,128)} %get-tuple-element.56.out_ref, f32[8,2048]{1,0:T(8,128)} %get-tuple-element.69.lse_ref, ...), custom_call_target="tpu_custom_call" | custom-call | flops 24999999488 | bytes 12582912 | tf_op jit(solution)/shard_map/pallas_call | solution.py:257
  579.6 5.8 fusion.37
  586.8 3.5 reduce_sum.224
  593.1 3.6 convolution_convert_fusion.9
  596.7 3.1 reduce_sum.225
  599.8 2.0 collective-permute-start.8
  601.8 38.2 %reduce-scatter.6.cloned.1.call-done = bf16[2048,128]{1,0:T(8,128)(2,1)} async-done(((bf16[16384,128]{1,0:T(8,128)(2,1)}), bf16[2048,128]{1,0:T(8,128)(2,1)}) %reduce-scatter.6.cloned.1.call-update) | async-done | bytes 524304 | tf_op jit(solution)/shard_map/reduce_scatter | solution.py:656
  640.0 3.0 fusion.75
  643.0 6.0 fusion.76
  649.3 1.4 convert_reduce_fusion.3
  651.3 3.6 convolution_convert_fusion.4
  656.8 2.9 add_convert_fusion.2
  661.2 1.6 collective-permute-start.5
  663.2 56.5 %collective-permute-done.5 = bf16[608,384]{1,0:T(8,128)(2,1)} collective-permute-done((bf16[608,384]{1,0:T(8,128)(2,1)S(1)}, bf16[608,384]{1,0:T(8,128)(2,1)}, u32[]{:S(2)}, u32[]{:S(2)}) %collective-permute-start.5) | collective-permute-done | bytes 466976 | tf_op jit(solution)/shard_map/ppermute | solution.py:317
  721.9 4.3 all-to-all-start.6
  727.4 1.4 copy.101
  731.7 2.6 reshape.380
  734.4 9.4 %all-to-all-done.6 = bf16[4,208,384]{2,1,0:T(8,128)(2,1)} async-done(((bf16[4,208,384]{2,1,0:T(8,128)(2,1)}), bf16[4,208,384]{2,1,0:T(8,128)(2,1)}, u32[]{:S(2)}, u32[]{:S(2)}) %all-to-all-start.6) | async-done | bytes 639008 | tf_op jit(solution)/shard_map/all_to_all | solution.py:465
  748.0 4.7 collective-permute-done.6
  755.4 1.8 fusion.35
  757.3 2.6 fusion.31
  (280 shorter events, 55.5 us)
Async XLA Ops:
  7.2 136.8 %copy-start = (bf16[768,384]{1,0:T(8,128)(2,1)S(1)}, bf16[768,384]{1,0:T(8,128)(2,1)}, u32[]{:S(2)}) copy-start(bf16[768,384]{1,0:T(8,128)(2,1)} %param.26) | copy-start | bytes 1769476
  7.2 88.0 %all-gather.6.cloned.1.call-start = ((), (), s32[]{:S(2)}) async-start(), calls=%async_computation.10 | async-start | bytes 3932160 | tf_op jit(solution)/shard_map/all_gather | solution.py:547
  15.1 52.2 %collective-permute-start = (bf16[304,384]{1,0:T(8,128)(2,1)S(1)}, bf16[304,384]{1,0:T(8,128)(2,1)S(1)}, u32[]{:S(2)}, u32[]{:S(2)}) collective-permute-start(bf16[304,384]{1,0:T(8,128)(2,1)S(1)} %get-tuple-element.188), channel_id=1, source_target_pairs={{0,4},{4,0},{1,5},{5,1},{2,6},{6,2},{3,7},{7,3},{8,12},{12,8},{9,1... | collective-permute-start | bytes 700424 | tf_op jit(solution)/shard_map/ppermute | solution.py:317
  68.9 24.0 %all-to-all-start = ((bf16[4,208,384]{2,1,0:T(8,128)(2,1)}), bf16[4,208,384]{2,1,0:T(8,128)(2,1)S(1)}, u32[]{:S(2)}, u32[]{:S(2)}) async-start(bf16[4,208,384]{2,1,0:T(8,128)(2,1)} %pad_maximum_fusion.11), calls=%async_computation | async-start | bytes 1277952 | tf_op jit(solution)/shard_map/all_to_all | solution.py:424
  74.7 65.5 %all-gather.8.cloned.1.call-start = ((), (), s32[]{:S(2)}) async-start(), calls=%async_computation.11 | async-start | bytes 4718592 | tf_op jit(solution)/shard_map/all_gather | solution.py:573
  93.0 1.9 collective-permute-start.1
  93.9 5.6 copy-start.30
  95.0 92.7 %copy-start.9 = (bf16[576,768]{1,0:T(8,128)(2,1)}, bf16[576,768]{1,0:T(8,128)(2,1)S(1)}, u32[]{:S(2)}) copy-start(bf16[576,768]{1,0:T(8,128)(2,1)S(1)} %maximum_select_fusion) | copy-start | bytes 2654212
  95.1 5.7 copy-start.11
  95.2 3.2 copy-start.2
  98.4 2.4 copy-start.28
  100.9 1.9 copy-start.4
  102.7 37.5 %copy-start.23 = (bf16[3072,96]{0,1:T(8,128)(2,1)S(1)}, bf16[3072,96]{0,1:T(8,128)(2,1)}, u32[]{:S(2)}) copy-start(bf16[3072,96]{0,1:T(8,128)(2,1)} %param.28) | copy-start | bytes 1769476
  104.0 75.4 %all-gather.10.cloned.1.call-start = ((), (), s32[]{:S(2)}) async-start(), calls=%async_computation.12 | async-start | bytes 4718592 | tf_op jit(solution)/shard_map/all_gather | solution.py:576
  140.2 164.2 %all-gather.12.cloned.1.call-start = ((), (), s32[]{:S(2)}) async-start(), calls=%async_computation.16 | async-start | bytes 5971968 | tf_op jit(solution)/shard_map/all_gather | solution.py:584
  140.2 4.2 copy-start.32
  182.0 5.6 copy-start.36
  182.0 84.4 %all-to-all-start.1 = ((bf16[8,2048,128]{2,1,0:T(8,128)(2,1)}), bf16[8,2048,128]{2,1,0:T(8,128)(2,1)}, u32[]{:S(2)}, u32[]{:S(2)}) async-start(bf16[8,2048,128]{2,1,0:T(8,128)(2,1)} %broadcast_in_dim.22), calls=%async_computation.1 | async-start | bytes 8388608 | tf_op jit(solution)/shard_map/all_to_all | solution.py:579
  266.4 37.8 %copy-start.24 = (f32[64,2048]{1,0:T(8,128)S(1)}, f32[64,2048]{1,0:T(8,128)}, u32[]{:S(2)}) copy-start(f32[64,2048]{1,0:T(8,128)} %get-tuple-element.54.out_ref) | copy-start | bytes 1572868
  304.4 29.9 %collective-permute-start.2 = (bf16[8,432,768]{2,1,0:T(8,128)(2,1)}, bf16[8,432,768]{2,1,0:T(8,128)(2,1)}, u32[]{:S(2)}, u32[]{:S(2)}) collective-permute-start(bf16[8,432,768]{2,1,0:T(8,128)(2,1)} %bitcast.162), channel_id=1, source_target_pairs={{0,1},{1,0},{2,3},{3,2},{4,5},{5,4},{6,7},{7,6},{8,9},{9,8},{10,11... | collective-permute-start | bytes 15925256 | tf_op jit(solution)/shard_map/ppermute | solution.py:317
  305.9 27.8 %all-to-all-start.2 = ((bf16[192,4,512]{2,0,1:T(8,128)(2,1)}), bf16[192,4,512]{2,0,1:T(8,128)(2,1)S(1)}, u32[]{:S(2)}, u32[]{:S(2)}) async-start(bf16[192,4,512]{2,0,1:T(8,128)(2,1)} %bitcast.155), calls=%async_computation.2 | async-start | bytes 1572864 | tf_op jit(solution)/shard_map/all_to_all | solution.py:597
  333.7 1.8 copy-start.6
  333.7 1.8 copy-start.3
  333.7 1.8 copy-start.37
  337.3 1.7 copy-start.10
  337.3 1.7 copy-start.38
  337.9 20.1 %copy-start.20 = (bf16[512,768]{1,0:T(8,128)(2,1)}, bf16[512,768]{1,0:T(8,128)(2,1)S(1)}, u32[]{:S(2)}) copy-start(bf16[512,768]{1,0:T(8,128)(2,1)S(1)} %add_convert_fusion.3) | copy-start | bytes 2359300
  339.0 1.6 copy-start.18
  339.0 1.8 copy-start.19
  340.4 5.2 copy-start.46
  350.3 3.4 copy-start.44
  353.6 4.4 copy-start.13
  353.7 4.4 copy-start.15
  361.8 1.9 copy-start.7
  363.7 4.3 copy-start.5
  367.5 15.8 %collective-permute-start.3 = (bf16[8,432,768]{2,1,0:T(8,128)(2,1)}, bf16[8,432,768]{2,1,0:T(8,128)(2,1)}, u32[]{:S(2)}, u32[]{:S(2)}) collective-permute-start(bf16[8,432,768]{2,1,0:T(8,128)(2,1)} %pad_maximum_fusion), channel_id=1, source_target_pairs={{0,1},{1,0},{2,3},{3,2},{4,5},{5,4},{6,7},{7,6},{8,9},{9,8},{10,11... | collective-permute-start | bytes 15925256 | tf_op jit(solution)/shard_map/ppermute | solution.py:317
  369.7 25.7 %all-to-all-start.3 = ((bf16[4,192,512]{2,1,0:T(8,128)(2,1)}), bf16[4,192,512]{2,1,0:T(8,128)(2,1)}, u32[]{:S(2)}, u32[]{:S(2)}) async-start(bf16[4,192,512]{2,1,0:T(8,128)(2,1)} %bitcast.172), calls=%async_computation.3 | async-start | bytes 1572864 | tf_op jit(solution)/shard_map/all_to_all | solution.py:634
  374.6 203.5 %reduce-scatter.4.cloned.1.call-start = ((), (), s32[]{:S(2)}) async-start(), calls=%async_computation.13 | async-start | bytes 5971968 | tf_op jit(solution)/shard_map/reduce_scatter | solution.py:643
  380.2 1.6 copy-start.43
  454.3 61.9 %all-to-all-start.4 = ((bf16[8,2048,128]{2,1,0:T(8,128)(2,1)}), bf16[8,2048,128]{2,1,0:T(8,128)(2,1)}, u32[]{:S(2)}, u32[]{:S(2)}) async-start(bf16[8,2048,128]{2,1,0:T(8,128)(2,1)} %bitcast.171), calls=%async_computation.4 | async-start | bytes 8388608 | tf_op jit(solution)/shard_map/all_to_all | solution.py:658
  516.2 61.9 %all-to-all-start.5 = ((bf16[8,2048,128]{2,1,0:T(8,128)(2,1)}), bf16[8,2048,128]{2,1,0:T(8,128)(2,1)}, u32[]{:S(2)}, u32[]{:S(2)}) async-start(bf16[8,2048,128]{2,1,0:T(8,128)(2,1)} %bitcast.170), calls=%async_computation.6 | async-start | bytes 8388608 | tf_op jit(solution)/shard_map/all_to_all | solution.py:658
  520.8 119.2 %reduce-scatter.6.cloned.1.call-start = ((), (), s32[]{:S(2)}) async-start(), calls=%async_computation.14 | async-start | bytes 4718592 | tf_op jit(solution)/shard_map/reduce_scatter | solution.py:656
  578.2 177.2 %reduce-scatter.8.cloned.1.call-start = ((), (), s32[]{:S(2)}) async-start(), calls=%async_computation.15 | async-start | bytes 3932160 | tf_op jit(solution)/shard_map/reduce_scatter | solution.py:680
  579.6 5.8 copy-start.25
  579.6 6.5 copy-start.26
  586.8 3.5 copy-start.27
  599.8 43.2 %copy-start.29 = (f32[2048]{0:T(1024)S(1)}, f32[2048]{0:T(1024)}, u32[]{:S(2)}) copy-start(f32[2048]{0:T(1024)} %copy-done.28) | copy-start | bytes 24580
  599.8 43.2 %copy-start.34 = (f32[2048]{0:T(1024)S(1)}, f32[2048]{0:T(1024)}, u32[]{:S(2)}) copy-start(f32[2048]{0:T(1024)} %copy-done.33) | copy-start | bytes 24580
  599.8 59.9 %collective-permute-start.8 = (bf16[432,768]{1,0:T(8,128)(2,1)}, bf16[432,768]{1,0:T(8,128)(2,1)}, u32[]{:S(2)}, u32[]{:S(2)}) collective-permute-start(bf16[432,768]{1,0:T(8,128)(2,1)} %bitcast.206), channel_id=1, source_target_pairs={{0,2},{2,0},{1,3},{3,1},{4,6},{6,4},{5,7},{7,5},{8,10},{10,8},{9,1... | collective-permute-start | bytes 1990664 | tf_op jit(solution)/shard_map/ppermute | solution.py:317
  651.3 3.7 copy-start.12
  651.3 4.0 copy-start.45
  651.3 4.0 copy-start.47
  654.9 1.5 copy-start.14
  654.9 1.9 copy-start.16
  655.2 4.5 copy-start.22
  655.2 5.9 collective-permute-start.4
  660.9 65.4 %collective-permute-start.9 = (bf16[432,768]{1,0:T(8,128)(2,1)S(1)}, bf16[432,768]{1,0:T(8,128)(2,1)}, u32[]{:S(2)}, u32[]{:S(2)}) collective-permute-start(bf16[432,768]{1,0:T(8,128)(2,1)S(1)} %add_convert_fusion.4), channel_id=1, source_target_pairs={{0,1},{1,0},{2,3},{3,2},{4,5},{5,4},{6,7},{7,6},{8,9},{9,8},{10,11... | collective-permute-start | bytes 1990664 | tf_op jit(solution)/shard_map/ppermute | solution.py:317
  661.2 58.5 %collective-permute-start.5 = (bf16[608,384]{1,0:T(8,128)(2,1)S(1)}, bf16[608,384]{1,0:T(8,128)(2,1)}, u32[]{:S(2)}, u32[]{:S(2)}) collective-permute-start(bf16[608,384]{1,0:T(8,128)(2,1)S(1)} %add_convert_fusion.6), channel_id=1, source_target_pairs={{0,2},{2,0},{1,3},{3,1},{4,6},{6,4},{5,7},{7,5},{8,10},{10,8},{9,1... | collective-permute-start | bytes 1400840 | tf_op jit(solution)/shard_map/ppermute | solution.py:317
  721.9 21.9 %all-to-all-start.6 = ((bf16[4,208,384]{2,1,0:T(8,128)(2,1)}), bf16[4,208,384]{2,1,0:T(8,128)(2,1)}, u32[]{:S(2)}, u32[]{:S(2)}) async-start(bf16[4,208,384]{2,1,0:T(8,128)(2,1)} %fusion.41), calls=%async_computation.9 | async-start | bytes 1277952 | tf_op jit(solution)/shard_map/all_to_all | solution.py:465
  745.7 9.7 %copy-start.31 = (f32[768]{0:T(1024)S(1)}, f32[768]{0:T(1024)}, u32[]{:S(2)}) copy-start(f32[768]{0:T(1024)} %copy-done.30) | copy-start | bytes 9220
  745.9 6.9 collective-permute-start.6
  747.3 10.0 %copy-start.8 = (f32[512,768]{1,0:T(8,128)S(1)}, f32[512,768]{1,0:T(8,128)}, u32[]{:S(2)}) copy-start(f32[512,768]{1,0:T(8,128)} %get-tuple-element.147) | copy-start | bytes 4718596
  752.9 1.5 collective-permute-start.7
  755.4 4.4 copy-start.1
  (8 other events, 9.1 us)
Sparse Core Ops, SparseCore 0:
  9.6 74.7 all-gather.5
  104.1 35.9 all-gather.7
  142.6 36.7 all-gather.9
  182.0 107.2 all-gather.11
  390.1 112.2 reduce-scatter.3
  578.3 61.6 reduce-scatter.5
  649.2 66.6 reduce-scatter.7

commit v4 on v3

--- a/solution.py
+++ b/solution.py
@@ -580,8 +580,6 @@
     )
 
     own_w = pack_weights(expand_weight, reduce_weight, out_weight, c)
-    own_w, keys[1] = lax.optimization_barrier((own_w, keys[1]))
-    mine_w = lax.all_gather(own_w, WEIGHT_AXES, axis=0, tiled=False)
     outs, lses = [], []
     for h in range(heads):
         q_h = head(q_t, h)
@@ -590,13 +588,26 @@
         out_h, lse_h = attend(info, q_h, keys[h])
         outs.append(out_h)
         lses.append(lse_h)
-    out_all = jnp.concatenate([o.astype(BF) for o in outs])
-    mine_w, out_all = lax.optimization_barrier((mine_w, out_all))
+        if h == 0:
+            own_w, keys[1], outs[0] = lax.optimization_barrier((own_w, keys[1], outs[0]))
+            mine_w = lax.all_gather(own_w, WEIGHT_AXES, axis=0, tiled=False)
+
+    def to_tokens(values):
+        low = jnp.concatenate([v.astype(BF) for v in values])
+        got = lax.all_to_all(
+            low, ALL, split_axis=1, concat_axis=0, axis_index_groups=groups, tiled=True
+        )
+        return got.reshape(depth, low.shape[0], tokens)
+
+    early = to_tokens(outs[:-1])
+    late = outs[-1].astype(BF)
+    mine_w, late, early = lax.optimization_barrier((mine_w, late, early))
+    att = jnp.concatenate([early, to_tokens([late])], axis=1).reshape(model, tokens)
+    w_all = jnp.concatenate([w_q, w_kv])
+    w_all, mine_w = lax.optimization_barrier((w_all, mine_w))
+    w_all = lax.all_gather(w_all, "z", axis=0, tiled=False)
     halves = [unpack_weights(w, half_hidden, here) for w in (mine_w, swap(mine_w, "c"))]
     expand_t, reduce_t, out_t = zip(*halves)
-    att = lax.all_to_all(
-        out_all, ALL, split_axis=1, concat_axis=0, axis_index_groups=groups, tiled=True
-    )
 
     sides = (c, 1 - c)
     atts = [part(att, side, half_model, 0) for side in sides]
@@ -608,16 +619,16 @@
     normed2 = (unit2 * gain2 + bias2).astype(BF)
     total = middle + r_bias
     grad_normed = 0.0
-    acts, grads_a, grads_r, grads_e = [], [], [], []
+    acts, grad_pres, grads_e = [], [], []
     for side, w_e, w_r in zip(sides, expand_t, reduce_t):
         bias = part(e_bias, side, half_hidden, 1).reshape(-1)
         pre = mm("tm,hm->th", normed2, w_e) + bias
         act, pullback = jax.vjp(smooth_gelu, pre)
         act = act.astype(BF)
         total = total + mm("th,mh->tm", act, w_r)
-        grads_r.append(mm("tm,th->mh", cotangent, act).astype(BF))
+        acts.append(act)
         grad_pre = pullback(mm("tm,mh->th", cotangent, w_r))[0].astype(BF)
-        grads_a.append(mm("th,tm->hm", grad_pre, normed2).astype(BF))
+        grad_pres.append(grad_pre)
         grads_e.append(jnp.sum(grad_pre.astype(F32), axis=0).reshape(shards, half_hidden))
         grad_normed = grad_normed + mm("th,hm->tm", grad_pre, w_e)
     result = total.astype(BF)
@@ -631,9 +642,24 @@
     grad_out_b = jnp.sum(grad_branch.astype(F32), axis=0)
     grad_atts = [mm("mf,tm->ft", w, grad_branch).astype(BF) for w in out_t]
     grad_att = in_order(c, grad_atts[0], grad_atts[1], 0)
-    grad_heads = lax.all_to_all(
-        grad_att, ALL, split_axis=0, concat_axis=1, axis_index_groups=groups, tiled=True
-    )
+    grad_att, acts, grad_pres = lax.optimization_barrier((grad_att, acts, grad_pres))
+    by_head = grad_att.reshape(depth, heads, HEAD_DIM, tokens)
+
+    def to_heads(first, last):
+        got = lax.all_to_all(
+            by_head[:, first:last].reshape(-1, tokens),
+            ALL,
+            split_axis=0,
+            concat_axis=1,
+            axis_index_groups=groups,
+            tiled=True,
+        )
+        return got
+
+    grad_first = to_heads(0, 1)
+    grad_rest = to_heads(1, heads)
+    grads_r = [mm("tm,th->mh", cotangent, act).astype(BF) for act in acts]
+    grads_a = [mm("th,tm->hm", g, normed2).astype(BF) for g in grad_pres]
     grads_o = [mm("tm,ft->mf", grad_branch, a).astype(BF) for a in atts]
 
     packs = [
@@ -644,7 +670,7 @@
 
     dqs, dkvs = [], []
     for h in range(heads):
-        g_h = head(grad_heads, h)
+        g_h = head(grad_rest, h - 1) if h else grad_first
         if h:
             g_h, dqs[-1] = lax.optimization_barrier((g_h, dqs[-1]))
         if h > 1:
@@ -667,19 +693,31 @@
         sum_w, swap(sum_w, "c"), c, half_hidden, here
     )
 
-    dq = jnp.concatenate(dqs)
-    dkv = jnp.concatenate(dkvs, axis=1)
-    grad_w_q = mm("ft,tm->fm", dq, normed1)
-    grad_w_kv = mm("tf,tm->fm", dkv, normed1).reshape(heads, 2, HEAD_DIM, model)
-    grad_w = jnp.concatenate([grad_w_q, grad_w_kv.transpose(1, 0, 2, 3).reshape(2 * width, model)])
-    grad_q_b = jnp.sum(dq.astype(F32), axis=1)
-    grad_v_b = jnp.sum(dkv.astype(F32), axis=0).reshape(heads, 2, HEAD_DIM)[:, 1].reshape(width)
-    part_norm = mm("ft,fm->tm", dq, w_q) + mm("tf,fm->tm", dkv, w_kv)
-    grad_gain1 = jnp.sum(part_norm * unit1, axis=0)
-    grad_bias1 = jnp.sum(part_norm, axis=0)
-    grad_normed1 = lax.psum_scatter(
-        part_norm.astype(BF), ALL, scatter_dimension=0, axis_index_groups=groups, tiled=True
-    ).astype(F32)
+    unit_low = unit1.astype(BF)
+    w_own = jnp.concatenate([w_q, w_kv])
+    rest = (heads - 1) * 128 + width
+    both = [
+        jnp.concatenate([jnp.concatenate(dqs).T] + dkvs[:-1], axis=1),
+        dkvs[-1],
+    ]
+    grad_w = jnp.concatenate([mm("tf,tm->fm", d, normed1) for d in both])
+    grad_u = jnp.concatenate([mm("tf,tm->fm", d, unit_low) for d in both])
+    grad_s = jnp.concatenate([jnp.sum(d.astype(F32), axis=0) for d in both])
+    grad_gain1 = jnp.sum(w_own.astype(F32) * grad_u, axis=0)
+    grad_bias1 = jnp.sum(w_own.astype(F32) * grad_s[:, None], axis=0)
+    grad_q_b = grad_s[:width]
+    grad_v_b = grad_s[width:].reshape(heads, 2, HEAD_DIM)[:, 1].reshape(width)
+    grad_w_kv = grad_w[width:].reshape(heads, 2, HEAD_DIM, model)
+    grad_w = jnp.concatenate(
+        [grad_w[:width], grad_w_kv.transpose(1, 0, 2, 3).reshape(2 * width, model)]
+    )
+    grad_normed1 = 0.0
+    for d, w in zip(both, (w_all[:, :rest], w_all[:, rest:])):
+        got = lax.all_to_all(
+            d, ALL, split_axis=0, concat_axis=0, axis_index_groups=groups, tiled=True
+        ).reshape(depth, tokens, -1)
+        for k in range(depth):
+            grad_normed1 = grad_normed1 + mm("tf,fm->tm", got[k], w[k])
     unit_in, root_in = normalise(wide)
     grad_in = (grad_middle + normalise_back(grad_normed1, unit_in, root_in, gain1)).astype(BF)
 

time: 777 us -> 759 us (0.977)
  waiting for transfers between devices: 265 us -> 208 us
  starting transfers between devices: 44.6 us -> 70.6 us
  matrix products: 59.6 us -> 75.6 us
    all_gather x1, waiting for transfers between devices: 34 us -> 0.01 us  [on_device(): keys.append(lax.all_gather(own_pair, RING, axis=0, tiled=True))]
    all_to_all x1, waiting for transfers between devices: 0.01 us -> 33.9 us  [on_device(): lax.all_to_all(copies, RING, split_axis=0, concat_axis=0, tiled=True)]
    reduce_scatter x1, waiting for transfers between devices: 38.2 us -> 7.35 us  [on_device(): dkvs.append(lax.psum_scatter(dkv_h, RING, scatter_dimension=0, tiled=True))]
    ppermute x10, waiting for transfers between devices: 111 us -> 85.7 us  [swap(): return lax.ppermute(array, axis, [(0, 1), (1, 0)])]
    all_to_all x2 -> x6, starting transfers between devices: 12 us -> 33.6 us  [the longest x2 11.8 us: on_device(): lax.all_to_all(d, ALL, split_axis=0, concat_axis=0, axis_index_groups=gro...]
    dot_general x24 -> x32, matrix products: 59.6 us -> 75.6 us  [mm(): return jnp.einsum(spec, a, b, preferred_element_type=F32)]
    all_to_all x2 -> x6, waiting for transfers between devices: 16.8 us -> 15.2 us  [the longest x2 14.8 us: to_heads(): lax.all_to_all(by_head[:, first:last].reshape(-1, tokens), ALL, split_axi...]
  transfers between devices with their start and end apart: 24 -> 28, of which waited for: 12 -> 15; matrix products, arithmetic and copies ran while one was open for 15% -> 16% of each run, Pallas kernels for 37% -> 37%
where the time goes in v4:
time: 759 us; the launch traced here: 752 us
  Pallas kernels  280 us (37%)
  waiting for transfers between devices  208 us (27%)
  matrix products  75.6 us (10%)
  starting transfers between devices  70.6 us (9%)
  local copies, waits for them, and re-layouts  59.6 us (8%)
  other arithmetic  41.5 us (5%)
  between operations  16 us (2%)
    pallas_call x3, Pallas kernels, attend_back(): pl.pallas_call(functools.partial(backward_kernel, strips, unroll), grid=(...  170 us
    pallas_call x3, Pallas kernels, attend(): pl.pallas_call(functools.partial(forward_kernel, strips, unroll), grid=(s...  110 us
    ppermute x10, waiting for transfers between devices, swap(): return lax.ppermute(array, axis, [(0, 1), (1, 0)])  85.7 us
    dot_general x32, matrix products, mm(): return jnp.einsum(spec, a, b, preferred_element_type=F32)  75.6 us
    all_gather x1, waiting for transfers between devices, on_device(): keys = [lax.all_gather(pair(0), RING, axis=0, tiled=True)]  36.1 us
    all_to_all x1, waiting for transfers between devices, on_device(): lax.all_to_all(copies, RING, split_axis=0, concat_axis=0, tiled=True)  33.9 us
    all_to_all x1, waiting for transfers between devices, fetch_triple(): got = lax.all_to_all(slots, 'z', split_axis=0, concat_axis=0, tiled=True)  18.1 us
  transfers between devices with their start and end apart: 28, of which 15 were waited for; matrix products, arithmetic and copies ran while one was open for 16% of the time, Pallas kernels for 37%

profile of v4, /device:TPU:0, one launch (start us, length us, event | category | flops | bytes accessed | tf_op | source)
XLA Modules:
  0.0 751.8 jit_solution(15122295738035909421)
XLA Ops:
  7.9 6.1 concatenate.147
  15.1 3.0 collective-permute-start
  18.1 49.2 %collective-permute-done = bf16[304,384]{1,0:T(8,128)(2,1)S(1)} collective-permute-done((bf16[304,384]{1,0:T(8,128)(2,1)S(1)}, bf16[304,384]{1,0:T(8,128)(2,1)S(1)}, u32[]{:S(2)}, u32[]{:S(2)}) %collective-permute-start) | collective-permute-done | bytes 233504 | tf_op jit(solution)/shard_map/ppermute | solution.py:317
  68.9 5.8 all-to-all-start
  74.7 18.1 %all-to-all-done = bf16[4,208,384]{2,1,0:T(8,128)(2,1)S(1)} async-done(((bf16[4,208,384]{2,1,0:T(8,128)(2,1)}), bf16[4,208,384]{2,1,0:T(8,128)(2,1)S(1)}, u32[]{:S(2)}, u32[]{:S(2)}) %all-to-all-start) | async-done | bytes 639008 | tf_op jit(solution)/shard_map/all_to_all | solution.py:424
  95.2 2.6 convert_reduce_fusion
  99.3 2.6 fusion.2
  101.9 1.8 add_convert_fusion.1
  105.0 36.1 %all-gather.10.cloned.1.call-done.kv_ref = bf16[16384,128]{1,0:T(8,128)(2,1)} async-done(((bf16[2048,128]{1,0:T(8,128)(2,1)}), bf16[16384,128]{1,0:T(8,128)(2,1)}) %all-gather.10.cloned.1.call-update) | async-done | bytes 4194320 | tf_op jit(solution)/shard_map/all_gather | solution.py:573
  141.8 2.9 reshape.374
  144.6 2.5 dynamic-slice_reduce_fusion
  149.1 3.3 fusion.21
  153.3 36.7 %shard_map.262 = (f32[64,2048]{1,0:T(8,128)}, f32[8,2048]{1,0:T(8,128)}) custom-call(s32[2]{0:T(128)} %pad_add_fusion.r_ref, bf16[64,2048]{1,0:T(8,128)(2,1)} %get-tuple-element.171.q_ref, bf16[16384,128]{1,0:T(8,128)(2,1)} %all-gather.10.cloned.1.call-done.kv_ref), custom_call_target="tpu_custom_call" | custom-call | flops 15000000512 | bytes 8388608 | tf_op jit(solution)/shard_map/pallas_call | solution.py:139
  190.1 2.5 broadcast_in_dim.22
  192.6 4.6 all-to-all-start.1
  198.6 36.9 %shard_map.263 = (f32[64,2048]{1,0:T(8,128)}, f32[8,2048]{1,0:T(8,128)}) custom-call(s32[2]{0:T(128)} %pad_add_fusion.r_ref, bf16[64,2048]{1,0:T(8,128)(2,1)} %get-tuple-element.60.q_ref, bf16[16384,128]{1,0:T(8,128)(2,1)} %all-gather.12.cloned.1.call-done.kv_ref), custom_call_target="tpu_custom_call" | custom-call | flops 15000000512 | bytes 8388608 | tf_op jit(solution)/shard_map/pallas_call | solution.py:139
  237.5 33.9 %all-to-all-done.1 = bf16[8,2048,128]{2,1,0:T(8,128)(2,1)} async-done(((bf16[8,2048,128]{2,1,0:T(8,128)(2,1)}), bf16[8,2048,128]{2,1,0:T(8,128)(2,1)}, u32[]{:S(2)}, u32[]{:S(2)}) %all-to-all-start.1) | async-done | bytes 4194336 | tf_op jit(solution)/shard_map/all_to_all | solution.py:579
  271.4 3.8 all-to-all-start.2
  275.2 36.7 %shard_map.264 = (f32[64,2048]{1,0:T(8,128)}, f32[8,2048]{1,0:T(8,128)}) custom-call(s32[2]{0:T(128)} %pad_add_fusion.r_ref, bf16[64,2048]{1,0:T(8,128)(2,1)} %get-tuple-element.63.q_ref, bf16[16384,128]{1,0:T(8,128)(2,1)} %bitcast.16.kv_ref), custom_call_target="tpu_custom_call" | custom-call | flops 15000000512 | bytes 8388608 | tf_op jit(solution)/shard_map/pallas_call | solution.py:139
  315.5 6.6 all-to-all-start.3
  324.9 3.2 slice.392
  328.1 3.2 fusion.84
  335.6 2.0 multiply_convert_fusion.1
  337.7 4.2 convert_reduce_fusion.3
  345.1 2.0 multiply_convert_fusion
  347.2 2.4 fusion.83
  349.6 5.2 convert_reduce_fusion.2
  354.7 2.3 multiply_reduce_fusion
  357.0 1.9 fusion.82
  369.1 5.0 collective-permute-done.3
  374.1 3.6 add_convert_fusion
  379.4 6.6 all-to-all-start.5
  386.0 1.9 slice.499
  388.0 14.8 %all-to-all-done.5 = bf16[4,64,512]{2,1,0:T(8,128)(2,1)S(1)} async-done(((bf16[4,64,512]{2,1,0:T(8,128)(2,1)}), bf16[4,64,512]{2,1,0:T(8,128)(2,1)S(1)}, u32[]{:S(2)}, u32[]{:S(2)}) %all-to-all-start.5) | async-done | bytes 262176 | tf_op jit(solution)/shard_map/all_to_all | solution.py:649
  402.8 4.8 all-to-all-start.4
  408.2 56.6 %shard_map.265 = (bf16[64,2048]{1,0:T(8,128)(2,1)}, bf16[16384,128]{1,0:T(8,128)(2,1)}) custom-call(s32[2]{0:T(128)} %pad_add_fusion.r_ref, bf16[64,2048]{1,0:T(8,128)(2,1)} %get-tuple-element.171.q_ref, bf16[64,2048]{1,0:T(8,128)(2,1)} %bitcast.302, f32[64,2048]{1,0:T(8,128)} %get-tuple-element.65.out_ref, f32[8,2048]{1,0:T(8,128)} %get-tuple-element.72.lse_ref, ...), custom_call_target="tpu_custom_call" | custom-call | flops 24999999488 | bytes 12582912 | tf_op jit(solution)/shard_map/pallas_call | solution.py:257
  464.8 4.6 all-to-all-start.6
  470.8 56.6 %shard_map.266 = (bf16[64,2048]{1,0:T(8,128)(2,1)}, bf16[16384,128]{1,0:T(8,128)(2,1)}) custom-call(s32[2]{0:T(128)} %pad_add_fusion.r_ref, bf16[64,2048]{1,0:T(8,128)(2,1)} %get-tuple-element.60.q_ref, bf16[64,2048]{1,0:T(8,128)(2,1)} %bitcast.301, f32[64,2048]{1,0:T(8,128)} %get-tuple-element.66.out_ref, f32[8,2048]{1,0:T(8,128)} %get-tuple-element.76.lse_ref, ...), custom_call_target="tpu_custom_call" | custom-call | flops 24999999488 | bytes 12582912 | tf_op jit(solution)/shard_map/pallas_call | solution.py:257
  527.4 4.6 all-to-all-start.7
  532.8 56.7 %shard_map.267 = (bf16[64,2048]{1,0:T(8,128)(2,1)}, bf16[16384,128]{1,0:T(8,128)(2,1)}) custom-call(s32[2]{0:T(128)} %pad_add_fusion.r_ref, bf16[64,2048]{1,0:T(8,128)(2,1)} %get-tuple-element.63.q_ref, bf16[64,2048]{1,0:T(8,128)(2,1)} %bitcast.300, f32[64,2048]{1,0:T(8,128)} %get-tuple-element.64.out_ref, f32[8,2048]{1,0:T(8,128)} %get-tuple-element.82.lse_ref, ...), custom_call_target="tpu_custom_call" | custom-call | flops 24999999488 | bytes 12582912 | tf_op jit(solution)/shard_map/pallas_call | solution.py:257
  590.9 3.7 fusion.37
  594.6 2.3 add_convert_fusion.2
  596.9 3.5 reduce_sum.224
  601.6 3.5 reduce_sum.225
  611.0 6.9 all-to-all-start.8
  617.9 4.3 convolution_convert_fusion.4
  622.6 4.6 fusion.98
  627.2 23.2 %collective-permute-done.8 = bf16[432,768]{1,0:T(8,128)(2,1)} collective-permute-done((bf16[432,768]{1,0:T(8,128)(2,1)}, bf16[432,768]{1,0:T(8,128)(2,1)}, u32[]{:S(2)}, u32[]{:S(2)}) %collective-permute-start.8) | collective-permute-done | bytes 663584 | tf_op jit(solution)/shard_map/ppermute | solution.py:317
  659.6 2.6 reshape.428
  663.8 1.9 fusion.41
  665.7 7.3 reduce-scatter.5.cloned.1.call-done
  675.1 4.9 all-to-all-start.9
  680.0 2.7 fusion.99
  683.4 2.6 convolution_convert_fusion.9
  687.8 3.0 fusion.42
  690.8 3.0 fusion.43
  695.9 2.5 fusion.63
  698.3 2.4 fusion.64
  700.8 2.4 fusion.65
  703.2 2.4 fusion.66
  709.0 6.4 all-to-all-start.10
  715.4 6.4 fusion.81
  721.8 10.5 %all-to-all-done.10 = bf16[4,208,384]{2,1,0:T(8,128)(2,1)} async-done(((bf16[4,208,384]{2,1,0:T(8,128)(2,1)}), bf16[4,208,384]{2,1,0:T(8,128)(2,1)}, u32[]{:S(2)}, u32[]{:S(2)}) %all-to-all-start.10) | async-done | bytes 639008 | tf_op jit(solution)/shard_map/all_to_all | solution.py:465
  737.4 3.8 collective-permute-done.6
  (292 shorter events, 81.1 us)
Async XLA Ops:
  7.2 134.2 %copy-start = (bf16[768,384]{1,0:T(8,128)(2,1)S(1)}, bf16[768,384]{1,0:T(8,128)(2,1)}, u32[]{:S(2)}) copy-start(bf16[768,384]{1,0:T(8,128)(2,1)} %param.26) | copy-start | bytes 1769476
  7.2 87.9 %all-gather.8.cloned.1.call-start = ((), (), s32[]{:S(2)}) async-start(), calls=%async_computation.13 | async-start | bytes 3932160 | tf_op jit(solution)/shard_map/all_gather | solution.py:547
  15.1 52.2 %collective-permute-start = (bf16[304,384]{1,0:T(8,128)(2,1)S(1)}, bf16[304,384]{1,0:T(8,128)(2,1)S(1)}, u32[]{:S(2)}, u32[]{:S(2)}) collective-permute-start(bf16[304,384]{1,0:T(8,128)(2,1)S(1)} %get-tuple-element.193), channel_id=1, source_target_pairs={{0,4},{4,0},{1,5},{5,1},{2,6},{6,2},{3,7},{7,3},{8,12},{12,8},{9,1... | collective-permute-start | bytes 700424 | tf_op jit(solution)/shard_map/ppermute | solution.py:317
  68.9 24.0 %all-to-all-start = ((bf16[4,208,384]{2,1,0:T(8,128)(2,1)}), bf16[4,208,384]{2,1,0:T(8,128)(2,1)S(1)}, u32[]{:S(2)}, u32[]{:S(2)}) async-start(bf16[4,208,384]{2,1,0:T(8,128)(2,1)} %pad_maximum_fusion.12), calls=%async_computation | async-start | bytes 1277952 | tf_op jit(solution)/shard_map/all_to_all | solution.py:424
  74.7 66.4 %all-gather.10.cloned.1.call-start = ((), (), s32[]{:S(2)}) async-start(), calls=%async_computation.14 | async-start | bytes 4718592 | tf_op jit(solution)/shard_map/all_gather | solution.py:573
  93.0 1.9 collective-permute-start.1
  93.8 5.5 copy-start.28
  95.1 102.1 %copy-start.8 = (bf16[2,3,64,768]{3,2,0,1:T(8,128)(2,1)}, bf16[2,3,64,768]{3,2,0,1:T(8,128)(2,1)S(1)}, u32[]{:S(2)}) copy-start(bf16[2,3,64,768]{3,2,0,1:T(8,128)(2,1)S(1)} %copy.75) | copy-start | bytes 1769476
  95.2 3.0 copy-start.2
  101.9 1.8 copy-start.4
  105.0 85.1 %all-gather.12.cloned.1.call-start = ((), (), s32[]{:S(2)}) async-start(), calls=%async_computation.15 | async-start | bytes 4718592 | tf_op jit(solution)/shard_map/all_gather | solution.py:576
  141.1 171.8 %all-gather.14.cloned.1.call-start = ((), (), s32[]{:S(2)}) async-start(), calls=%async_computation.18 | async-start | bytes 5971968 | tf_op jit(solution)/shard_map/all_gather | solution.py:593
  141.6 6.5 copy-start.27
  153.3 36.8 %copy-start.13 = (bf16[2048,128]{1,0:T(8,128)(2,1)S(1)}, bf16[2048,128]{1,0:T(8,128)(2,1)}, u32[]{:S(2)}) copy-start(bf16[2048,128]{1,0:T(8,128)(2,1)} %get-tuple-element.163) | copy-start | bytes 1572868
  192.6 78.8 %all-to-all-start.1 = ((bf16[8,2048,128]{2,1,0:T(8,128)(2,1)}), bf16[8,2048,128]{2,1,0:T(8,128)(2,1)}, u32[]{:S(2)}, u32[]{:S(2)}) async-start(bf16[8,2048,128]{2,1,0:T(8,128)(2,1)} %broadcast_in_dim.22), calls=%async_computation.1 | async-start | bytes 8388608 | tf_op jit(solution)/shard_map/all_to_all | solution.py:579
  197.2 1.4 copy-start.23
  197.2 38.3 %copy-start.10 = (bf16[192,768]{1,0:T(8,128)(2,1)}, bf16[192,768]{1,0:T(8,128)(2,1)S(1)}, u32[]{:S(2)}) copy-start(bf16[192,768]{1,0:T(8,128)(2,1)S(1)} %slice.485) | copy-start | bytes 884740
  271.4 41.5 %all-to-all-start.2 = ((bf16[128,4,512]{2,0,1:T(8,128)(2,1)}), bf16[128,4,512]{2,0,1:T(8,128)(2,1)S(1)}, u32[]{:S(2)}, u32[]{:S(2)}) async-start(bf16[128,4,512]{2,0,1:T(8,128)(2,1)} %bitcast.232), calls=%async_computation.2 | async-start | bytes 1048576 | tf_op jit(solution)/shard_map/all_to_all | solution.py:597
  313.0 19.0 %collective-permute-start.2 = (bf16[8,432,768]{2,1,0:T(8,128)(2,1)}, bf16[8,432,768]{2,1,0:T(8,128)(2,1)}, u32[]{:S(2)}, u32[]{:S(2)}) collective-permute-start(bf16[8,432,768]{2,1,0:T(8,128)(2,1)} %bitcast.240), channel_id=1, source_target_pairs={{0,1},{1,0},{2,3},{3,2},{4,5},{5,4},{6,7},{7,6},{8,9},{9,8},{10,11... | collective-permute-start | bytes 15925256 | tf_op jit(solution)/shard_map/ppermute | solution.py:317
  315.5 15.8 %all-to-all-start.3 = ((bf16[64,4,512]{2,0,1:T(8,128)(2,1)}), bf16[64,4,512]{2,0,1:T(8,128)(2,1)S(1)}, u32[]{:S(2)}, u32[]{:S(2)}) async-start(bf16[64,4,512]{2,0,1:T(8,128)(2,1)} %bitcast.233), calls=%async_computation.3 | async-start | bytes 524288 | tf_op jit(solution)/shard_map/all_to_all | solution.py:597
  322.1 267.4 %reduce-scatter.3.cloned.1.call-start = ((), (), s32[]{:S(2)}) async-start(), calls=%async_computation.16 | async-start | bytes 5971968 | tf_op jit(solution)/shard_map/reduce_scatter | solution.py:669
  331.4 1.8 copy-start.3
  334.0 1.7 copy-start.12
  334.0 1.7 copy-start.32
  335.6 2.0 copy-start.16
  335.6 2.1 copy-start.17
  335.6 2.1 copy-start.22
  337.7 28.4 %copy-start.38 = (bf16[512,1536]{1,0:T(8,128)(2,1)}, bf16[512,1536]{1,0:T(8,128)(2,1)S(1)}, u32[]{:S(2)}) copy-start(bf16[512,1536]{1,0:T(8,128)(2,1)S(1)} %get-tuple-element.87) | copy-start | bytes 4718596
  343.3 1.8 copy-start.31
  347.2 16.1 %copy-start.36 = (bf16[512,1536]{1,0:T(8,128)(2,1)}, bf16[512,1536]{1,0:T(8,128)(2,1)S(1)}, u32[]{:S(2)}) copy-start(bf16[512,1536]{1,0:T(8,128)(2,1)S(1)} %get-tuple-element.89) | copy-start | bytes 4718596
  349.5 5.2 copy-start.18
  349.6 5.2 copy-start.20
  365.3 8.8 %collective-permute-start.3 = (bf16[8,432,768]{2,1,0:T(8,128)(2,1)S(1)}, bf16[8,432,768]{2,1,0:T(8,128)(2,1)S(1)}, u32[]{:S(2)}, u32[]{:S(2)}) collective-permute-start(bf16[8,432,768]{2,1,0:T(8,128)(2,1)S(1)} %pad_maximum_fusion), channel_id=1, source_target_pairs={{0,1},{1,0},{2,3},{3,2},{4,5},{5,4},{6,7},{7,6},{8,9},{9,8},{10,11... | collective-permute-start | bytes 15925256 | tf_op jit(solution)/shard_map/ppermute | solution.py:317
  379.4 23.3 %all-to-all-start.5 = ((bf16[4,64,512]{2,1,0:T(8,128)(2,1)}), bf16[4,64,512]{2,1,0:T(8,128)(2,1)S(1)}, u32[]{:S(2)}, u32[]{:S(2)}) async-start(bf16[4,64,512]{2,1,0:T(8,128)(2,1)} %slice_bitcast_fusion.17), calls=%async_computation.5 | async-start | bytes 524288 | tf_op jit(solution)/shard_map/all_to_all | solution.py:649
  402.8 62.1 %all-to-all-start.4 = ((bf16[4,128,512]{2,1,0:T(8,128)(2,1)}), bf16[4,128,512]{2,1,0:T(8,128)(2,1)S(1)}, u32[]{:S(2)}, u32[]{:S(2)}) async-start(bf16[4,128,512]{2,1,0:T(8,128)(2,1)} %bitcast.36), calls=%async_computation.4 | async-start | bytes 1048576 | tf_op jit(solution)/shard_map/all_to_all | solution.py:649
  464.8 62.5 %all-to-all-start.6 = ((bf16[8,2048,128]{2,1,0:T(8,128)(2,1)}), bf16[8,2048,128]{2,1,0:T(8,128)(2,1)}, u32[]{:S(2)}, u32[]{:S(2)}) async-start(bf16[8,2048,128]{2,1,0:T(8,128)(2,1)} %bitcast.251), calls=%async_computation.6 | async-start | bytes 8388608 | tf_op jit(solution)/shard_map/all_to_all | solution.py:684
  469.5 194.3 %all-gather.16.cloned.1.call-start = ((), (), s32[]{:S(2)}) async-start(), calls=%async_computation.19 | async-start | bytes 4423680 | tf_op jit(solution)/shard_map/all_gather | solution.py:608
  527.4 62.1 %all-to-all-start.7 = ((bf16[8,2048,128]{2,1,0:T(8,128)(2,1)}), bf16[8,2048,128]{2,1,0:T(8,128)(2,1)}, u32[]{:S(2)}, u32[]{:S(2)}) async-start(bf16[8,2048,128]{2,1,0:T(8,128)(2,1)} %bitcast.252), calls=%async_computation.8 | async-start | bytes 8388608 | tf_op jit(solution)/shard_map/all_to_all | solution.py:684
  532.0 141.1 %reduce-scatter.5.cloned.1.call-start = ((), (), s32[]{:S(2)}) async-start(), calls=%async_computation.17 | async-start | bytes 4718592 | tf_op jit(solution)/shard_map/reduce_scatter | solution.py:682
  589.5 1.0 copy-start.34
  590.9 3.7 copy-start.19
  590.9 3.7 copy-start.21
  590.9 3.7 copy-start.37
  596.9 3.7 copy-start.24
  596.9 3.7 copy-start.25
  596.9 3.7 copy-start.26
  606.1 44.3 %collective-permute-start.8 = (bf16[432,768]{1,0:T(8,128)(2,1)}, bf16[432,768]{1,0:T(8,128)(2,1)}, u32[]{:S(2)}, u32[]{:S(2)}) collective-permute-start(bf16[432,768]{1,0:T(8,128)(2,1)} %bitcast.54), channel_id=1, source_target_pairs={{0,2},{2,0},{1,3},{3,1},{4,6},{6,4},{5,7},{7,5},{8,10},{10,8},{9,1... | collective-permute-start | bytes 1990664 | tf_op jit(solution)/shard_map/ppermute | solution.py:317
  611.0 52.8 %all-to-all-start.8 = ((bf16[4,512,448]{1,2,0:T(8,128)(2,1)}), bf16[4,512,448]{1,2,0:T(8,128)(2,1)}, u32[]{:S(2)}, u32[]{:S(2)}) async-start(bf16[4,512,448]{1,2,0:T(8,128)(2,1)} %bitcast.229), calls=%async_computation.9 | async-start | bytes 3670016 | tf_op jit(solution)/shard_map/all_to_all | solution.py:716
  651.9 2.3 collective-permute-start.9
  673.0 7.0 copy-start.5
  675.1 20.8 %all-to-all-start.9 = ((bf16[4,512,128]{2,1,0:T(8,128)(2,1)}), bf16[4,512,128]{2,1,0:T(8,128)(2,1)S(1)}, u32[]{:S(2)}, u32[]{:S(2)}) async-start(bf16[4,512,128]{2,1,0:T(8,128)(2,1)} %bitcast.234), calls=%async_computation.11 | async-start | bytes 1048576 | tf_op jit(solution)/shard_map/all_to_all | solution.py:716
  680.0 2.7 copy-start.9
  680.0 2.7 copy-start.11
  680.0 2.7 copy-start.15
  683.4 2.6 copy-start.14
  687.1 6.7 collective-permute-start.4
  693.9 12.8 %collective-permute-start.5 = (bf16[608,384]{1,0:T(8,128)(2,1)S(1)}, bf16[608,384]{1,0:T(8,128)(2,1)}, u32[]{:S(2)}, u32[]{:S(2)}) collective-permute-start(bf16[608,384]{1,0:T(8,128)(2,1)S(1)} %add_convert_fusion.6), channel_id=1, source_target_pairs={{0,2},{2,0},{1,3},{3,1},{4,6},{6,4},{5,7},{7,5},{8,10},{10,8},{9,1... | collective-permute-start | bytes 1400840 | tf_op jit(solution)/shard_map/ppermute | solution.py:317
  707.9 7.4 copy-start.29
  709.0 23.3 %all-to-all-start.10 = ((bf16[4,208,384]{2,1,0:T(8,128)(2,1)}), bf16[4,208,384]{2,1,0:T(8,128)(2,1)}, u32[]{:S(2)}, u32[]{:S(2)}) async-start(bf16[4,208,384]{2,1,0:T(8,128)(2,1)} %fusion.44), calls=%async_computation.12 | async-start | bytes 1277952 | tf_op jit(solution)/shard_map/all_to_all | solution.py:465
  721.8 14.2 %copy-start.6 = (f32[512,768]{1,0:T(8,128)S(1)}, f32[512,768]{1,0:T(8,128)}, u32[]{:S(2)}) copy-start(f32[512,768]{1,0:T(8,128)} %get-tuple-element.150) | copy-start | bytes 4718596
  732.3 3.7 copy-start.7
  734.5 6.7 collective-permute-start.6
  736.0 8.5 %copy-start.1 = (bf16[768,384]{1,0:T(8,128)(2,1)S(1)}, bf16[768,384]{1,0:T(8,128)(2,1)}, u32[]{:S(2)}) copy-start(bf16[768,384]{1,0:T(8,128)(2,1)} %param.26) | copy-start | bytes 1769476
  741.9 1.5 collective-permute-start.7
  (4 other events, 3.4 us)
Sparse Core Ops, SparseCore 0:
  9.6 74.7 all-gather.7
  105.1 35.9 all-gather.9
  143.6 36.7 all-gather.11
  190.2 116.7 all-gather.13
  377.9 127.4 reduce-scatter.2
  507.5 68.5 all-gather.15
  589.7 83.2 reduce-scatter.4

commit v5 on v4

--- a/solution.py
+++ b/solution.py
@@ -133,7 +133,7 @@
     lse_ref[...] = jnp.broadcast_to(top_s[...] + jnp.log2(mass), lse_ref.shape)
 
 
-def attend(r, query, kv, unroll=4):
+def attend(r, query, kv, column, unroll=4):
     keys, rows = kv.shape[0], query.shape[1]
     strips = rows // CH
     return pl.pallas_call(
@@ -142,7 +142,7 @@
         in_specs=[
             pl.BlockSpec(memory_space=pltpu.SMEM),
             pl.BlockSpec((64, CH), lambda i: (0, i)),
-            pl.BlockSpec((keys, 128), lambda i: (0, 0)),
+            pl.BlockSpec((keys, 128), lambda i: (0, column)),
         ],
         out_specs=[
             pl.BlockSpec((64, CH), lambda i: (0, i)),
@@ -249,7 +249,7 @@
         lax.fori_loop(0, dkv.shape[0] // CH, write, 0)
 
 
-def attend_back(r, query, grad, out, lse, kv, unroll=2):
+def attend_back(r, query, grad, out, lse, kv, column, unroll=2):
     keys, rows = kv.shape[0], query.shape[1]
     strips = rows // CH
     strip = pl.BlockSpec((64, CH), lambda i: (0, i))
@@ -263,7 +263,7 @@
             strip,
             strip,
             pl.BlockSpec((8, CH), lambda i: (0, i)),
-            whole,
+            pl.BlockSpec((keys, 128), lambda i: (0, column)),
         ],
         out_specs=[strip, whole],
         out_shape=[
@@ -405,6 +405,21 @@
     w = in_order(c, reduce_of(own), reduce_of(other), 2).reshape(here, -1)
     o = in_order(c, out_of(own), out_of(other), 1)
     return e.T.astype(F32), w.T.astype(F32), o.T.astype(F32)
+
+
+def sum_pieces(parts):
+    return jnp.sum(parts.astype(F32), axis=0).astype(BF)
+
+
+def exchange(values, z, groups):
+    depth = len(groups[0])
+    blocks = values.reshape(depth, -1, values.shape[1])
+    got = [lax.dynamic_index_in_dim(blocks, z, 0, keepdims=False)]
+    for k in range(1, depth):
+        sent = lax.dynamic_index_in_dim(blocks, (z + k) % depth, 0, keepdims=False)
+        pairs = [(g[i], g[(i + k) % depth]) for g in groups for i in range(depth)]
+        got.append(lax.ppermute(sent, ALL, pairs))
+    return got
 
 
 def fetch_triple(triple_weight, small, at):
@@ -571,13 +586,8 @@
         return kv[:, h * 128 : (h + 1) * 128]
 
     keys = [lax.all_gather(pair(0), RING, axis=0, tiled=True)]
-    for h in range(1, heads - 1):
-        own_pair, keys[-1] = lax.optimization_barrier((pair(h), keys[-1]))
-        keys.append(lax.all_gather(own_pair, RING, axis=0, tiled=True))
-    copies = jnp.broadcast_to(pair(heads - 1), (ring,) + pair(0).shape)
-    keys.append(
-        lax.all_to_all(copies, RING, split_axis=0, concat_axis=0, tiled=True).reshape(-1, 128)
-    )
+    rest_pairs, keys[0] = lax.optimization_barrier((kv[:, 128:], keys[0]))
+    keys.append(lax.all_gather(rest_pairs, RING, axis=0, tiled=True))
 
     own_w = pack_weights(expand_weight, reduce_weight, out_weight, c)
     outs, lses = [], []
@@ -585,7 +595,7 @@
         q_h = head(q_t, h)
         if h:
             q_h, outs[-1] = lax.optimization_barrier((q_h, outs[-1]))
-        out_h, lse_h = attend(info, q_h, keys[h])
+        out_h, lse_h = attend(info, q_h, keys[min(h, 1)], max(h - 1, 0))
         outs.append(out_h)
         lses.append(lse_h)
         if h == 0:
@@ -603,8 +613,10 @@
     late = outs[-1].astype(BF)
     mine_w, late, early = lax.optimization_barrier((mine_w, late, early))
     att = jnp.concatenate([early, to_tokens([late])], axis=1).reshape(model, tokens)
-    w_all = jnp.concatenate([w_q, w_kv])
-    w_all, mine_w = lax.optimization_barrier((w_all, mine_w))
+    w_own = jnp.concatenate(
+        [w_q[:128], w_kv[:128], w_q[128:], w_kv[128:256], w_kv[256:]]
+    )
+    w_all, mine_w = lax.optimization_barrier((w_own, mine_w))
     w_all = lax.all_gather(w_all, "z", axis=0, tiled=False)
     halves = [unpack_weights(w, half_hidden, here) for w in (mine_w, swap(mine_w, "c"))]
     expand_t, reduce_t, out_t = zip(*halves)
@@ -673,51 +685,58 @@
         g_h = head(grad_rest, h - 1) if h else grad_first
         if h:
             g_h, dqs[-1] = lax.optimization_barrier((g_h, dqs[-1]))
-        if h > 1:
-            g_h, dkvs[h - 2] = lax.optimization_barrier((g_h, dkvs[h - 2]))
-        dq_h, dkv_h = attend_back(info, head(q_t, h), g_h, outs[h], lses[h], keys[h])
+        if h == heads - 1:
+            first = sum_pieces(dkvs[0])
+            pieces = [jnp.concatenate([jnp.concatenate(dqs).T, first], axis=1)]
+            g_h, sum_w, first_piece = lax.optimization_barrier((g_h, sum_w, pieces[0]))
+            pieces[0] = first_piece
+            got = [exchange(first_piece, z, groups)]
+            swapped = swap(sum_w, "y")
+        dq_h, dkv_h = attend_back(
+            info, head(q_t, h), g_h, outs[h], lses[h], keys[min(h, 1)], max(h - 1, 0)
+        )
         dqs.append(dq_h)
         if h == heads - 1:
-            dkv_h, sum_w, dkvs[-1] = lax.optimization_barrier((dkv_h, sum_w, dkvs[-1]))
+            dkv_h, swapped, dkvs[-1], got[0] = lax.optimization_barrier(
+                (dkv_h, swapped, dkvs[-1], got[0])
+            )
             dkvs.append(lax.psum_scatter(dkv_h, RING, scatter_dimension=0, tiled=True))
         else:
-            pieces = lax.all_to_all(
+            parts = lax.all_to_all(
                 dkv_h.reshape(ring, depth * tokens, 128), RING, split_axis=0, concat_axis=0, tiled=True
             )
-            dkvs.append(pieces)
-
-    for h in range(heads - 1):
-        dkvs[h] = jnp.sum(dkvs[h].astype(F32), axis=0).astype(BF)
-    sum_w = swap_sum(sum_w, "y").astype(BF)
+            dkvs.append(parts)
+
+    sum_w = (sum_w.astype(F32) + swapped.astype(F32)).astype(BF)
     grad_expand_w, grad_reduce_w, grad_out_w = unpack_grads(
         sum_w, swap(sum_w, "c"), c, half_hidden, here
     )
 
     unit_low = unit1.astype(BF)
-    w_own = jnp.concatenate([w_q, w_kv])
-    rest = (heads - 1) * 128 + width
-    both = [
-        jnp.concatenate([jnp.concatenate(dqs).T] + dkvs[:-1], axis=1),
-        dkvs[-1],
-    ]
-    grad_w = jnp.concatenate([mm("tf,tm->fm", d, normed1) for d in both])
-    grad_u = jnp.concatenate([mm("tf,tm->fm", d, unit_low) for d in both])
-    grad_s = jnp.concatenate([jnp.sum(d.astype(F32), axis=0) for d in both])
+    pieces.append(jnp.concatenate([dqs[-1].T, sum_pieces(dkvs[1])], axis=1))
+    pieces.append(dkvs[2])
+    got += [exchange(d, z, groups) for d in pieces[1:]]
+    grad_w = jnp.concatenate([mm("tf,tm->fm", d, normed1) for d in pieces])
+    grad_u = jnp.concatenate([mm("tf,tm->fm", d, unit_low) for d in pieces])
+    grad_s = jnp.concatenate([jnp.sum(d.astype(F32), axis=0) for d in pieces])
     grad_gain1 = jnp.sum(w_own.astype(F32) * grad_u, axis=0)
     grad_bias1 = jnp.sum(w_own.astype(F32) * grad_s[:, None], axis=0)
-    grad_q_b = grad_s[:width]
-    grad_v_b = grad_s[width:].reshape(heads, 2, HEAD_DIM)[:, 1].reshape(width)
-    grad_w_kv = grad_w[width:].reshape(heads, 2, HEAD_DIM, model)
-    grad_w = jnp.concatenate(
-        [grad_w[:width], grad_w_kv.transpose(1, 0, 2, 3).reshape(2 * width, model)]
-    )
+
+    def of_kind(values, kind):
+        starts = ((0, 64, 256), (128, 320, 448), (192, 384, 512))[kind]
+        return jnp.concatenate([values[at : at + HEAD_DIM] for at in starts])
+
+    grad_q_b = of_kind(grad_s, 0)
+    grad_v_b = of_kind(grad_s, 2)
+    grad_w = jnp.concatenate([of_kind(grad_w, kind) for kind in range(3)])
     grad_normed1 = 0.0
-    for d, w in zip(both, (w_all[:, :rest], w_all[:, rest:])):
-        got = lax.all_to_all(
-            d, ALL, split_axis=0, concat_axis=0, axis_index_groups=groups, tiled=True
-        ).reshape(depth, tokens, -1)
-        for k in range(depth):
-            grad_normed1 = grad_normed1 + mm("tf,fm->tm", got[k], w[k])
+    at_row = 0
+    for blocks_got in got:
+        size = blocks_got[0].shape[1]
+        for k, block in enumerate(blocks_got):
+            w = lax.dynamic_index_in_dim(w_all, (z - k) % depth, 0, keepdims=False)
+            grad_normed1 = grad_normed1 + mm("tf,fm->tm", block, w[at_row : at_row + size])
+        at_row += size
     unit_in, root_in = normalise(wide)
     grad_in = (grad_middle + normalise_back(grad_normed1, unit_in, root_in, gain1)).astype(BF)
 

time: 759 us -> 748 us (0.986)
  waiting for transfers between devices: 208 us -> 171 us
  local copies, waits for them, and re-layouts: 59.6 us -> 81.1 us
    all_to_all x3 -> x0, waiting for transfers between devices: 34.3 us -> none  [the longest x1 33.9 us: on_device(): lax.all_to_all(copies, RING, split_axis=0, concat_axis=0, tiled=True)]
    ppermute x0 -> x9, starting transfers between devices: none -> 20.5 us  [exchange(): got.append(lax.ppermute(sent, ALL, pairs))]
    ppermute x10, waiting for transfers between devices: 85.7 us -> 66.6 us  [swap(): return lax.ppermute(array, axis, [(0, 1), (1, 0)])]
    all_to_all x3 -> x0, starting transfers between devices: 16.4 us -> none  [the longest x2 11.8 us: on_device(): lax.all_to_all(d, ALL, split_axis=0, concat_axis=0, axis_index_groups=gro...]
    all_gather x1, waiting for transfers between devices: 0.02 us -> 15.9 us  [on_device(): mine_w = lax.all_gather(own_w, WEIGHT_AXES, axis=0, tiled=False)]
    unnamed x81 -> x141, local copies, waits for them, and re-layouts: 3.5 us -> 14.8 us
    all_gather x1, waiting for transfers between devices: 0.01 us -> 7.84 us  [on_device(): keys.append(lax.all_gather(rest_pairs, RING, axis=0, tiled=True))]
    dot_general x32 -> x38, matrix products: 75.6 us -> 80.9 us  [mm(): return jnp.einsum(spec, a, b, preferred_element_type=F32)]
  transfers between devices with their start and end apart: 28 -> 34, of which waited for: 15 -> 14; matrix products, arithmetic and copies ran while one was open for 16% -> 18% of each run, Pallas kernels for 37% -> 38%
where the time goes in v5:
time: 748 us; the launch traced here: 741 us
  Pallas kernels  280 us (37%)
  waiting for transfers between devices  171 us (23%)
  local copies, waits for them, and re-layouts  81.1 us (11%)
  matrix products  80.9 us (11%)
  starting transfers between devices  69.5 us (9%)
  other arithmetic  41.2 us (6%)
  between operations  16.3 us (2%)
    pallas_call x3, Pallas kernels, attend_back(): pl.pallas_call(functools.partial(backward_kernel, strips, unroll), grid=(...  170 us
    pallas_call x3, Pallas kernels, attend(): pl.pallas_call(functools.partial(forward_kernel, strips, unroll), grid=(s...  110 us
    dot_general x38, matrix products, mm(): return jnp.einsum(spec, a, b, preferred_element_type=F32)  80.9 us
    ppermute x10, waiting for transfers between devices, swap(): return lax.ppermute(array, axis, [(0, 1), (1, 0)])  66.6 us
    all_gather x1, waiting for transfers between devices, on_device(): keys = [lax.all_gather(pair(0), RING, axis=0, tiled=True)]  33.8 us
    ppermute x9, starting transfers between devices, exchange(): got.append(lax.ppermute(sent, ALL, pairs))  20.5 us
    all_to_all x1, waiting for transfers between devices, fetch_triple(): got = lax.all_to_all(slots, 'z', split_axis=0, concat_axis=0, tiled=True)  18.1 us
    all_gather x1, waiting for transfers between devices, on_device(): mine_w = lax.all_gather(own_w, WEIGHT_AXES, axis=0, tiled=False)  15.9 us
  transfers between devices with their start and end apart: 34, of which 14 were waited for; matrix products, arithmetic and copies ran while one was open for 18% of the time, Pallas kernels for 38%

profile of v5, /device:TPU:0, one launch (start us, length us, event | category | flops | bytes accessed | tf_op | source)
XLA Modules:
  0.0 740.9 jit_solution(15497727325701426191)
XLA Ops:
  7.9 6.1 concatenate.153
  15.1 3.0 collective-permute-start
  18.1 49.2 %collective-permute-done = bf16[304,384]{1,0:T(8,128)(2,1)S(1)} collective-permute-done((bf16[304,384]{1,0:T(8,128)(2,1)S(1)}, bf16[304,384]{1,0:T(8,128)(2,1)S(1)}, u32[]{:S(2)}, u32[]{:S(2)}) %collective-permute-start) | collective-permute-done | bytes 233504 | tf_op jit(solution)/shard_map/ppermute | solution.py:317
  68.9 5.8 all-to-all-start
  74.7 18.1 %all-to-all-done = bf16[4,208,384]{2,1,0:T(8,128)(2,1)S(1)} async-done(((bf16[4,208,384]{2,1,0:T(8,128)(2,1)}), bf16[4,208,384]{2,1,0:T(8,128)(2,1)S(1)}, u32[]{:S(2)}, u32[]{:S(2)}) %all-to-all-start) | async-done | bytes 639008 | tf_op jit(solution)/shard_map/all_to_all | solution.py:439
  95.2 2.5 convert_reduce_fusion
  99.1 2.6 fusion.2
  105.7 2.3 slice.537
  107.9 33.8 %all-gather.10.cloned.1.call-done.kv_ref = bf16[16384,128]{1,0:T(8,128)(2,1)} async-done(((bf16[2048,128]{1,0:T(8,128)(2,1)}), bf16[16384,128]{1,0:T(8,128)(2,1)}) %all-gather.10.cloned.1.call-update) | async-done | bytes 4194320 | tf_op jit(solution)/shard_map/all_gather | solution.py:588
  142.4 2.9 reshape.354
  145.3 2.5 dynamic-slice_reduce_fusion
  149.8 3.4 fusion.21
  154.1 36.7 %shard_map.262 = (f32[64,2048]{1,0:T(8,128)}, f32[8,2048]{1,0:T(8,128)}) custom-call(s32[2]{0:T(128)} %pad_add_fusion.r_ref, bf16[64,2048]{1,0:T(8,128)(2,1)} %get-tuple-element.259.q_ref, bf16[16384,128]{1,0:T(8,128)(2,1)} %all-gather.10.cloned.1.call-done.kv_ref), custom_call_target="tpu_custom_call" | custom-call | flops 15000000512 | bytes 8388608 | tf_op jit(solution)/shard_map/pallas_call | solution.py:139
  190.8 7.8 %all-gather.12.cloned.1.call-done.kv_ref = bf16[16384,256]{1,0:T(8,128)(2,1)} async-done(((bf16[2048,256]{1,0:T(8,128)(2,1)}), bf16[16384,256]{1,0:T(8,128)(2,1)}) %all-gather.12.cloned.1.call-update) | async-done | bytes 8388624 | tf_op jit(solution)/shard_map/all_gather | solution.py:590
  198.8 37.0 %shard_map.263 = (f32[64,2048]{1,0:T(8,128)}, f32[8,2048]{1,0:T(8,128)}) custom-call(s32[2]{0:T(128)} %pad_add_fusion.r_ref, bf16[64,2048]{1,0:T(8,128)(2,1)} %get-tuple-element.65.q_ref, bf16[16384,256]{1,0:T(8,128)(2,1)} %all-gather.12.cloned.1.call-done.kv_ref), custom_call_target="tpu_custom_call" | custom-call | flops 15000000512 | bytes 8388608 | tf_op jit(solution)/shard_map/pallas_call | solution.py:139
  237.9 5.6 all-to-all-start.1
  243.5 36.7 %shard_map.264 = (f32[64,2048]{1,0:T(8,128)}, f32[8,2048]{1,0:T(8,128)}) custom-call(s32[2]{0:T(128)} %pad_add_fusion.r_ref, bf16[64,2048]{1,0:T(8,128)(2,1)} %get-tuple-element.68.q_ref, bf16[16384,256]{1,0:T(8,128)(2,1)} %all-gather.12.cloned.1.call-done.kv_ref), custom_call_target="tpu_custom_call" | custom-call | flops 15000000512 | bytes 8388608 | tf_op jit(solution)/shard_map/pallas_call | solution.py:139
  281.3 15.9 %all-gather.14.cloned.1.call-done = bf16[3456,768]{1,0:T(8,128)(2,1)} async-done(((bf16[432,768]{1,0:T(8,128)(2,1)}), bf16[3456,768]{1,0:T(8,128)(2,1)}) %all-gather.14.cloned.1.call-update) | async-done | bytes 5308432 | tf_op jit(solution)/shard_map/all_gather | solution.py:603
  298.2 4.6 all-to-all-start.2
  305.3 3.3 slice.438
  308.7 3.2 fusion.104
  318.3 4.8 convert_reduce_fusion.2
  326.4 2.0 multiply_convert_fusion
  328.4 2.4 fusion.103
  330.8 5.2 convert_reduce_fusion.1
  336.0 2.3 multiply_reduce_fusion
  338.2 2.4 fusion.102
  350.9 5.0 collective-permute-done.3
  355.8 3.7 add_convert_fusion
  361.4 6.6 all-to-all-start.4
  370.3 14.4 %all-to-all-done.4 = bf16[4,64,512]{2,1,0:T(8,128)(2,1)S(1)} async-done(((bf16[4,64,512]{2,1,0:T(8,128)(2,1)}), bf16[4,64,512]{2,1,0:T(8,128)(2,1)S(1)}, u32[]{:S(2)}, u32[]{:S(2)}) %all-to-all-start.4) | async-done | bytes 262176 | tf_op jit(solution)/shard_map/all_to_all | solution.py:661
  384.7 4.8 all-to-all-start.3
  390.2 56.6 %shard_map.265 = (bf16[64,2048]{1,0:T(8,128)(2,1)}, bf16[16384,128]{1,0:T(8,128)(2,1)}) custom-call(s32[2]{0:T(128)} %pad_add_fusion.r_ref, bf16[64,2048]{1,0:T(8,128)(2,1)} %get-tuple-element.259.q_ref, bf16[64,2048]{1,0:T(8,128)(2,1)} %bitcast.339, f32[64,2048]{1,0:T(8,128)} %get-tuple-element.70.out_ref, f32[8,2048]{1,0:T(8,128)} %get-tuple-element.77.lse_ref, ...), custom_call_target="tpu_custom_call" | custom-call | flops 24999999488 | bytes 12582912 | tf_op jit(solution)/shard_map/pallas_call | solution.py:257
  446.9 4.6 all-to-all-start.5
  455.0 3.7 fusion.37
  458.7 2.3 add_convert_fusion.2
  462.5 56.6 %shard_map.266 = (bf16[64,2048]{1,0:T(8,128)(2,1)}, bf16[16384,128]{1,0:T(8,128)(2,1)}) custom-call(s32[2]{0:T(128)} %pad_add_fusion.r_ref, bf16[64,2048]{1,0:T(8,128)(2,1)} %get-tuple-element.65.q_ref, bf16[64,2048]{1,0:T(8,128)(2,1)} %bitcast.338, f32[64,2048]{1,0:T(8,128)} %get-tuple-element.71.out_ref, f32[8,2048]{1,0:T(8,128)} %get-tuple-element.80.lse_ref, ...), custom_call_target="tpu_custom_call" | custom-call | flops 24999999488 | bytes 12582912 | tf_op jit(solution)/shard_map/pallas_call | solution.py:257
  519.1 4.7 all-to-all-start.6
  523.9 3.1 reduce_sum.233
  529.7 5.8 collective-permute-start.5
  535.4 2.5 collective-permute-start.6
  538.8 57.0 %shard_map.267 = (bf16[64,2048]{1,0:T(8,128)(2,1)}, bf16[16384,128]{1,0:T(8,128)(2,1)}) custom-call(s32[2]{0:T(128)} %pad_add_fusion.r_ref, bf16[64,2048]{1,0:T(8,128)(2,1)} %get-tuple-element.68.q_ref, bf16[64,2048]{1,0:T(8,128)(2,1)} %bitcast.337, f32[64,2048]{1,0:T(8,128)} %get-tuple-element.69.out_ref, f32[8,2048]{1,0:T(8,128)} %get-tuple-element.91.lse_ref, ...), custom_call_target="tpu_custom_call" | custom-call | flops 24999999488 | bytes 12582912 | tf_op jit(solution)/shard_map/pallas_call | solution.py:257
  601.0 2.1 add_convert_fusion.4
  606.2 3.6 reduce_sum.234
  611.3 2.4 constant_dynamic-slice_fusion.9
  614.4 3.2 collective-permute-start.8
  624.5 2.8 fusion.62
  627.3 2.5 fusion.53
  631.4 2.6 fusion.51
  634.0 2.5 fusion.50
  647.2 2.6 reshape.407
  652.3 4.3 reduce-scatter.5.cloned.1.call-done
  658.1 2.7 convolution_convert_fusion.10
  666.8 2.7 fusion.121
  674.5 2.5 collective-permute-start.11
  677.0 2.4 collective-permute-start.12
  681.1 2.4 fusion.70
  686.2 2.4 fusion.69
  688.8 2.5 fusion.68
  691.3 7.1 collective-permute-done.15
  699.6 4.7 all-to-all-start.7
  704.4 8.0 %fusion.101 = (f32[512]{0:T(512)S(1)}, f32[512]{0:T(512)S(1)}, f32[512,768]{1,0:T(8,128)}) fusion(f32[512]{0:T(512)S(1)} %add_rsqrt_fusion.1, f32[512]{0:T(512)S(1)} %broadcast_multiply_fusion.3, bf16[512,768]{1,0:T(8,128)(2,1)S(1)} %copy-done.3, f32[768]{0:T(1024)S(1)} %copy-done.43, bf16[512,128]{1,0:T(8,128)(2,1)S(1)} %collective-permute-done.13, ...), kind=kOutput, calls=%fused_computation.281 | convolution fusion | flops 107740160 | bytes 19999752 | tf_op jit(solution)/shard_map/tf,fm->tm/dot_general | solution.py:313
  712.4 9.1 %all-to-all-done.7 = bf16[4,208,384]{2,1,0:T(8,128)(2,1)} async-done(((bf16[4,208,384]{2,1,0:T(8,128)(2,1)}), bf16[4,208,384]{2,1,0:T(8,128)(2,1)}, u32[]{:S(2)}, u32[]{:S(2)}) %all-to-all-start.7) | async-done | bytes 639008 | tf_op jit(solution)/shard_map/all_to_all | solution.py:480
  726.5 3.8 collective-permute-done.16
  (375 shorter events, 112.3 us)
Async XLA Ops:
  7.2 134.8 %copy-start = (bf16[768,384]{1,0:T(8,128)(2,1)S(1)}, bf16[768,384]{1,0:T(8,128)(2,1)}, u32[]{:S(2)}) copy-start(bf16[768,384]{1,0:T(8,128)(2,1)} %param.26) | copy-start | bytes 1769476
  7.2 87.9 %all-gather.8.cloned.1.call-start = ((), (), s32[]{:S(2)}) async-start(), calls=%async_computation.10 | async-start | bytes 3932160 | tf_op jit(solution)/shard_map/all_gather | solution.py:562
  15.1 52.2 %collective-permute-start = (bf16[304,384]{1,0:T(8,128)(2,1)S(1)}, bf16[304,384]{1,0:T(8,128)(2,1)S(1)}, u32[]{:S(2)}, u32[]{:S(2)}) collective-permute-start(bf16[304,384]{1,0:T(8,128)(2,1)S(1)} %get-tuple-element.289), channel_id=1, source_target_pairs={{0,4},{4,0},{1,5},{5,1},{2,6},{6,2},{3,7},{7,3},{8,12},{12,8},{9,1... | collective-permute-start | bytes 700424 | tf_op jit(solution)/shard_map/ppermute | solution.py:317
  68.9 24.0 %all-to-all-start = ((bf16[4,208,384]{2,1,0:T(8,128)(2,1)}), bf16[4,208,384]{2,1,0:T(8,128)(2,1)S(1)}, u32[]{:S(2)}, u32[]{:S(2)}) async-start(bf16[4,208,384]{2,1,0:T(8,128)(2,1)} %pad_maximum_fusion.12), calls=%async_computation | async-start | bytes 1277952 | tf_op jit(solution)/shard_map/all_to_all | solution.py:439
  74.7 67.1 %all-gather.10.cloned.1.call-start = ((), (), s32[]{:S(2)}) async-start(), calls=%async_computation.11 | async-start | bytes 4718592 | tf_op jit(solution)/shard_map/all_gather | solution.py:588
  93.0 1.9 collective-permute-start.1
  93.8 5.3 copy-start.42
  105.6 93.0 %all-gather.12.cloned.1.call-start = ((), (), s32[]{:S(2)}) async-start(), calls=%async_computation.12 | async-start | bytes 9437184 | tf_op jit(solution)/shard_map/all_gather | solution.py:590
  141.8 155.5 %all-gather.14.cloned.1.call-start = ((), (), s32[]{:S(2)}) async-start(), calls=%async_computation.15 | async-start | bytes 5971968 | tf_op jit(solution)/shard_map/all_gather | solution.py:603
  142.4 6.3 copy-start.41
  198.8 37.1 %copy-start.13 = (bf16[576,768]{1,0:T(8,128)(2,1)}, bf16[576,768]{1,0:T(8,128)(2,1)S(1)}, u32[]{:S(2)}) copy-start(bf16[576,768]{1,0:T(8,128)(2,1)S(1)} %constant_dynamic-update-slice_fusion) | copy-start | bytes 2654212
  198.8 38.1 %copy-start.33 = (f32[64,2048]{1,0:T(8,128)S(1)}, f32[64,2048]{1,0:T(8,128)}, u32[]{:S(2)}) copy-start(f32[64,2048]{1,0:T(8,128)} %get-tuple-element.70.out_ref) | copy-start | bytes 1572868
  237.9 43.4 %all-to-all-start.1 = ((bf16[128,4,512]{2,0,1:T(8,128)(2,1)}), bf16[128,4,512]{2,0,1:T(8,128)(2,1)S(1)}, u32[]{:S(2)}, u32[]{:S(2)}) async-start(bf16[128,4,512]{2,0,1:T(8,128)(2,1)} %bitcast.257), calls=%async_computation.1 | async-start | bytes 1048576 | tf_op jit(solution)/shard_map/all_to_all | solution.py:607
  297.2 15.3 %collective-permute-start.2 = (bf16[8,432,768]{2,1,0:T(8,128)(2,1)}, bf16[8,432,768]{2,1,0:T(8,128)(2,1)}, u32[]{:S(2)}, u32[]{:S(2)}) collective-permute-start(bf16[8,432,768]{2,1,0:T(8,128)(2,1)} %bitcast.268), channel_id=1, source_target_pairs={{0,1},{1,0},{2,3},{3,2},{4,5},{5,4},{6,7},{7,6},{8,9},{9,8},{10,11... | collective-permute-start | bytes 15925256 | tf_op jit(solution)/shard_map/ppermute | solution.py:317
  298.2 13.7 %all-to-all-start.2 = ((bf16[64,4,512]{2,0,1:T(8,128)(2,1)}), bf16[64,4,512]{2,0,1:T(8,128)(2,1)S(1)}, u32[]{:S(2)}, u32[]{:S(2)}) async-start(bf16[64,4,512]{2,0,1:T(8,128)(2,1)} %bitcast.258), calls=%async_computation.2 | async-start | bytes 524288 | tf_op jit(solution)/shard_map/all_to_all | solution.py:607
  302.8 224.6 %reduce-scatter.3.cloned.1.call-start = ((), (), s32[]{:S(2)}) async-start(), calls=%async_computation.13 | async-start | bytes 5971968 | tf_op jit(solution)/shard_map/reduce_scatter | solution.py:681
  318.3 29.5 %copy-start.61 = (bf16[512,1536]{1,0:T(8,128)(2,1)}, bf16[512,1536]{1,0:T(8,128)(2,1)S(1)}, u32[]{:S(2)}) copy-start(bf16[512,1536]{1,0:T(8,128)(2,1)S(1)} %get-tuple-element.84) | copy-start | bytes 4718596
  328.4 16.6 %copy-start.59 = (bf16[512,1536]{1,0:T(8,128)(2,1)}, bf16[512,1536]{1,0:T(8,128)(2,1)S(1)}, u32[]{:S(2)}) copy-start(bf16[512,1536]{1,0:T(8,128)(2,1)S(1)} %get-tuple-element.86) | copy-start | bytes 4718596
  330.8 5.2 copy-start.21
  330.8 5.2 copy-start.23
  347.0 8.8 %collective-permute-start.3 = (bf16[8,432,768]{2,1,0:T(8,128)(2,1)S(1)}, bf16[8,432,768]{2,1,0:T(8,128)(2,1)S(1)}, u32[]{:S(2)}, u32[]{:S(2)}) collective-permute-start(bf16[8,432,768]{2,1,0:T(8,128)(2,1)S(1)} %pad_maximum_fusion), channel_id=1, source_target_pairs={{0,1},{1,0},{2,3},{3,2},{4,5},{5,4},{6,7},{7,6},{8,9},{9,8},{10,11... | collective-permute-start | bytes 15925256 | tf_op jit(solution)/shard_map/ppermute | solution.py:317
  361.4 23.3 %all-to-all-start.4 = ((bf16[4,64,512]{2,1,0:T(8,128)(2,1)}), bf16[4,64,512]{2,1,0:T(8,128)(2,1)S(1)}, u32[]{:S(2)}, u32[]{:S(2)}) async-start(bf16[4,64,512]{2,1,0:T(8,128)(2,1)} %slice_bitcast_fusion), calls=%async_computation.4 | async-start | bytes 524288 | tf_op jit(solution)/shard_map/all_to_all | solution.py:661
  384.7 62.1 %all-to-all-start.3 = ((bf16[4,128,512]{2,1,0:T(8,128)(2,1)}), bf16[4,128,512]{2,1,0:T(8,128)(2,1)S(1)}, u32[]{:S(2)}, u32[]{:S(2)}) async-start(bf16[4,128,512]{2,1,0:T(8,128)(2,1)} %bitcast.37), calls=%async_computation.3 | async-start | bytes 1048576 | tf_op jit(solution)/shard_map/all_to_all | solution.py:661
  446.8 5.2 copy-start.55
  446.8 5.3 copy-start.54
  446.9 5.4 copy-start.45
  446.9 6.7 copy-start.57
  446.9 7.4 copy-start.56
  446.9 72.2 %all-to-all-start.5 = ((bf16[8,2048,128]{2,1,0:T(8,128)(2,1)}), bf16[8,2048,128]{2,1,0:T(8,128)(2,1)}, u32[]{:S(2)}, u32[]{:S(2)}) async-start(bf16[8,2048,128]{2,1,0:T(8,128)(2,1)} %bitcast.277), calls=%async_computation.6 | async-start | bytes 8388608 | tf_op jit(solution)/shard_map/all_to_all | solution.py:705
  451.5 173.0 %all-gather.16.cloned.1.call-start = ((), (), s32[]{:S(2)}) async-start(), calls=%async_computation.16 | async-start | bytes 4423680 | tf_op jit(solution)/shard_map/all_gather | solution.py:620
  519.1 80.5 %all-to-all-start.6 = ((bf16[8,2048,128]{2,1,0:T(8,128)(2,1)}), bf16[8,2048,128]{2,1,0:T(8,128)(2,1)}, u32[]{:S(2)}, u32[]{:S(2)}) async-start(bf16[8,2048,128]{2,1,0:T(8,128)(2,1)} %bitcast.278), calls=%async_computation.7 | async-start | bytes 8388608 | tf_op jit(solution)/shard_map/all_to_all | solution.py:705
  523.8 132.8 %reduce-scatter.5.cloned.1.call-start = ((), (), s32[]{:S(2)}) async-start(), calls=%async_computation.14 | async-start | bytes 4718592 | tf_op jit(solution)/shard_map/reduce_scatter | solution.py:703
  528.1 67.7 %copy-start.52 = (f32[256]{0:T(256)}, f32[256]{0:T(256)S(1)}, u32[]{:S(2)}) copy-start(f32[256]{0:T(256)S(1)} %convert_reduce_fusion.4) | copy-start | bytes 3076
  529.7 69.9 %collective-permute-start.5 = (bf16[512,256]{1,0:T(8,128)(2,1)}, bf16[512,256]{1,0:T(8,128)(2,1)S(1)}, u32[]{:S(2)}, u32[]{:S(2)}) collective-permute-start(bf16[512,256]{1,0:T(8,128)(2,1)} %get-tuple-element.248), channel_id=1, source_target_pairs={{0,15},{15,16},{16,31},{31,0},{1,14},{14,17},{17,30},{30,1},{2,13}... | collective-permute-start | bytes 786440 | tf_op jit(solution)/shard_map/ppermute | solution.py:421
  535.4 64.2 %collective-permute-start.6 = (bf16[512,256]{1,0:T(8,128)(2,1)}, bf16[512,256]{1,0:T(8,128)(2,1)}, u32[]{:S(2)}, u32[]{:S(2)}) collective-permute-start(bf16[512,256]{1,0:T(8,128)(2,1)} %get-tuple-element.247), channel_id=1, source_target_pairs={{0,16},{15,31},{16,0},{31,15},{1,17},{14,30},{17,1},{30,14},{2,18}... | collective-permute-start | bytes 786440 | tf_op jit(solution)/shard_map/ppermute | solution.py:421
  537.9 61.7 %collective-permute-start.7 = (bf16[512,256]{1,0:T(8,128)(2,1)}, bf16[512,256]{1,0:T(8,128)(2,1)}, u32[]{:S(2)}, u32[]{:S(2)}) collective-permute-start(bf16[512,256]{1,0:T(8,128)(2,1)} %get-tuple-element.246), channel_id=1, source_target_pairs={{0,31},{15,0},{16,15},{31,16},{1,30},{14,1},{17,14},{30,17},{2,29}... | collective-permute-start | bytes 786440 | tf_op jit(solution)/shard_map/ppermute | solution.py:421
  537.9 61.7 %collective-permute-start.4 = (bf16[432,768]{1,0:T(8,128)(2,1)}, bf16[432,768]{1,0:T(8,128)(2,1)S(1)}, u32[]{:S(2)}, u32[]{:S(2)}) collective-permute-start(bf16[432,768]{1,0:T(8,128)(2,1)} %bitcast.53), channel_id=1, source_target_pairs={{0,2},{2,0},{1,3},{3,1},{4,6},{6,4},{5,7},{7,5},{8,10},{10,8},{9,1... | collective-permute-start | bytes 1990664 | tf_op jit(solution)/shard_map/ppermute | solution.py:317
  538.8 57.0 %copy-start.7 = (bf16[2048,768]{1,0:T(8,128)(2,1)S(1)}, bf16[2048,768]{1,0:T(8,128)(2,1)}, u32[]{:S(2)}) copy-start(bf16[2048,768]{1,0:T(8,128)(2,1)} %copy-done.6) | copy-start | bytes 9437188
  603.1 41.2 %collective-permute-start.18 = (bf16[432,768]{1,0:T(8,128)(2,1)}, bf16[432,768]{1,0:T(8,128)(2,1)}, u32[]{:S(2)}, u32[]{:S(2)}) collective-permute-start(bf16[432,768]{1,0:T(8,128)(2,1)} %add_convert_fusion.4), channel_id=1, source_target_pairs={{0,1},{1,0},{2,3},{3,2},{4,5},{5,4},{6,7},{7,6},{8,9},{9,8},{10,11... | collective-permute-start | bytes 1990664 | tf_op jit(solution)/shard_map/ppermute | solution.py:317
  611.3 9.5 %copy-start.8 = (bf16[2048,768]{1,0:T(8,128)(2,1)S(1)}, bf16[2048,768]{1,0:T(8,128)(2,1)}, u32[]{:S(2)}) copy-start(bf16[2048,768]{1,0:T(8,128)(2,1)} %copy-done.6) | copy-start | bytes 9437188
  611.3 9.5 %copy-start.27 = (bf16[64,2048]{1,0:T(8,128)(2,1)S(1)}, bf16[64,2048]{1,0:T(8,128)(2,1)}, u32[]{:S(2)}) copy-start(bf16[64,2048]{1,0:T(8,128)(2,1)} %get-tuple-element.101) | copy-start | bytes 786436
  614.4 25.2 %collective-permute-start.8 = (bf16[512,192]{0,1:T(8,128)(2,1)}, bf16[512,192]{0,1:T(8,128)(2,1)S(1)}, u32[]{:S(2)}, u32[]{:S(2)}) collective-permute-start(bf16[512,192]{0,1:T(8,128)(2,1)} %bitcast.261), channel_id=1, source_target_pairs={{0,15},{15,16},{16,31},{31,0},{1,14},{14,17},{17,30},{30,1},{2,13}... | collective-permute-start | bytes 589832 | tf_op jit(solution)/shard_map/ppermute | solution.py:421
  618.3 22.8 %collective-permute-start.9 = (bf16[512,192]{0,1:T(8,128)(2,1)}, bf16[512,192]{0,1:T(8,128)(2,1)S(1)}, u32[]{:S(2)}, u32[]{:S(2)}) collective-permute-start(bf16[512,192]{0,1:T(8,128)(2,1)} %bitcast.260), channel_id=1, source_target_pairs={{0,16},{15,31},{16,0},{31,15},{1,17},{14,30},{17,1},{30,14},{2,18}... | collective-permute-start | bytes 589832 | tf_op jit(solution)/shard_map/ppermute | solution.py:421
  619.0 5.5 copy-start.29
  619.0 23.7 %collective-permute-start.10 = (bf16[512,192]{0,1:T(8,128)(2,1)S(1)}, bf16[512,192]{0,1:T(8,128)(2,1)S(1)}, u32[]{:S(2)}, u32[]{:S(2)}) collective-permute-start(bf16[512,192]{0,1:T(8,128)(2,1)S(1)} %bitcast.341), channel_id=1, source_target_pairs={{0,31},{15,0},{16,15},{31,16},{1,30},{14,1},{17,14},{30,17},{2,29}... | collective-permute-start | bytes 589832 | tf_op jit(solution)/shard_map/ppermute | solution.py:421
  621.6 5.7 copy-start.25
  624.5 5.3 copy-start.15
  624.5 5.3 copy-start.37
  631.4 5.1 copy-start.28
  647.2 10.9 %copy-start.53 = (f32[256]{0:T(256)S(1)}, f32[256]{0:T(256)}, u32[]{:S(2)}) copy-start(f32[256]{0:T(256)} %copy-done.52) | copy-start | bytes 3076
  660.8 5.7 copy-start.58
  660.8 5.9 copy-start.9
  671.1 12.4 %collective-permute-start.14 = (bf16[608,384]{1,0:T(8,128)(2,1)}, bf16[608,384]{1,0:T(8,128)(2,1)}, u32[]{:S(2)}, u32[]{:S(2)}) collective-permute-start(bf16[608,384]{1,0:T(8,128)(2,1)} %fusion.46), channel_id=1, source_target_pairs={{0,1},{1,0},{2,3},{3,2},{4,5},{5,4},{6,7},{7,6},{8,9},{9,8},{10,11... | collective-permute-start | bytes 1400840 | tf_op jit(solution)/shard_map/ppermute | solution.py:317
  674.5 11.7 %collective-permute-start.11 = (bf16[512,128]{1,0:T(8,128)(2,1)S(1)}, bf16[512,128]{1,0:T(8,128)(2,1)S(1)}, u32[]{:S(2)}, u32[]{:S(2)}) collective-permute-start(bf16[512,128]{1,0:T(8,128)(2,1)S(1)} %get-tuple-element.281), channel_id=1, source_target_pairs={{0,15},{15,16},{16,31},{31,0},{1,14},{14,17},{17,30},{30,1},{2,13}... | collective-permute-start | bytes 393224 | tf_op jit(solution)/shard_map/ppermute | solution.py:421
  677.0 11.8 %collective-permute-start.12 = (bf16[512,128]{1,0:T(8,128)(2,1)S(1)}, bf16[512,128]{1,0:T(8,128)(2,1)S(1)}, u32[]{:S(2)}, u32[]{:S(2)}) collective-permute-start(bf16[512,128]{1,0:T(8,128)(2,1)S(1)} %get-tuple-element.280), channel_id=1, source_target_pairs={{0,16},{15,31},{16,0},{31,15},{1,17},{14,30},{17,1},{30,14},{2,18}... | collective-permute-start | bytes 393224 | tf_op jit(solution)/shard_map/ppermute | solution.py:421
  679.4 24.9 %collective-permute-start.13 = (bf16[512,128]{1,0:T(8,128)(2,1)S(1)}, bf16[512,128]{1,0:T(8,128)(2,1)S(1)}, u32[]{:S(2)}, u32[]{:S(2)}) collective-permute-start(bf16[512,128]{1,0:T(8,128)(2,1)S(1)} %get-tuple-element.279), channel_id=1, source_target_pairs={{0,31},{15,0},{16,15},{31,16},{1,30},{14,1},{17,14},{30,17},{2,29}... | collective-permute-start | bytes 393224 | tf_op jit(solution)/shard_map/ppermute | solution.py:421
  684.7 13.7 %collective-permute-start.15 = (bf16[608,384]{1,0:T(8,128)(2,1)S(1)}, bf16[608,384]{1,0:T(8,128)(2,1)S(1)}, u32[]{:S(2)}, u32[]{:S(2)}) collective-permute-start(bf16[608,384]{1,0:T(8,128)(2,1)S(1)} %add_convert_fusion.6), channel_id=1, source_target_pairs={{0,2},{2,0},{1,3},{3,1},{4,6},{6,4},{5,7},{7,5},{8,10},{10,8},{9,1... | collective-permute-start | bytes 1400840 | tf_op jit(solution)/shard_map/ppermute | solution.py:317
  698.5 5.8 copy-start.11
  698.6 5.8 copy-start.43
  699.6 21.8 %all-to-all-start.7 = ((bf16[4,208,384]{2,1,0:T(8,128)(2,1)}), bf16[4,208,384]{2,1,0:T(8,128)(2,1)}, u32[]{:S(2)}, u32[]{:S(2)}) async-start(bf16[4,208,384]{2,1,0:T(8,128)(2,1)} %fusion.41), calls=%async_computation.9 | async-start | bytes 1277952 | tf_op jit(solution)/shard_map/all_to_all | solution.py:480
  712.3 12.8 %copy-start.10 = (f32[512,768]{1,0:T(8,128)S(1)}, f32[512,768]{1,0:T(8,128)}, u32[]{:S(2)}) copy-start(f32[512,768]{1,0:T(8,128)} %get-tuple-element.235) | copy-start | bytes 4718596
  723.6 6.7 collective-permute-start.16
  725.1 8.4 %copy-start.1 = (bf16[768,384]{1,0:T(8,128)(2,1)S(1)}, bf16[768,384]{1,0:T(8,128)(2,1)}, u32[]{:S(2)}) copy-start(bf16[768,384]{1,0:T(8,128)(2,1)} %param.26) | copy-start | bytes 1769476
  731.1 1.5 collective-permute-start.17
  (33 other events, 80.0 us)
Sparse Core Ops, SparseCore 0:
  9.6 74.7 all-gather.7
  105.7 35.9 all-gather.9
  144.2 54.3 all-gather.11
  201.2 95.9 all-gather.13
  359.7 127.9 reduce-scatter.2
  489.7 89.8 all-gather.15
  599.8 56.8 reduce-scatter.4

commit v6 on v5

--- a/solution.py
+++ b/solution.py
@@ -457,45 +457,53 @@
     return jnp.concatenate(rows), vectors
 
 
-def send_triple(grads, small, at):
+def send_rows(grads, small, at):
     z, x, c = at
     model = grads.shape[1]
     half = model // 2
-    width = model // 4
-    three = 3 * width // 2
-    extra = small.shape[1] // half
+    width = grads.shape[0] // 3
     low = grads.astype(BF)
-    vectors = small.astype(BF).reshape(8 * extra, half)
-    vectors = pad_rows(vectors, 32)
-    mine = jnp.concatenate([part(low, c, half, 1), vectors])
-    other = jnp.concatenate([part(low, 1 - c, half, 1), vectors])
+    mine, other = part(low, c, half, 1), part(low, 1 - c, half, 1)
+    extra = 0
+    if small is not None:
+        extra = small.shape[1] // half
+        vectors = pad_rows(small.astype(BF).reshape(8 * extra, half), 32)
+        mine = jnp.concatenate([mine, vectors])
+        other = jnp.concatenate([other, vectors])
     total = (mine.astype(F32) + swap(other, "c").astype(F32)).astype(BF)
     total = swap_sum(total, "y").astype(BF)
-    by_depth = total[3 * width : 3 * width + 8 * extra].reshape(4, 2 * extra, half)
-    by_depth = jnp.pad(by_depth, ((0, 0), (0, 16 - 2 * extra), (0, 0)))
     slots = jnp.zeros((4, width, half), BF)
     for kind in range(3):
         piece = total[kind * width : (kind + 1) * width][None]
         slots = lax.dynamic_update_slice(slots, piece, ((z + 4 * kind) // 3, 0, 0))
-    got = lax.all_to_all(
-        jnp.concatenate([slots, by_depth], axis=1), "z", split_axis=0, concat_axis=0, tiled=True
-    )
-    pairs = jnp.concatenate(
+    if extra:
+        by_depth = total[3 * width : 3 * width + 8 * extra].reshape(4, 2 * extra, half)
+        by_depth = jnp.pad(by_depth, ((0, 0), (0, 16 - 2 * extra), (0, 0)))
+        slots = jnp.concatenate([slots, by_depth], axis=1)
+    got = lax.all_to_all(slots, "z", split_axis=0, concat_axis=0, tiled=True)
+    rows = jnp.concatenate(
         [
             lax.dynamic_index_in_dim(got, (i - z) % 4, 0, keepdims=False)[:width]
             for i in range(3)
         ]
     )
-    sums = jnp.sum(got[:, width : width + 2 * extra].astype(F32), axis=0).astype(BF)
-
-    def portion(index):
-        rows = part(pairs, index, three, 0)
-        return jnp.concatenate([rows, pad_rows(part(sums, index, extra, 0), 16)])
-
-    total = portion(x).astype(F32) + swap(portion(1 - x), "x").astype(F32)
-    own = total[:three].astype(BF)
+    if extra:
+        sums = jnp.sum(got[:, width : width + 2 * extra].astype(F32), axis=0).astype(BF)
+        rows = jnp.concatenate([rows, pad_rows(sums, 16)])
+    total = swap_sum(rows, "x")
+    pairs = total[: 3 * width].astype(BF).reshape(3, width, half)
+    if extra:
+        return pairs, part(total[3 * width : 3 * width + 2 * extra], x, extra, 0).reshape(-1)
+    return pairs
+
+
+def send_triple(grads, small, at, early):
+    z, x, c = at
+    late, vectors = send_rows(grads, small, at)
+    pairs = jnp.concatenate([early, late], axis=1)
+    own = part(pairs.reshape(-1, pairs.shape[2]), x, 3 * pairs.shape[1] // 2, 0)
     shard = in_order(c, own, swap(own, "c"), 1).astype(F32)
-    return shard.T, total[three : three + extra].reshape(-1)
+    return shard.T, vectors
 
 
 def send_triple_whole(grads, small, at):
@@ -655,21 +663,9 @@
     grad_atts = [mm("mf,tm->ft", w, grad_branch).astype(BF) for w in out_t]
     grad_att = in_order(c, grad_atts[0], grad_atts[1], 0)
     grad_att, acts, grad_pres = lax.optimization_barrier((grad_att, acts, grad_pres))
-    by_head = grad_att.reshape(depth, heads, HEAD_DIM, tokens)
-
-    def to_heads(first, last):
-        got = lax.all_to_all(
-            by_head[:, first:last].reshape(-1, tokens),
-            ALL,
-            split_axis=0,
-            concat_axis=1,
-            axis_index_groups=groups,
-            tiled=True,
-        )
-        return got
-
-    grad_first = to_heads(0, 1)
-    grad_rest = to_heads(1, heads)
+    grad_heads = lax.all_to_all(
+        grad_att, ALL, split_axis=0, concat_axis=1, axis_index_groups=groups, tiled=True
+    )
     grads_r = [mm("tm,th->mh", cotangent, act).astype(BF) for act in acts]
     grads_a = [mm("th,tm->hm", g, normed2).astype(BF) for g in grad_pres]
     grads_o = [mm("tm,ft->mf", grad_branch, a).astype(BF) for a in atts]
@@ -677,12 +673,14 @@
     packs = [
         pack_grads(e, w, o, shards) for e, w, o in zip(grads_a, grads_r, grads_o)
     ]
-    sum_w = (packs[0].astype(F32) + swap(packs[1], "c").astype(F32)).astype(BF)
+    swapped_w = swap(packs[1], "c")
+    swapped_w, grad_heads = lax.optimization_barrier((swapped_w, grad_heads))
+    sum_w = (packs[0].astype(F32) + swapped_w.astype(F32)).astype(BF)
     sum_w = lax.psum_scatter(sum_w, WEIGHT_AXES, scatter_dimension=0, tiled=False)
 
     dqs, dkvs = [], []
     for h in range(heads):
-        g_h = head(grad_rest, h - 1) if h else grad_first
+        g_h = head(grad_heads, h)
         if h:
             g_h, dqs[-1] = lax.optimization_barrier((g_h, dqs[-1]))
         if h == heads - 1:
@@ -716,7 +714,7 @@
     pieces.append(jnp.concatenate([dqs[-1].T, sum_pieces(dkvs[1])], axis=1))
     pieces.append(dkvs[2])
     got += [exchange(d, z, groups) for d in pieces[1:]]
-    grad_w = jnp.concatenate([mm("tf,tm->fm", d, normed1) for d in pieces])
+    grad_w = [mm("tf,tm->fm", d, normed1) for d in pieces]
     grad_u = jnp.concatenate([mm("tf,tm->fm", d, unit_low) for d in pieces])
     grad_s = jnp.concatenate([jnp.sum(d.astype(F32), axis=0) for d in pieces])
     grad_gain1 = jnp.sum(w_own.astype(F32) * grad_u, axis=0)
@@ -728,7 +726,17 @@
 
     grad_q_b = of_kind(grad_s, 0)
     grad_v_b = of_kind(grad_s, 2)
-    grad_w = jnp.concatenate([of_kind(grad_w, kind) for kind in range(3)])
+    (w_a, w_b, w_c) = grad_w
+    kinds = [
+        jnp.concatenate([w_a[:128], w_b[:64]]),
+        jnp.concatenate([w_a[128:192], w_b[64:128], w_c[:64]]),
+        jnp.concatenate([w_a[192:256], w_b[128:192], w_c[64:]]),
+    ]
+    if special:
+        early = send_rows(jnp.concatenate([k[:128] for k in kinds]), None, at)
+        grad_w = jnp.concatenate([k[128:] for k in kinds])
+    else:
+        grad_w = jnp.concatenate(kinds)
     grad_normed1 = 0.0
     at_row = 0
     for blocks_got in got:
@@ -759,7 +767,10 @@
         ],
         axis=1,
     )
-    grad_triple_w, flat = (send_triple if special else send_triple_whole)(grad_w, small_grads, at)
+    if special:
+        grad_triple_w, flat = send_triple(grad_w, small_grads, at, early)
+    else:
+        grad_triple_w, flat = send_triple_whole(grad_w, small_grads, at)
     vecs = [flat[i * here : (i + 1) * here] for i in range(8)]
     grad_e_b = flat[8 * here : 8 * here + hidden_here]
     return (

time: 748 us -> 750 us (level)
    ppermute x9, waiting for transfers between devices: 0.19 us -> 11 us  [exchange(): got.append(lax.ppermute(sent, ALL, pairs))]
    ppermute x10 -> x13, waiting for transfers between devices: 66.6 us -> 63.2 us  [swap(): return lax.ppermute(array, axis, [(0, 1), (1, 0)])]
  transfers between devices with their start and end apart: 34 -> 37, of which waited for: 14 -> 17; matrix products, arithmetic and copies ran while one was open for 18% -> 20% of each run, Pallas kernels for 38% -> 38%
where the time goes in v6:
time: 750 us; the launch traced here: 743 us
  Pallas kernels  280 us (37%)
  waiting for transfers between devices  174 us (23%)
  matrix products  85.8 us (11%)
  local copies, waits for them, and re-layouts  76.7 us (10%)
  starting transfers between devices  63.3 us (8%)
  other arithmetic  46.8 us (6%)
  between operations  16.4 us (2%)
    pallas_call x3, Pallas kernels, attend_back(): pl.pallas_call(functools.partial(backward_kernel, strips, unroll), grid=(...  170 us
    pallas_call x3, Pallas kernels, attend(): pl.pallas_call(functools.partial(forward_kernel, strips, unroll), grid=(s...  110 us
    dot_general x38, matrix products, mm(): return jnp.einsum(spec, a, b, preferred_element_type=F32)  85.8 us
    ppermute x13, waiting for transfers between devices, swap(): return lax.ppermute(array, axis, [(0, 1), (1, 0)])  63.2 us
    all_gather x1, waiting for transfers between devices, on_device(): keys = [lax.all_gather(pair(0), RING, axis=0, tiled=True)]  33.8 us
    all_to_all x1, waiting for transfers between devices, fetch_triple(): got = lax.all_to_all(slots, 'z', split_axis=0, concat_axis=0, tiled=True)  18.1 us
    all_gather x1, waiting for transfers between devices, on_device(): mine_w = lax.all_gather(own_w, WEIGHT_AXES, axis=0, tiled=False)  15.5 us
  transfers between devices with their start and end apart: 37, of which 17 were waited for; matrix products, arithmetic and copies ran while one was open for 20% of the time, Pallas kernels for 38%

profile of v6, /device:TPU:0, one launch (start us, length us, event | category | flops | bytes accessed | tf_op | source)
XLA Modules:
  0.0 742.9 jit_solution(11307540541738189102)
XLA Ops:
  7.9 6.1 concatenate.158
  15.1 3.0 collective-permute-start
  18.1 49.2 %collective-permute-done = bf16[304,384]{1,0:T(8,128)(2,1)S(1)} collective-permute-done((bf16[304,384]{1,0:T(8,128)(2,1)S(1)}, bf16[304,384]{1,0:T(8,128)(2,1)S(1)}, u32[]{:S(2)}, u32[]{:S(2)}) %collective-permute-start) | collective-permute-done | bytes 233504 | tf_op jit(solution)/shard_map/ppermute | solution.py:317
  68.9 5.8 all-to-all-start
  74.7 18.1 %all-to-all-done = bf16[4,208,384]{2,1,0:T(8,128)(2,1)S(1)} async-done(((bf16[4,208,384]{2,1,0:T(8,128)(2,1)}), bf16[4,208,384]{2,1,0:T(8,128)(2,1)S(1)}, u32[]{:S(2)}, u32[]{:S(2)}) %all-to-all-start) | async-done | bytes 639008 | tf_op jit(solution)/shard_map/all_to_all | solution.py:439
  95.2 2.5 convert_reduce_fusion
  99.1 2.6 fusion.2
  107.9 33.8 %all-gather.10.cloned.1.call-done.kv_ref = bf16[16384,128]{1,0:T(8,128)(2,1)} async-done(((bf16[2048,128]{1,0:T(8,128)(2,1)}), bf16[16384,128]{1,0:T(8,128)(2,1)}) %all-gather.10.cloned.1.call-update) | async-done | bytes 4194320 | tf_op jit(solution)/shard_map/all_gather | solution.py:596
  142.4 2.9 reshape.351
  145.3 2.5 dynamic-slice_reduce_fusion
  149.8 3.4 fusion.21
  154.1 36.7 %shard_map.262 = (f32[64,2048]{1,0:T(8,128)}, f32[8,2048]{1,0:T(8,128)}) custom-call(s32[2]{0:T(128)} %pad_add_fusion.r_ref, bf16[64,2048]{1,0:T(8,128)(2,1)} %get-tuple-element.264.q_ref, bf16[16384,128]{1,0:T(8,128)(2,1)} %all-gather.10.cloned.1.call-done.kv_ref), custom_call_target="tpu_custom_call" | custom-call | flops 15000000512 | bytes 8388608 | tf_op jit(solution)/shard_map/pallas_call | solution.py:139
  190.9 7.8 %all-gather.12.cloned.1.call-done.kv_ref = bf16[16384,256]{1,0:T(8,128)(2,1)} async-done(((bf16[2048,256]{1,0:T(8,128)(2,1)}), bf16[16384,256]{1,0:T(8,128)(2,1)}) %all-gather.12.cloned.1.call-update) | async-done | bytes 8388624 | tf_op jit(solution)/shard_map/all_gather | solution.py:598
  199.7 36.7 %shard_map.263 = (f32[64,2048]{1,0:T(8,128)}, f32[8,2048]{1,0:T(8,128)}) custom-call(s32[2]{0:T(128)} %pad_add_fusion.r_ref, bf16[64,2048]{1,0:T(8,128)(2,1)} %get-tuple-element.67.q_ref, bf16[16384,256]{1,0:T(8,128)(2,1)} %all-gather.12.cloned.1.call-done.kv_ref), custom_call_target="tpu_custom_call" | custom-call | flops 15000000512 | bytes 8388608 | tf_op jit(solution)/shard_map/pallas_call | solution.py:139
  238.4 5.6 all-to-all-start.1
  244.0 36.7 %shard_map.264 = (f32[64,2048]{1,0:T(8,128)}, f32[8,2048]{1,0:T(8,128)}) custom-call(s32[2]{0:T(128)} %pad_add_fusion.r_ref, bf16[64,2048]{1,0:T(8,128)(2,1)} %get-tuple-element.70.q_ref, bf16[16384,256]{1,0:T(8,128)(2,1)} %all-gather.12.cloned.1.call-done.kv_ref), custom_call_target="tpu_custom_call" | custom-call | flops 15000000512 | bytes 8388608 | tf_op jit(solution)/shard_map/pallas_call | solution.py:139
  281.8 15.5 %all-gather.14.cloned.1.call-done = bf16[3456,768]{1,0:T(8,128)(2,1)} async-done(((bf16[432,768]{1,0:T(8,128)(2,1)}), bf16[3456,768]{1,0:T(8,128)(2,1)}) %all-gather.14.cloned.1.call-update) | async-done | bytes 5308432 | tf_op jit(solution)/shard_map/all_gather | solution.py:611
  298.0 4.6 all-to-all-start.2
  305.3 3.3 slice.428
  308.6 3.2 fusion.108
  316.4 3.2 multiply_convert_fusion.1
  319.6 4.8 convert_reduce_fusion.2
  329.6 2.4 fusion.107
  332.0 5.2 convert_reduce_fusion.1
  337.2 2.3 multiply_reduce_fusion
  339.5 2.4 fusion.106
  347.9 3.0 pad_maximum_fusion
  350.9 6.6 all-to-all-start.3
  363.6 2.9 convolution_convert_fusion.1
  366.5 12.6 %all-to-all-done.3 = bf16[4,192,512]{2,1,0:T(8,128)(2,1)} async-done(((bf16[4,192,512]{2,1,0:T(8,128)(2,1)}), bf16[4,192,512]{2,1,0:T(8,128)(2,1)}, u32[]{:S(2)}, u32[]{:S(2)}) %all-to-all-start.3) | async-done | bytes 786464 | tf_op jit(solution)/shard_map/all_to_all | solution.py:666
  381.4 7.4 add_convert_fusion
  391.2 56.5 %shard_map.265 = (bf16[64,2048]{1,0:T(8,128)(2,1)}, bf16[16384,128]{1,0:T(8,128)(2,1)}) custom-call(s32[2]{0:T(128)} %pad_add_fusion.r_ref, bf16[64,2048]{1,0:T(8,128)(2,1)} %get-tuple-element.264.q_ref, bf16[64,2048]{1,0:T(8,128)(2,1)} %get-tuple-element.259.g_ref, f32[64,2048]{1,0:T(8,128)} %get-tuple-element.72.out_ref, ...), custom_call_target="tpu_custom_call" | custom-call | flops 24999999488 | bytes 12582912 | tf_op jit(solution)/shard_map/pallas_call | solution.py:257
  447.7 4.6 all-to-all-start.4
  455.9 3.7 fusion.37
  461.9 56.6 %shard_map.266 = (bf16[64,2048]{1,0:T(8,128)(2,1)}, bf16[16384,128]{1,0:T(8,128)(2,1)}) custom-call(s32[2]{0:T(128)} %pad_add_fusion.r_ref, bf16[64,2048]{1,0:T(8,128)(2,1)} %get-tuple-element.67.q_ref, bf16[64,2048]{1,0:T(8,128)(2,1)} %get-tuple-element.84.g_ref, f32[64,2048]{1,0:T(8,128)} %get-tuple-element.73.out_ref, ...), custom_call_target="tpu_custom_call" | custom-call | flops 24999999488 | bytes 12582912 | tf_op jit(solution)/shard_map/pallas_call | solution.py:257
  518.5 4.7 all-to-all-start.5
  523.3 3.1 reduce_sum.233
  527.6 2.9 convolution_convert_fusion.6
  533.9 2.6 collective-permute-start.7
  537.7 56.7 %shard_map.267 = (bf16[64,2048]{1,0:T(8,128)(2,1)}, bf16[16384,128]{1,0:T(8,128)(2,1)}) custom-call(s32[2]{0:T(128)} %pad_add_fusion.r_ref, bf16[64,2048]{1,0:T(8,128)(2,1)} %get-tuple-element.70.q_ref, bf16[64,2048]{1,0:T(8,128)(2,1)} %get-tuple-element.94.g_ref, f32[64,2048]{1,0:T(8,128)} %get-tuple-element.71.out_ref, ...), custom_call_target="tpu_custom_call" | custom-call | flops 24999999488 | bytes 12582912 | tf_op jit(solution)/shard_map/pallas_call | solution.py:257
  600.6 3.1 reduce_sum.234
  604.6 2.7 convolution_convert_fusion.9
  609.3 2.4 constant_dynamic-slice_fusion.7
  612.4 4.1 collective-permute-start.10
  619.2 2.7 fusion.58
  621.9 2.6 fusion.47
  624.5 2.6 fusion.44
  627.1 2.7 fusion.45
  629.8 2.6 fusion.46
  637.9 2.6 fusion.55
  642.8 10.3 %collective-permute-done.9 = bf16[512,192]{0,1:T(8,128)(2,1)S(1)} collective-permute-done((bf16[512,192]{0,1:T(8,128)(2,1)S(1)}, bf16[512,192]{0,1:T(8,128)(2,1)S(1)}, u32[]{:S(2)}, u32[]{:S(2)}) %collective-permute-start.9) | collective-permute-done | bytes 196640 | tf_op jit(solution)/shard_map/ppermute | solution.py:421
  653.1 2.5 fusion.56
  655.6 2.6 fusion.57
  662.5 3.5 all-to-all-start.7
  672.6 2.6 reshape.406
  675.2 3.1 all-to-all-done.7
  680.2 6.6 collective-permute-done.19
  690.5 3.3 collective-permute-start.11
  694.1 2.8 fusion.127
  698.0 2.7 convolution_convert_fusion.10
  706.5 3.6 fusion.105
  713.0 5.9 all-to-all-start.6
  718.9 8.0 %all-to-all-done.6 = bf16[4,80,384]{2,1,0:T(8,128)(2,1)S(1)} async-done(((bf16[4,80,384]{2,1,0:T(8,128)(2,1)}), bf16[4,80,384]{2,1,0:T(8,128)(2,1)S(1)}, u32[]{:S(2)}, u32[]{:S(2)}) %all-to-all-start.6) | async-done | bytes 245792 | tf_op jit(solution)/shard_map/all_to_all | solution.py:483
  727.4 2.9 fusion.32
  (423 shorter events, 114.2 us)
Async XLA Ops:
  7.2 134.8 %copy-start = (bf16[768,384]{1,0:T(8,128)(2,1)S(1)}, bf16[768,384]{1,0:T(8,128)(2,1)}, u32[]{:S(2)}) copy-start(bf16[768,384]{1,0:T(8,128)(2,1)} %param.26) | copy-start | bytes 1769476
  7.2 87.9 %all-gather.8.cloned.1.call-start = ((), (), s32[]{:S(2)}) async-start(), calls=%async_computation.10 | async-start | bytes 3932160 | tf_op jit(solution)/shard_map/all_gather | solution.py:570
  15.1 52.2 %collective-permute-start = (bf16[304,384]{1,0:T(8,128)(2,1)S(1)}, bf16[304,384]{1,0:T(8,128)(2,1)S(1)}, u32[]{:S(2)}, u32[]{:S(2)}) collective-permute-start(bf16[304,384]{1,0:T(8,128)(2,1)S(1)} %get-tuple-element.298), channel_id=1, source_target_pairs={{0,4},{4,0},{1,5},{5,1},{2,6},{6,2},{3,7},{7,3},{8,12},{12,8},{9,1... | collective-permute-start | bytes 700424 | tf_op jit(solution)/shard_map/ppermute | solution.py:317
  68.9 24.0 %all-to-all-start = ((bf16[4,208,384]{2,1,0:T(8,128)(2,1)}), bf16[4,208,384]{2,1,0:T(8,128)(2,1)S(1)}, u32[]{:S(2)}, u32[]{:S(2)}) async-start(bf16[4,208,384]{2,1,0:T(8,128)(2,1)} %pad_maximum_fusion.12), calls=%async_computation | async-start | bytes 1277952 | tf_op jit(solution)/shard_map/all_to_all | solution.py:439
  74.7 67.1 %all-gather.10.cloned.1.call-start = ((), (), s32[]{:S(2)}) async-start(), calls=%async_computation.11 | async-start | bytes 4718592 | tf_op jit(solution)/shard_map/all_gather | solution.py:596
  93.0 1.9 collective-permute-start.1
  105.6 93.0 %all-gather.12.cloned.1.call-start = ((), (), s32[]{:S(2)}) async-start(), calls=%async_computation.12 | async-start | bytes 9437184 | tf_op jit(solution)/shard_map/all_gather | solution.py:598
  141.8 155.5 %all-gather.14.cloned.1.call-start = ((), (), s32[]{:S(2)}) async-start(), calls=%async_computation.15 | async-start | bytes 5971968 | tf_op jit(solution)/shard_map/all_gather | solution.py:611
  142.4 6.3 copy-start.54
  198.8 37.6 %copy-start.20 = (bf16[576,768]{1,0:T(8,128)(2,1)}, bf16[576,768]{1,0:T(8,128)(2,1)S(1)}, u32[]{:S(2)}) copy-start(bf16[576,768]{1,0:T(8,128)(2,1)S(1)} %constant_dynamic-update-slice_fusion) | copy-start | bytes 2654212
  238.4 43.4 %all-to-all-start.1 = ((bf16[128,4,512]{2,0,1:T(8,128)(2,1)}), bf16[128,4,512]{2,0,1:T(8,128)(2,1)S(1)}, u32[]{:S(2)}, u32[]{:S(2)}) async-start(bf16[128,4,512]{2,0,1:T(8,128)(2,1)} %bitcast.266), calls=%async_computation.1 | async-start | bytes 1048576 | tf_op jit(solution)/shard_map/all_to_all | solution.py:615
  297.2 15.3 %collective-permute-start.2 = (bf16[8,432,768]{2,1,0:T(8,128)(2,1)}, bf16[8,432,768]{2,1,0:T(8,128)(2,1)}, u32[]{:S(2)}, u32[]{:S(2)}) collective-permute-start(bf16[8,432,768]{2,1,0:T(8,128)(2,1)} %bitcast.277), channel_id=1, source_target_pairs={{0,1},{1,0},{2,3},{3,2},{4,5},{5,4},{6,7},{7,6},{8,9},{9,8},{10,11... | collective-permute-start | bytes 15925256 | tf_op jit(solution)/shard_map/ppermute | solution.py:317
  298.0 13.8 %all-to-all-start.2 = ((bf16[64,4,512]{2,0,1:T(8,128)(2,1)}), bf16[64,4,512]{2,0,1:T(8,128)(2,1)S(1)}, u32[]{:S(2)}, u32[]{:S(2)}) async-start(bf16[64,4,512]{2,0,1:T(8,128)(2,1)} %bitcast.267), calls=%async_computation.2 | async-start | bytes 524288 | tf_op jit(solution)/shard_map/all_to_all | solution.py:615
  311.9 31.1 %copy-start.9 = (bf16[4,192,512]{2,1,0:T(8,128)(2,1)}, bf16[4,192,512]{2,1,0:T(8,128)(2,1)S(1)}, u32[]{:S(2)}) copy-start(bf16[4,192,512]{2,1,0:T(8,128)(2,1)S(1)} %pad_maximum_fusion.10) | copy-start | bytes 2359300
  315.2 29.6 %copy-start.37 = (bf16[512,768]{1,0:T(8,128)(2,1)}, bf16[512,768]{1,0:T(8,128)(2,1)S(1)}, u32[]{:S(2)}) copy-start(bf16[512,768]{1,0:T(8,128)(2,1)S(1)} %add_convert_fusion.3) | copy-start | bytes 2359300
  329.6 16.7 %copy-start.76 = (bf16[512,1536]{1,0:T(8,128)(2,1)}, bf16[512,1536]{1,0:T(8,128)(2,1)S(1)}, u32[]{:S(2)}) copy-start(bf16[512,1536]{1,0:T(8,128)(2,1)S(1)} %get-tuple-element.79) | copy-start | bytes 4718596
  350.9 30.5 %collective-permute-start.3 = (bf16[8,432,768]{2,1,0:T(8,128)(2,1)}, bf16[8,432,768]{2,1,0:T(8,128)(2,1)}, u32[]{:S(2)}, u32[]{:S(2)}) collective-permute-start(bf16[8,432,768]{2,1,0:T(8,128)(2,1)} %pad_maximum_fusion), channel_id=1, source_target_pairs={{0,1},{1,0},{2,3},{3,2},{4,5},{5,4},{6,7},{7,6},{8,9},{9,8},{10,11... | collective-permute-start | bytes 15925256 | tf_op jit(solution)/shard_map/ppermute | solution.py:317
  350.9 28.2 %all-to-all-start.3 = ((bf16[4,192,512]{2,1,0:T(8,128)(2,1)}), bf16[4,192,512]{2,1,0:T(8,128)(2,1)}, u32[]{:S(2)}, u32[]{:S(2)}) async-start(bf16[4,192,512]{2,1,0:T(8,128)(2,1)} %bitcast.301), calls=%async_computation.3 | async-start | bytes 1572864 | tf_op jit(solution)/shard_map/all_to_all | solution.py:666
  357.6 169.2 %reduce-scatter.3.cloned.1.call-start = ((), (), s32[]{:S(2)}) async-start(), calls=%async_computation.13 | async-start | bytes 5971968 | tf_op jit(solution)/shard_map/reduce_scatter | solution.py:679
  447.7 5.3 copy-start.70
  447.7 5.4 copy-start.73
  447.7 6.0 copy-start.72
  447.7 6.7 copy-start.60
  447.7 70.7 %all-to-all-start.4 = ((bf16[8,2048,128]{2,1,0:T(8,128)(2,1)}), bf16[8,2048,128]{2,1,0:T(8,128)(2,1)}, u32[]{:S(2)}, u32[]{:S(2)}) async-start(bf16[8,2048,128]{2,1,0:T(8,128)(2,1)} %bitcast.287), calls=%async_computation.5 | async-start | bytes 8388608 | tf_op jit(solution)/shard_map/all_to_all | solution.py:703
  452.3 166.8 %all-gather.16.cloned.1.call-start = ((), (), s32[]{:S(2)}) async-start(), calls=%async_computation.16 | async-start | bytes 4423680 | tf_op jit(solution)/shard_map/all_gather | solution.py:628
  518.5 77.8 %all-to-all-start.5 = ((bf16[8,2048,128]{2,1,0:T(8,128)(2,1)}), bf16[8,2048,128]{2,1,0:T(8,128)(2,1)}, u32[]{:S(2)}, u32[]{:S(2)}) async-start(bf16[8,2048,128]{2,1,0:T(8,128)(2,1)} %bitcast.286), calls=%async_computation.6 | async-start | bytes 8388608 | tf_op jit(solution)/shard_map/all_to_all | solution.py:703
  523.2 163.6 %reduce-scatter.5.cloned.1.call-start = ((), (), s32[]{:S(2)}) async-start(), calls=%async_computation.14 | async-start | bytes 4718592 | tf_op jit(solution)/shard_map/reduce_scatter | solution.py:701
  531.0 65.8 %collective-permute-start.4 = (bf16[432,768]{1,0:T(8,128)(2,1)}, bf16[432,768]{1,0:T(8,128)(2,1)}, u32[]{:S(2)}, u32[]{:S(2)}) collective-permute-start(bf16[432,768]{1,0:T(8,128)(2,1)} %bitcast.346), channel_id=1, source_target_pairs={{0,2},{2,0},{1,3},{3,1},{4,6},{6,4},{5,7},{7,5},{8,10},{10,8},{9,1... | collective-permute-start | bytes 1990664 | tf_op jit(solution)/shard_map/ppermute | solution.py:317
  533.9 62.3 %collective-permute-start.7 = (bf16[512,256]{1,0:T(8,128)(2,1)}, bf16[512,256]{1,0:T(8,128)(2,1)S(1)}, u32[]{:S(2)}, u32[]{:S(2)}) collective-permute-start(bf16[512,256]{1,0:T(8,128)(2,1)} %get-tuple-element.250), channel_id=1, source_target_pairs={{0,31},{15,0},{16,15},{31,16},{1,30},{14,1},{17,14},{30,17},{2,29}... | collective-permute-start | bytes 786440 | tf_op jit(solution)/shard_map/ppermute | solution.py:421
  536.5 59.8 %collective-permute-start.6 = (bf16[512,256]{1,0:T(8,128)(2,1)}, bf16[512,256]{1,0:T(8,128)(2,1)S(1)}, u32[]{:S(2)}, u32[]{:S(2)}) collective-permute-start(bf16[512,256]{1,0:T(8,128)(2,1)} %get-tuple-element.251), channel_id=1, source_target_pairs={{0,16},{15,31},{16,0},{31,15},{1,17},{14,30},{17,1},{30,14},{2,18}... | collective-permute-start | bytes 786440 | tf_op jit(solution)/shard_map/ppermute | solution.py:421
  536.5 59.8 %collective-permute-start.5 = (bf16[512,256]{1,0:T(8,128)(2,1)}, bf16[512,256]{1,0:T(8,128)(2,1)S(1)}, u32[]{:S(2)}, u32[]{:S(2)}) collective-permute-start(bf16[512,256]{1,0:T(8,128)(2,1)} %get-tuple-element.252), channel_id=1, source_target_pairs={{0,15},{15,16},{16,31},{31,0},{1,14},{14,17},{17,30},{30,1},{2,13}... | collective-permute-start | bytes 786440 | tf_op jit(solution)/shard_map/ppermute | solution.py:421
  537.7 56.7 %copy-start.5 = (bf16[2048,768]{1,0:T(8,128)(2,1)S(1)}, bf16[2048,768]{1,0:T(8,128)(2,1)}, u32[]{:S(2)}) copy-start(bf16[2048,768]{1,0:T(8,128)(2,1)} %get-tuple-element.244) | copy-start | bytes 9437188
  600.6 65.3 %collective-permute-start.21 = (bf16[432,768]{1,0:T(8,128)(2,1)}, bf16[432,768]{1,0:T(8,128)(2,1)}, u32[]{:S(2)}, u32[]{:S(2)}) collective-permute-start(bf16[432,768]{1,0:T(8,128)(2,1)} %add_convert_fusion.4), channel_id=1, source_target_pairs={{0,1},{1,0},{2,3},{3,2},{4,5},{5,4},{6,7},{7,6},{8,9},{9,8},{10,11... | collective-permute-start | bytes 1990664 | tf_op jit(solution)/shard_map/ppermute | solution.py:317
  608.8 31.7 %collective-permute-start.17 = (bf16[384,384]{1,0:T(8,128)(2,1)}, bf16[384,384]{1,0:T(8,128)(2,1)}, u32[]{:S(2)}, u32[]{:S(2)}) collective-permute-start(bf16[384,384]{1,0:T(8,128)(2,1)} %constant_dynamic-slice_fusion.2), channel_id=1, source_target_pairs={{0,1},{1,0},{2,3},{3,2},{4,5},{5,4},{6,7},{7,6},{8,9},{9,8},{10,11... | collective-permute-start | bytes 884744 | tf_op jit(solution)/shard_map/ppermute | solution.py:317
  612.4 25.5 %collective-permute-start.10 = (bf16[512,192]{0,1:T(8,128)(2,1)}, bf16[512,192]{0,1:T(8,128)(2,1)}, u32[]{:S(2)}, u32[]{:S(2)}) collective-permute-start(bf16[512,192]{0,1:T(8,128)(2,1)} %bitcast.268), channel_id=1, source_target_pairs={{0,31},{15,0},{16,15},{31,16},{1,30},{14,1},{17,14},{30,17},{2,29}... | collective-permute-start | bytes 589832 | tf_op jit(solution)/shard_map/ppermute | solution.py:421
  616.7 17.4 %copy-start.58 = (f32[192]{0:T(256)}, f32[192]{0:T(256)S(1)}, u32[]{:S(2)}) copy-start(f32[192]{0:T(256)S(1)} %convert_reduce_fusion.5) | copy-start | bytes 2308
  619.2 5.3 copy-start.45
  635.7 19.9 %collective-permute-start.8 = (bf16[512,192]{0,1:T(8,128)(2,1)S(1)}, bf16[512,192]{0,1:T(8,128)(2,1)S(1)}, u32[]{:S(2)}, u32[]{:S(2)}) collective-permute-start(bf16[512,192]{0,1:T(8,128)(2,1)S(1)} %bitcast.350), channel_id=1, source_target_pairs={{0,15},{15,16},{16,31},{31,0},{1,14},{14,17},{17,30},{30,1},{2,13}... | collective-permute-start | bytes 589832 | tf_op jit(solution)/shard_map/ppermute | solution.py:421
  636.5 16.6 %collective-permute-start.9 = (bf16[512,192]{0,1:T(8,128)(2,1)S(1)}, bf16[512,192]{0,1:T(8,128)(2,1)S(1)}, u32[]{:S(2)}, u32[]{:S(2)}) collective-permute-start(bf16[512,192]{0,1:T(8,128)(2,1)S(1)} %bitcast.351), channel_id=1, source_target_pairs={{0,16},{15,31},{16,0},{31,15},{1,17},{14,30},{17,1},{30,14},{2,18}... | collective-permute-start | bytes 589832 | tf_op jit(solution)/shard_map/ppermute | solution.py:421
  641.6 18.1 %collective-permute-start.18 = (bf16[384,384]{1,0:T(8,128)(2,1)S(1)}, bf16[384,384]{1,0:T(8,128)(2,1)S(1)}, u32[]{:S(2)}, u32[]{:S(2)}) collective-permute-start(bf16[384,384]{1,0:T(8,128)(2,1)S(1)} %add_convert_fusion.7), channel_id=1, source_target_pairs={{0,2},{2,0},{1,3},{3,1},{4,6},{6,4},{5,7},{7,5},{8,10},{10,8},{9,1... | collective-permute-start | bytes 884744 | tf_op jit(solution)/shard_map/ppermute | solution.py:317
  662.5 15.8 %all-to-all-start.7 = ((bf16[4,128,384]{2,1,0:T(8,128)(2,1)}), bf16[4,128,384]{2,1,0:T(8,128)(2,1)S(1)}, u32[]{:S(2)}, u32[]{:S(2)}) async-start(bf16[4,128,384]{2,1,0:T(8,128)(2,1)} %fusion.75), calls=%async_computation.9 | async-start | bytes 786432 | tf_op jit(solution)/shard_map/all_to_all | solution.py:483
  672.6 6.9 copy-start.52
  672.6 6.9 copy-start.53
  675.2 13.1 %copy-start.59 = (f32[192]{0:T(256)S(1)}, f32[192]{0:T(256)}, u32[]{:S(2)}) copy-start(f32[192]{0:T(256)} %copy-done.58) | copy-start | bytes 2308
  675.2 13.1 %copy-start.69 = (f32[256]{0:T(256)S(1)}, f32[256]{0:T(256)}, u32[]{:S(2)}) copy-start(f32[256]{0:T(256)} %copy-done.68) | copy-start | bytes 3076
  678.3 15.5 %copy-start.74 = (f32[64]{0:T(128)S(1)}, f32[64]{0:T(128)}, u32[]{:S(2)}) copy-start(f32[64]{0:T(128)} %get-tuple-element.319) | copy-start | bytes 772
  678.3 15.5 %copy-start.75 = (f32[64]{0:T(128)S(1)}, f32[64]{0:T(128)}, u32[]{:S(2)}) copy-start(f32[64]{0:T(128)} %slice.469) | copy-start | bytes 772
  678.4 8.4 %collective-permute-start.19 = (bf16[384,384]{1,0:T(8,128)(2,1)S(1)}, bf16[384,384]{1,0:T(8,128)(2,1)S(1)}, u32[]{:S(2)}, u32[]{:S(2)}) collective-permute-start(bf16[384,384]{1,0:T(8,128)(2,1)S(1)} %pad_maximum_fusion.17), channel_id=1, source_target_pairs={{0,4},{4,0},{1,5},{5,1},{2,6},{6,2},{3,7},{7,3},{8,12},{12,8},{9,1... | collective-permute-start | bytes 884744 | tf_op jit(solution)/shard_map/ppermute | solution.py:317
  690.1 16.3 %collective-permute-start.13 = (bf16[512,128]{1,0:T(8,128)(2,1)}, bf16[512,128]{1,0:T(8,128)(2,1)S(1)}, u32[]{:S(2)}, u32[]{:S(2)}) collective-permute-start(bf16[512,128]{1,0:T(8,128)(2,1)} %get-tuple-element.281), channel_id=1, source_target_pairs={{0,31},{15,0},{16,15},{31,16},{1,30},{14,1},{17,14},{30,17},{2,29}... | collective-permute-start | bytes 393224 | tf_op jit(solution)/shard_map/ppermute | solution.py:421
  690.5 14.1 %collective-permute-start.12 = (bf16[512,128]{1,0:T(8,128)(2,1)}, bf16[512,128]{1,0:T(8,128)(2,1)}, u32[]{:S(2)}, u32[]{:S(2)}) collective-permute-start(bf16[512,128]{1,0:T(8,128)(2,1)} %get-tuple-element.282), channel_id=1, source_target_pairs={{0,16},{15,31},{16,0},{31,15},{1,17},{14,30},{17,1},{30,14},{2,18}... | collective-permute-start | bytes 393224 | tf_op jit(solution)/shard_map/ppermute | solution.py:421
  690.5 12.4 %collective-permute-start.11 = (bf16[512,128]{1,0:T(8,128)(2,1)}, bf16[512,128]{1,0:T(8,128)(2,1)}, u32[]{:S(2)}, u32[]{:S(2)}) collective-permute-start(bf16[512,128]{1,0:T(8,128)(2,1)} %get-tuple-element.283), channel_id=1, source_target_pairs={{0,15},{15,16},{16,31},{31,0},{1,14},{14,17},{17,30},{30,1},{2,13}... | collective-permute-start | bytes 393224 | tf_op jit(solution)/shard_map/ppermute | solution.py:421
  697.0 9.4 %copy-start.18 = (f32[512,768]{1,0:T(8,128)S(1)}, f32[512,768]{1,0:T(8,128)}, u32[]{:S(2)}) copy-start(f32[512,768]{1,0:T(8,128)} %fusion.57) | copy-start | bytes 4718596
  698.0 8.4 %copy-start.15 = (f32[512,768]{1,0:T(8,128)S(1)}, f32[512,768]{1,0:T(8,128)}, u32[]{:S(2)}) copy-start(f32[512,768]{1,0:T(8,128)} %fusion.46) | copy-start | bytes 4718596
  698.0 8.4 %copy-start.16 = (f32[512,768]{1,0:T(8,128)S(1)}, f32[512,768]{1,0:T(8,128)}, u32[]{:S(2)}) copy-start(f32[512,768]{1,0:T(8,128)} %fusion.55) | copy-start | bytes 4718596
  698.0 8.4 %copy-start.17 = (f32[512,768]{1,0:T(8,128)S(1)}, f32[512,768]{1,0:T(8,128)}, u32[]{:S(2)}) copy-start(f32[512,768]{1,0:T(8,128)} %fusion.56) | copy-start | bytes 4718596
  700.8 5.7 copy-start.14
  700.8 5.2 collective-permute-start.14
  700.9 5.6 copy-start.13
  706.0 6.0 collective-permute-start.15
  710.1 17.3 %copy-start.10 = (f32[512,768]{1,0:T(8,128)S(1)}, f32[512,768]{1,0:T(8,128)}, u32[]{:S(2)}) copy-start(f32[512,768]{1,0:T(8,128)} %get-tuple-element.239) | copy-start | bytes 4718596
  713.0 13.9 %all-to-all-start.6 = ((bf16[4,80,384]{2,1,0:T(8,128)(2,1)}), bf16[4,80,384]{2,1,0:T(8,128)(2,1)S(1)}, u32[]{:S(2)}, u32[]{:S(2)}) async-start(bf16[4,80,384]{2,1,0:T(8,128)(2,1)} %fusion.60), calls=%async_computation.8 | async-start | bytes 491520 | tf_op jit(solution)/shard_map/all_to_all | solution.py:483
  726.9 5.3 collective-permute-start.16
  727.4 8.2 %copy-start.1 = (bf16[768,384]{1,0:T(8,128)(2,1)S(1)}, bf16[768,384]{1,0:T(8,128)(2,1)}, u32[]{:S(2)}) copy-start(bf16[768,384]{1,0:T(8,128)(2,1)} %param.26) | copy-start | bytes 1769476
  733.0 1.5 collective-permute-start.20
  (57 other events, 175.3 us)
Sparse Core Ops, SparseCore 0:
  9.6 74.7 all-gather.7
  105.7 35.9 all-gather.9
  144.2 54.3 all-gather.11
  201.3 95.9 all-gather.13
  388.9 111.7 reduce-scatter.2
  502.8 90.7 all-gather.15
  616.6 58.7 reduce-scatter.4
